TPU v7x, 128 devices: a whole 4x4x4 slice. The times are simulated.
128 devices in a mesh: slab: 32 (over z, y, x_hi), rxn: 4 (over x_lo, core).
Axes of the slice: x: 4 (x_hi: 2, x_lo: 2; x = x_hi * 2 + x_lo), y: 4, z: 4, core: 2. Of those that a mesh axis runs over, the one named last changes fastest.
Arguments:
- conc: float32 [256, 64, 4096], P('rxn', 'slab'), may hold values from 0.5 to 4
- order: int32 [2048, 256], P('rxn'), may hold values from 0 to 2, as said below
- stoich: int32 [256, 2048], P(None, 'rxn'), may hold values from -2 to 2, as said below
- species_class: int32 [256], P('rxn'), may hold values from 0 to 3
- diff_coef: float32 [4], replicated, may hold values from 0.1 to 1.5
- rate: float32 [2048], P('rxn'), may hold values from 0.05 to 1
- noise_load: float32 [2, 2048, 32], P(None, 'rxn'), may hold values from -6 to 6
- cell_noise: float32 [2, 32, 64, 4096], P(None, None, 'slab'), may hold values from -6 to 6
Outputs:
- final_conc: float32 [256, 64, 4096], P('rxn', 'slab')
Inputs may be any that keep to these rules, and one draw needn't show every extreme that they name: `order`: each reaction has one or two reactant picks among the species; its row sums to 1 or 2. `stoich`: each column is minus the reaction's reactant orders plus two product picks.
All inputs are finite; a program needn't handle non-finite values.
Results may differ from a plain program's by a relative error of at most 0.0045.
Values may be sent and summed in bfloat16 or wider, within the bound.
No kernel may reach another device: no remote copies, remote signals or barrier semaphores. Data moves between devices by JAX's collectives and lax.ppermute only.
A program may use at most 192 MiB of HBM per device.

v0:
```python
import functools

import jax
import jax.numpy as jnp
from jax import lax
from jax.experimental import pallas as pl
from jax.experimental.pallas import tpu as pltpu
from jax.sharding import Mesh, PartitionSpec as P

GY = 64
K = 32
STEPS = 2
S = 256
TAU = 0.1
FLOOR = 0.02
HALF_LOG2E = 0.7213475204444817

RING = ("x_hi", "x_lo", "core")
N = 8
SB = 64
LN = 512
FAR = 384
WROWS = 656

F32 = jnp.float32
BF16 = jnp.bfloat16
COST = pl.CostEstimate(flops=1, bytes_accessed=1, transcendentals=0)
VMEM = pl.BlockSpec(memory_space=pltpu.VMEM)
SMEM = pl.BlockSpec(memory_space=pltpu.SMEM)


def split2(v):
    hi = v.astype(BF16)
    return hi, (v - hi.astype(F32)).astype(BF16)


def split3(v):
    hi = v.astype(BF16)
    rest = v - hi.astype(F32)
    mid = rest.astype(BF16)
    return hi, mid, (rest - mid.astype(F32)).astype(BF16)


def pack_weights(order_ref, stoich_ref, load_ref, rate_ref, class_ref, coef_ref, w_ref):
    cls = class_ref[...]
    coef = jnp.zeros(cls.shape, F32)
    for c in range(coef_ref.shape[0]):
        coef = jnp.where(cls == c, coef_ref[c], coef)
    lr = 0.5 * jnp.log2(rate_ref[...] * TAU)
    lr3 = [v.astype(F32) for v in split3(lr)]
    co3 = [jnp.concatenate([v.astype(F32), jnp.zeros((1, 192), F32)], axis=1) for v in split3(coef * TAU)]
    for h in range(2):
        out = w_ref.at[h]
        rs = slice(h * 256, h * 256 + 256)
        out[0:256, :] = order_ref[rs, :].astype(F32).astype(BF16)
        out[256:512, :] = stoich_ref[:, rs].astype(F32).astype(BF16)
        for t in range(STEPS):
            hi, lo = split2(load_ref[t, :, rs] * (K ** -0.5))
            out[512 + 64 * t:544 + 64 * t, :] = hi
            out[544 + 64 * t:576 + 64 * t, :] = lo
        tail = jnp.concatenate([v[:, rs] for v in lr3] + co3 + [jnp.zeros((10, 256), F32)], axis=0)
        out[640:656, :] = tail.astype(BF16)


def params(mib):
    return pltpu.CompilerParams(vmem_limit_bytes=mib << 20)


def weights_call(order, stoich, load_t, rate, cls, coef):
    return pl.pallas_call(
        pack_weights,
        out_shape=jax.ShapeDtypeStruct((2, WROWS, 256), BF16),
        in_specs=[VMEM] * 5 + [SMEM],
        out_specs=VMEM,
        compiler_params=params(60),
        name="pack_weights",
        cost_estimate=COST,
    )(order, stoich, load_t, rate, cls, coef)


def pack_state(info_ref, conc_ref, cell_ref, self_ref, peer_ref, inner_ref, opp_ref, outer_ref, near_ref,
               buf, cells, sem, cell_sem):
    me = info_ref[0]
    order = (2, 3, 6, 7, 4, 5, 0, 1)
    places = {2: (inner_ref, 0), 3: (inner_ref, 2), 6: (outer_ref, 0), 7: (outer_ref, 2), 4: (opp_ref, 0),
              5: (opp_ref, 2), 0: (self_ref, 0), 1: (peer_ref, 0)}

    def lanes(k):
        return pl.ds(pl.multiple_of((me ^ k) * LN, LN), LN)

    copies = {}
    for k in order:
        for p in range(2):
            copies[k, p] = pltpu.make_async_copy(conc_ref.at[:, p, lanes(k)], buf.at[k, p], sem.at[k, p])
            copies[k, p].start()
    noise = {}
    for i, k in enumerate((6, 0)):
        for t in range(STEPS):
            for p in range(2):
                c = pltpu.make_async_copy(cell_ref.at[t, :, p, lanes(k)], cells.at[i, t, p], cell_sem.at[i, t, p])
                c.start()
                noise[i, t, p] = c
    for k in order:
        out, at = places[k]
        for p in range(2):
            copies[k, p].wait()
            out[SB * (at + p):SB * (at + p + 1)] = buf[k, p].astype(BF16)
    for t in range(STEPS):
        for p in range(2):
            for i in range(2):
                noise[i, t, p].wait()
            hi, lo = split2(cells[1, t, p])
            near_ref[t, p, 0:32] = hi
            near_ref[t, p, 32:64] = lo
            at = 4 * SB + 2 * K * t + K * p
            outer_ref[at:at + K] = cells[0, t, p].astype(BF16)


def state_call(info, conc, cell):
    def m(rows):
        return jax.ShapeDtypeStruct((rows, LN), BF16)

    any_ = pl.BlockSpec(memory_space=pl.ANY)
    return pl.pallas_call(
        pack_state,
        out_shape=(m(128), m(128), m(256), m(256), m(FAR), jax.ShapeDtypeStruct((STEPS, 2, SB, LN), BF16)),
        in_specs=[SMEM, any_, any_],
        out_specs=(VMEM,) * 6,
        scratch_shapes=[
            pltpu.VMEM((N, 2, SB, LN), F32),
            pltpu.VMEM((2, STEPS, 2, K, LN), F32),
            pltpu.SemaphoreType.DMA((N, 2)),
            pltpu.SemaphoreType.DMA((2, STEPS, 2)),
        ],
        compiler_params=params(60),
        name="pack_state",
        cost_estimate=COST,
    )(info, conc, cell)


PARTS = (0, 224, 448, WROWS)


def sort_weights(info_ref, *refs):
    own, beside, far, *parts = refs[:6]
    order_ref, stoich_ref, load_ref, lr_ref, coef_ref = refs[6:]
    me = info_ref[0]
    for i in range(N):
        def rows_of(start, stop, i=i):
            if i < 6:
                return (own, beside, far)[i // 2][i % 2, start:stop]
            cuts = [(max(start, lo) - lo, min(stop, hi) - lo) for lo, hi in zip(PARTS, PARTS[1:])]
            return jnp.concatenate([p[i % 2, lo:hi] for p, (lo, hi) in zip(parts, cuts) if lo < hi], axis=0)

        rows = pl.ds(i * 256, 256)
        order_ref[rows, :] = rows_of(0, 256)
        stoich_ref[:, rows] = rows_of(256, 512)
        loads = rows_of(512, WROWS).astype(F32)
        tail = loads[128:]
        for t in range(STEPS):
            hi, lo = loads[64 * t:64 * t + 32], loads[64 * t + 32:64 * t + 64]
            block = jnp.concatenate([hi, hi, lo, tail, jnp.zeros((16, 256), F32)], axis=0)
            turned = block.T
            lane = lax.broadcasted_iota(jnp.int32, turned.shape, 1)
            load_ref[t, rows, :] = jnp.where(lane < 96, turned, 0.0).astype(BF16)
        lr = turned[:, 96:97] + turned[:, 97:98] + turned[:, 98:99]
        lr_ref[rows, :] = jnp.broadcast_to(lr, (256, 128))
        if i % 2 == 0:
            co = turned[:SB, 99:100] + turned[:SB, 100:101] + turned[:SB, 101:102]
            at = pl.ds(pl.multiple_of(((me & 3) ^ (i // 2)) * SB, SB), SB)
            coef_ref[at, :] = jnp.broadcast_to(co, (SB, 128))


def sort_call(info, ws):
    return pl.pallas_call(
        sort_weights,
        out_shape=(
            jax.ShapeDtypeStruct((2048, S), BF16),
            jax.ShapeDtypeStruct((S, 2048), BF16),
            jax.ShapeDtypeStruct((STEPS, 2048, 128), BF16),
            jax.ShapeDtypeStruct((2048, 128), F32),
            jax.ShapeDtypeStruct((S, 128), F32),
        ),
        in_specs=[SMEM] + [VMEM] * 6,
        out_specs=(VMEM,) * 5,
        compiler_params=params(10),
        name="sort_weights",
        cost_estimate=COST,
    )(info, *ws)


def gather_planes(at, info_ref, *refs):
    pieces, out_ref = refs[:4], refs[4]
    me = info_ref[0]
    for j in range(4):
        rows = pl.ds(pl.multiple_of(((me & 3) ^ j) * SB, SB), SB)
        for p in range(2):
            out_ref[p, rows, :] = pieces[j][SB * (at[j] + p):SB * (at[j] + p + 1)]


def gather_call(info, pieces, at):
    return pl.pallas_call(
        functools.partial(gather_planes, at),
        out_shape=jax.ShapeDtypeStruct((2, S, LN), BF16),
        in_specs=[SMEM] + [VMEM] * 4,
        out_specs=VMEM,
        compiler_params=params(6),
        name="gather_planes",
        cost_estimate=COST,
    )(info, *pieces)


def put_edges(info_ref, a, b, ev_ref, od_ref, peer_ref, chip_ref):
    me = info_ref[0]
    first = (me >> 2) == 0
    core = me & 1
    even = (info_ref[1] & 1) == 0
    lo = jnp.where(first, a[0].astype(F32), b[0].astype(F32))
    hi = jnp.where(first, b[1].astype(F32), a[1].astype(F32))
    ev_ref[...] = jnp.where(even, hi, lo).astype(BF16)
    od_ref[...] = jnp.where(even, lo, hi).astype(BF16)
    for q in range(2):
        sides = []
        for cut in (slice(0, 128), slice(LN - 128, LN)):
            va, vb = a[q][:, cut].astype(F32), b[q][:, cut].astype(F32)
            sides.append((jnp.where(first, va, vb), jnp.where(first, vb, va)))
        low = lax.broadcasted_iota(jnp.int32, sides[0][0].shape, 1) < GY
        left = jnp.where(low, sides[0][0], pltpu.roll(sides[0][1], GY, 1))
        right = jnp.where(low, pltpu.roll(sides[1][0], GY, 1), sides[1][1])
        peer_ref[q] = jnp.where(core == 0, right, left).astype(BF16)
        chip_ref[q] = jnp.where(core == 0, left, right).astype(BF16)


EDGES = (
    jax.ShapeDtypeStruct((S, LN), BF16),
    jax.ShapeDtypeStruct((S, LN), BF16),
    jax.ShapeDtypeStruct((2, S, 128), BF16),
    jax.ShapeDtypeStruct((2, S, 128), BF16),
)


def edge_kernel(info_ref, a_ref, b_ref, *edges):
    put_edges(info_ref, [a_ref[0], a_ref[1]], [b_ref[0], b_ref[1]], *edges)


def edges_call(info, a, b):
    return pl.pallas_call(
        edge_kernel,
        out_shape=EDGES,
        in_specs=[SMEM, VMEM, VMEM],
        out_specs=(VMEM,) * 4,
        compiler_params=params(6),
        name="edges",
        cost_estimate=COST,
    )(info, a, b)


def react(far, conc_ref, cell_ref, order_ref, stoich_ref, load_ref, lr_ref, change_ref, flux_s):
    logs = jnp.log(conc_ref[0].astype(F32)).astype(BF16)
    zeros = jnp.zeros((K, LN), BF16)
    if far:
        hi, lo = cell_ref[...], zeros
    else:
        hi, lo = cell_ref[0, 0, :K], cell_ref[0, 0, K:]
    cells = jnp.concatenate([hi, lo, hi, zeros], axis=0)
    for i in range(N):
        rows = pl.ds(i * 256, 256)
        expo = jnp.dot(order_ref[rows, :], logs, preferred_element_type=F32)
        noise = jnp.dot(load_ref[0, rows, :], cells, preferred_element_type=F32)
        lr = lr_ref[rows, :]
        root = jnp.exp2(expo * HALF_LOG2E + jnp.concatenate([lr] * (LN // 128), axis=1))
        flux_s[rows, :] = (root * (root + noise)).astype(BF16)
    change_ref[0] = jnp.dot(stoich_ref[...], flux_s[...], preferred_element_type=F32)


def react_call(step, conc, cells, sorted_ws, far=False):
    order, stoich, load, lr, _ = sorted_ws
    plane = pl.BlockSpec((1, S, LN), lambda p: (p, 0, 0))
    if far:
        cell = pl.BlockSpec((K, LN), lambda p: (4 * SB // K + 2 * step + p, 0))
    else:
        cell = pl.BlockSpec((1, 1, 2 * K, LN), lambda p: (step, p, 0, 0))
    return pl.pallas_call(
        functools.partial(react, far),
        grid=(2,),
        out_shape=jax.ShapeDtypeStruct((2, S, LN), F32),
        in_specs=[
            plane,
            cell,
            pl.BlockSpec((2048, S), lambda p: (0, 0)),
            pl.BlockSpec((S, 2048), lambda p: (0, 0)),
            pl.BlockSpec((1, 2048, 128), lambda p: (step, 0, 0)),
            pl.BlockSpec((2048, 128), lambda p: (0, 0)),
        ],
        out_specs=plane,
        scratch_shapes=[pltpu.VMEM((2048, LN), BF16)],
        compiler_params=params(20),
        name="react",
        cost_estimate=COST,
    )(conc, cells, order, stoich, load, lr)


def diffuse(info_ref, which, a, b, ev, od, from_peer, from_chip, change, coef):
    me = info_ref[0]
    ring = info_ref[1]
    x_hi = (me >> 2) ^ which
    first = x_hi == 0
    own, other = (a, b) if which == 0 else (b, a)
    own, other = [v.astype(F32) for v in own], [v.astype(F32) for v in other]
    even = (ring & 1) == 0
    ev, od = ev.astype(F32), od.astype(F32)
    lo = jnp.where(ring == 0, own[0], jnp.where(even, od, ev))
    hi = jnp.where(ring == 15, own[1], jnp.where(even, ev, od))
    below = [jnp.where(first, lo, other[1]), own[0]]
    above = [own[1], jnp.where(first, other[0], hi)]
    rows = own[0].shape[0]
    lane = lax.broadcasted_iota(jnp.int32, (rows, 128), 1)
    low = lane < GY
    column = lane & (GY - 1)
    core = me & 1
    out = []
    for p in range(2):
        c = own[p]
        peer, chip = from_peer[p].astype(F32), from_chip[p].astype(F32)
        left, right = jnp.where(core == 0, chip, peer), jnp.where(core == 0, peer, chip)
        left = jnp.where(first, left, pltpu.roll(left, GY, 1))
        right = jnp.where(first, pltpu.roll(right, GY, 1), right)
        vs = [c[:, 128 * j:128 * j + 128] for j in range(LN // 128)]
        sw = [pltpu.roll(v, GY, 1) for v in vs]
        left = jnp.where(me == 0, vs[0], left)
        right = jnp.where(me == N - 1, vs[-1], right)
        lat = []
        for j, v in enumerate(vs):
            prev = left if j == 0 else sw[j - 1]
            nxt = right if j == len(vs) - 1 else sw[j + 1]
            x_dn = jnp.where(low, prev, sw[j])
            x_up = jnp.where(low, sw[j], nxt)
            y_up = jnp.where(column == GY - 1, v, pltpu.roll(v, 127, 1))
            y_dn = jnp.where(column == 0, v, pltpu.roll(v, 1, 1))
            lat.append(x_up + x_dn + y_up + y_dn)
        lap = above[p] + below[p] + jnp.concatenate(lat, axis=1) - 6.0 * c
        co = jnp.concatenate([coef] * (LN // 128), axis=1)
        out.append(jnp.maximum(c + co * lap + change[p], FLOOR))
    return out


def two(ref):
    return [ref[0], ref[1]]


def advance(info_ref, a_ref, b_ref, da_ref, db_ref, ev_ref, od_ref, peer_ref, chip_ref, coef_ref, na_ref, nb_ref, *edges):
    a, b = two(a_ref), two(b_ref)
    args = (ev_ref[...], od_ref[...], two(peer_ref), two(chip_ref))
    new = [diffuse(info_ref, w, a, b, *args, two(d), coef_ref[...]) for w, d in ((0, da_ref), (1, db_ref))]
    for v, ref in zip(new, (na_ref, nb_ref)):
        ref[0], ref[1] = v
    put_edges(info_ref, *new, *edges)


ROWS = 64


def specs_of(at):
    return dict(
        two=pl.BlockSpec((2, ROWS, LN), lambda s, i: (0, at(s, i), 0)),
        one=pl.BlockSpec((ROWS, LN), lambda s, i: (at(s, i), 0)),
        side=pl.BlockSpec((2, ROWS, 128), lambda s, i: (0, at(s, i), 0)),
        col=pl.BlockSpec((ROWS, 128), lambda s, i: (at(s, i), 0)),
    )


def advance_call(info, a, b, da, db, halos, coef):
    n = specs_of(lambda s, i: s)
    pair = jax.ShapeDtypeStruct((2, S, LN), F32)
    return pl.pallas_call(
        advance,
        grid_spec=pltpu.PrefetchScalarGridSpec(
            num_scalar_prefetch=1,
            grid=(S // ROWS,),
            in_specs=[n["two"]] * 4 + [n["one"]] * 2 + [n["side"]] * 2 + [n["col"]],
            out_specs=[n["two"]] * 2 + [n["one"]] * 2 + [n["side"]] * 2,
        ),
        out_shape=(pair, pair) + EDGES,
        compiler_params=params(12),
        name="advance",
        cost_estimate=COST,
    )(info, a, b, da, db, *halos, coef)


def finish(which, info_ref, a_ref, b_ref, d_ref, ev_ref, od_ref, peer_ref, chip_ref, coef_ref, *outs):
    new = diffuse(info_ref, which, two(a_ref), two(b_ref), ev_ref[...], od_ref[...], two(peer_ref), two(chip_ref),
                  two(d_ref), coef_ref[...])
    j = pl.program_id(0)
    each = 4 // len(outs)
    for n, ref in enumerate(outs):
        @pl.when(j // each == n)
        def _(ref=ref):
            ref[0, 0], ref[0, 1] = [v.astype(BF16) for v in new]


def finish_call(which, info, a, b, d, halos, coef, count):
    n = specs_of(lambda s, i: (i[0] & 3) ^ s)
    each = 4 // count
    m = jax.ShapeDtypeStruct((each, 2, SB, LN), BF16)
    return pl.pallas_call(
        functools.partial(finish, which),
        grid_spec=pltpu.PrefetchScalarGridSpec(
            num_scalar_prefetch=1,
            grid=(4,),
            in_specs=[n["two"]] * 3 + [n["one"]] * 2 + [n["side"]] * 2 + [n["col"]],
            out_specs=[
                pl.BlockSpec((1, 2, SB, LN), lambda s, i, n=n: (jnp.clip(s - each * n, 0, each - 1), 0, 0, 0))
                for n in range(count)
            ],
        ),
        out_shape=(m,) * count,
        compiler_params=params(12),
        name="finish",
        cost_estimate=COST,
    )(info, a, b, d, *halos, coef)


def join_out(at, info_ref, *refs):
    pieces, out_ref, buf, sem = refs[:N], refs[N], refs[N + 1], refs[N + 2]
    me = info_ref[0]
    copies = []
    for k in range(N):
        lanes = pl.ds(pl.multiple_of((me ^ k) * LN, LN), LN)
        for p in range(2):
            buf[k, p] = pieces[k][at[k], p].astype(F32)
            c = pltpu.make_async_copy(buf.at[k, p], out_ref.at[:, p, lanes], sem.at[k, p])
            c.start()
            copies.append(c)
    for c in copies:
        c.wait()


def join_call(info, pieces, at):
    return pl.pallas_call(
        functools.partial(join_out, at),
        out_shape=jax.ShapeDtypeStruct((SB, 2, N * LN), F32),
        in_specs=[SMEM] + [VMEM] * N,
        out_specs=pl.BlockSpec(memory_space=pl.ANY),
        scratch_shapes=[pltpu.VMEM((N, 2, SB, LN), F32), pltpu.SemaphoreType.DMA((N, 2))],
        compiler_params=params(12),
        name="join_out",
        cost_estimate=COST,
    )(info, *pieces)


def send(v, k):
    return lax.ppermute(v, RING, [(i, i ^ k) for i in range(N)])


def swap(v, axis, firsts):
    return lax.ppermute(v, axis, [(i, i + 1) for i in firsts] + [(i + 1, i) for i in firsts])


def exchange(edges):
    ev, od, peer, chip = edges
    return (
        swap(ev, "zy", range(0, 15, 2)),
        swap(od, "zy", range(1, 15, 2)),
        send(peer, 1),
        swap(chip, RING, (1, 3, 5)),
    )


def on_device(conc, order, stoich, species_class, diff_coef, rate, noise_load, cell_noise):
    info = jnp.stack([lax.axis_index(RING), lax.axis_index("zy")]).astype(jnp.int32)
    w = weights_call(
        order, stoich, jnp.transpose(noise_load, (0, 2, 1)), rate[None, :], species_class[None, :], diff_coef
    )
    far = lax.ppermute(w, RING, [(i, i ^ (6 if i % 2 else 2)) for i in range(N)])
    beside = send(w, 1)
    after_w, w = lax.optimization_barrier((info, w))
    mine, peer, inner, opp, outer, near = state_call(after_w, conc, cell_noise)
    far, mine = lax.optimization_barrier((far, mine))
    inner, opp, outer = send(inner, 2), send(opp, 4), send(outer, 6)
    ws = sort_call(info, [w, beside, far, *[send(far[:, lo:hi], 1) for lo, hi in zip(PARTS, PARTS[1:])]])
    inner, *ws = lax.optimization_barrier((inner, *ws))
    coef = ws[-1]
    a = gather_call(info, [mine, send(peer, 1), inner, send(inner[2 * SB:], 1)], (0, 0, 0, 0))
    da = react_call(0, a, near, ws)
    opp, outer, da = lax.optimization_barrier((opp, outer, da))
    cells = outer
    b = gather_call(info, [opp, send(opp, 1), outer, send(outer, 1)], (0, 2, 0, 2))
    around = exchange(edges_call(info, a, b))
    db = react_call(0, b, cells, ws, far=True)
    a, b, *edges = advance_call(info, a, b, da, db, around, coef)
    around = exchange(edges)
    db = react_call(1, b, cells, ws, far=True)
    opp, outer = finish_call(1, info, a, b, db, around, coef, 2)
    opp, outer, near = lax.optimization_barrier((opp, outer, near))
    opp, outer = send(opp, 4), send(outer, 6)
    da = react_call(1, a, near, ws)
    near_out = finish_call(0, info, a, b, da, around, coef, 4)
    back = [near_out[0]] + [send(near_out[k], k) for k in range(1, 4)]
    opp, outer, *back = lax.optimization_barrier((opp, outer, *back))
    back += [opp, send(opp, 1), outer, send(outer, 1)]
    return join_call(info, back, (0, 0, 0, 0, 0, 1, 0, 1))


def solution(mesh):
    grid = Mesh(mesh.devices.reshape(16, 2, 2, 2), ("zy", "x_hi", "x_lo", "core"))
    rxn, slab = ("x_lo", "core"), ("zy", "x_hi")
    placed = (
        P(rxn, slab, None),
        P(rxn, None),
        P(None, rxn),
        P(rxn),
        P(),
        P(rxn),
        P(None, rxn, None),
        P(None, None, slab, None),
    )
    return jax.shard_map(
        on_device, mesh=grid, in_specs=placed, out_specs=P(rxn, slab, None), check_vma=False
    )
```

profile of v0, /device:TPU:103, one launch (start us, length us, event | category | flops | bytes accessed | tf_op | source)
XLA Modules:
  0.0 84.6 jit_solution(25424898027984914)
XLA Ops:
  0.0 2.2 %pack_weights.1.refs_0_ = bf16[2,656,256]{2,1,0:T(8,128)(2,1)} custom-call(s32[512,256]{1,0:T(8,128)} %order_ref.1, s32[256,512]{1,0:T(8,128)} %stoich_ref.1, f32[2,32,512]{2,1,0:T(8,128)} %bitcast.5, f32[1,512]{1,0:T(1,128)} %bitcast.6, s32[1,64]{1,0:T(1,128)} %bitcast.7, f32[4]{0:T(128)} %coef_ref.1), custom_call_target="tpu_custom_call" | custom-call | flops 1 | bytes 1 | tf_op jit(solution)/shard_map/pack_weights/pallas_call | solution.py:70
  2.4 1.3 %collective-permute-start.3 = (bf16[2,656,256]{2,1,0:T(8,128)(2,1)}, bf16[2,656,256]{2,1,0:T(8,128)(2,1)S(1)}, u32[]{:S(2)}, u32[]{:S(2)}) collective-permute-start(bf16[2,656,256]{2,1,0:T(8,128)(2,1)} %pack_weights.1.refs_0_), channel_id=1, source_target_pairs={{0,1},{1,0},{2,3},{3,2},{4,5},{5,4},{6,7},{7,6},{8,9},{9,8},{10,11... | collective-permute-start | bytes 2015240 | tf_op jit(solution)/shard_map/ppermute | solution.py:452
  4.4 4.2 %pack_state.1 = (bf16[128,512]{1,0:T(8,128)(2,1)}, bf16[128,512]{1,0:T(8,128)(2,1)}, bf16[256,512]{1,0:T(8,128)(2,1)}, bf16[256,512]{1,0:T(8,128)(2,1)}, bf16[38...) custom-call(s32[2]{0:T(128)} %pad_add_fusion.info_ref, f32[64,2,4096]{2,1,0:T(2,128)} %conc_ref.1, ...), custom_call_target="tpu_custom_call" | custom-call | flops 1 | bytes 1 | tf_op jit(solution)/shard_map/pack_state/pallas_call | solution.py:124
  8.5 1.0 %collective-permute-start.2 = (bf16[256,512]{1,0:T(8,128)(2,1)}, bf16[256,512]{1,0:T(8,128)(2,1)S(1)}, u32[]{:S(2)}, u32[]{:S(2)}) collective-permute-start(bf16[256,512]{1,0:T(8,128)(2,1)} %get-tuple-element.58), channel_id=1, source_target_pairs={{0,2},{1,3},{2,0},{3,1},{4,6},{5,7},{6,4},{7,5},{8,10},{9,11},{10,... | collective-permute-start | bytes 786440 | tf_op jit(solution)/shard_map/ppermute | solution.py:452
  9.9 3.3 %collective-permute-done.refs_2_ = bf16[2,656,256]{2,1,0:T(8,128)(2,1)S(1)} collective-permute-done((bf16[2,656,256]{2,1,0:T(8,128)(2,1)}, bf16[2,656,256]{2,1,0:T(8,128)(2,1)S(1)}, u32[]{:S(2)}, u32[]{:S(2)}) %collective-permute-start) | collective-permute-done | bytes 671776 | tf_op jit(solution)/shard_map/ppermute | solution.py:474
  13.2 2.5 %collective-permute-start.6 = (bf16[2,208,256]{2,1,0:T(8,128)(2,1)S(1)}, bf16[2,208,256]{2,1,0:T(8,128)(2,1)S(1)}, u32[]{:S(2)}, u32[]{:S(2)}) collective-permute-start(bf16[2,208,256]{2,1,0:T(8,128)(2,1)S(1)} %slice.14), channel_id=1, source_target_pairs={{0,1},{1,0},{2,3},{3,2},{4,5},{5,4},{6,7},{7,6},{8,9},{9,8},{10,11... | collective-permute-start | bytes 638984 | tf_op jit(solution)/shard_map/ppermute | solution.py:452
  16.9 1.4 %collective-permute-start.8 = (bf16[256,512]{1,0:T(8,128)(2,1)}, bf16[256,512]{1,0:T(8,128)(2,1)S(1)}, u32[]{:S(2)}, u32[]{:S(2)}) collective-permute-start(bf16[256,512]{1,0:T(8,128)(2,1)} %get-tuple-element.67), channel_id=1, source_target_pairs={{0,4},{1,5},{2,6},{3,7},{4,0},{5,1},{6,2},{7,3},{8,12},{9,13},{10,... | collective-permute-start | bytes 786440 | tf_op jit(solution)/shard_map/ppermute | solution.py:452
  18.9 2.2 %sort_weights.1 = (bf16[2048,256]{1,0:T(8,128)(2,1)S(1)}, bf16[256,2048]{1,0:T(8,128)(2,1)S(1)}, bf16[2,2048,128]{2,1,0:T(8,128)(2,1)S(1)}, f32[2048,128]{1,0:T(8,128)S(1)}, f32[256,128]{1,0:T(8,128)S(1)}) custom-call(s32[2]{0:T(128)S(1)} %copy-done.3, bf16[2,656,256]{2,1,0:T(8,128)(2,1)S(1)} %copy-done, ...), custom_call_target="tpu_custom_call" | custom-call | flops 1 | bytes 1 | tf_op jit(solution)/shard_map/sort_weights/pallas_call | solution.py:175
  21.2 1.3 %collective-permute-done.7.refs_3_ = bf16[128,512]{1,0:T(8,128)(2,1)S(1)} collective-permute-done((bf16[128,512]{1,0:T(8,128)(2,1)S(1)}, bf16[128,512]{1,0:T(8,128)(2,1)S(1)}, u32[]{:S(2)}, u32[]{:S(2)}) %collective-permute-start.7) | collective-permute-done | bytes 131104 | tf_op jit(solution)/shard_map/ppermute | solution.py:452
  23.1 3.8 %react.4.da_ref = f32[2,256,512]{2,1,0:T(8,128)S(1)} custom-call(bf16[2,256,512]{2,1,0:T(8,128)(2,1)S(1)} %gather_planes.2.conc_ref.a_ref, bf16[2,2,64,512]{3,2,1,0:T(8,128)(2,1)S(1)} %copy-done.1, bf16[2048,256]{1,0:T(8,128)(2,1)S(1)} %get-tuple-element.70.order_ref, bf16[256,2048]{1,0:T(8,128)(2,1)S(1)} %get-tuple-element.71.stoich_ref, ...), custom_call_target="tpu_custom_call" | custom-call | flops 1 | bytes 1 | tf_op jit(solution)/shard_map/react/pallas_call | solution.py:283
  27.0 1.1 %collective-permute-start.11 = (bf16[384,512]{1,0:T(8,128)(2,1)S(1)}, bf16[384,512]{1,0:T(8,128)(2,1)S(1)}, u32[]{:S(2)}, u32[]{:S(2)}) collective-permute-start(bf16[384,512]{1,0:T(8,128)(2,1)S(1)} %collective-permute-done.9.refs_2_.cell_ref), channel_id=1, source_target_pairs={{0,1},{1,0},{2,3},{3,2},{4,5},{5,4},{6,7},{7,6},{8,9},{9,8},{10,11... | collective-permute-start | bytes 1179656 | tf_op jit(solution)/shard_map/ppermute | solution.py:452
  28.1 1.7 %collective-permute-done.10.refs_1_ = bf16[256,512]{1,0:T(8,128)(2,1)S(1)} collective-permute-done((bf16[256,512]{1,0:T(8,128)(2,1)S(1)}, bf16[256,512]{1,0:T(8,128)(2,1)S(1)}, u32[]{:S(2)}, u32[]{:S(2)}) %collective-permute-start.10) | collective-permute-done | bytes 262176 | tf_op jit(solution)/shard_map/ppermute | solution.py:452
  31.3 1.4 %collective-permute-start.12 = (bf16[256,512]{1,0:T(8,128)(2,1)S(1)}, bf16[256,512]{1,0:T(8,128)(2,1)S(1)}, u32[]{:S(2)}, u32[]{:S(2)}) collective-permute-start(bf16[256,512]{1,0:T(8,128)(2,1)S(1)} %get-tuple-element.77), channel_id=1, source_target_pairs={{0,8},{16,24},{32,40},{48,56},{64,72},{80,88},{96,104},{112,120},{... | collective-permute-start | bytes 786440 | tf_op jit(solution)/shard_map/ppermute | solution.py:456
  32.6 3.6 %collective-permute-start.13 = (bf16[256,512]{1,0:T(8,128)(2,1)S(1)}, bf16[256,512]{1,0:T(8,128)(2,1)S(1)}, u32[]{:S(2)}, u32[]{:S(2)}) collective-permute-start(bf16[256,512]{1,0:T(8,128)(2,1)S(1)} %get-tuple-element.78), channel_id=1, source_target_pairs={{8,16},{24,32},{40,48},{56,64},{72,80},{88,96},{104,112},{16,8},{3... | collective-permute-start | bytes 786440 | tf_op jit(solution)/shard_map/ppermute | solution.py:456
  36.3 1.0 %collective-permute-start.14 = (bf16[2,256,128]{2,1,0:T(8,128)(2,1)S(1)}, bf16[2,256,128]{2,1,0:T(8,128)(2,1)S(1)}, u32[]{:S(2)}, u32[]{:S(2)}) collective-permute-start(bf16[2,256,128]{2,1,0:T(8,128)(2,1)S(1)} %get-tuple-element.79), channel_id=1, source_target_pairs={{0,1},{1,0},{2,3},{3,2},{4,5},{5,4},{6,7},{7,6},{8,9},{9,8},{10,11... | collective-permute-start | bytes 393224 | tf_op jit(solution)/shard_map/ppermute | solution.py:452
  38.0 3.8 %react.5.db_ref = f32[2,256,512]{2,1,0:T(8,128)S(1)} custom-call(bf16[2,256,512]{2,1,0:T(8,128)(2,1)S(1)} %gather_planes.3.conc_ref.b_ref, bf16[384,512]{1,0:T(8,128)(2,1)S(1)} %collective-permute-done.9.refs_2_.cell_ref, bf16[2048,256]{1,0:T(8,128)(2,1)S(1)} %get-tuple-element.70.order_ref, bf16[256,2048]{1,0:T(8,128)(2,1)S(1)} %get-tuple-element.71.stoich_ref, ...), custom_call_target="tpu_custom_call" | custom-call | flops 1 | bytes 1 | tf_op jit(solution)/shard_map/react/pallas_call | solution.py:283
  41.8 2.1 %collective-permute-done.13.od_ref = bf16[256,512]{1,0:T(8,128)(2,1)S(1)} collective-permute-done((bf16[256,512]{1,0:T(8,128)(2,1)S(1)}, bf16[256,512]{1,0:T(8,128)(2,1)S(1)}, u32[]{:S(2)}, u32[]{:S(2)}) %collective-permute-start.13) | collective-permute-done | bytes 262176 | tf_op jit(solution)/shard_map/ppermute | solution.py:456
  43.8 3.1 %advance.1 = (f32[2,256,512]{2,1,0:T(8,128)S(1)}, f32[2,256,512]{2,1,0:T(8,128)S(1)}, bf16[256,512]{1,0:T(8,128)(2,1)S(1)}, bf16[256,512]{1,0:T(8,128)(2,1)S(1)}...) custom-call(s32[2]{0:T(128)S(1)} %copy-done.3, ...), custom_call_target="tpu_custom_call" | custom-call | flops 1 | bytes 1 | tf_op jit(solution)/shard_map/advance/pallas_call | solution.py:375
  47.0 3.6 %collective-permute-start.17 = (bf16[256,512]{1,0:T(8,128)(2,1)S(1)}, bf16[256,512]{1,0:T(8,128)(2,1)S(1)}, u32[]{:S(2)}, u32[]{:S(2)}) collective-permute-start(bf16[256,512]{1,0:T(8,128)(2,1)S(1)} %get-tuple-element.85), channel_id=1, source_target_pairs={{8,16},{24,32},{40,48},{56,64},{72,80},{88,96},{104,112},{16,8},{3... | collective-permute-start | bytes 786440 | tf_op jit(solution)/shard_map/ppermute | solution.py:456
  50.7 1.9 %collective-permute-start.18 = (bf16[2,256,128]{2,1,0:T(8,128)(2,1)S(1)}, bf16[2,256,128]{2,1,0:T(8,128)(2,1)S(1)}, u32[]{:S(2)}, u32[]{:S(2)}) collective-permute-start(bf16[2,256,128]{2,1,0:T(8,128)(2,1)S(1)} %get-tuple-element.86), channel_id=1, source_target_pairs={{0,1},{1,0},{2,3},{3,2},{4,5},{5,4},{6,7},{7,6},{8,9},{9,8},{10,11... | collective-permute-start | bytes 393224 | tf_op jit(solution)/shard_map/ppermute | solution.py:452
  53.4 3.8 %react.6.d_ref = f32[2,256,512]{2,1,0:T(8,128)S(1)} custom-call(f32[2,256,512]{2,1,0:T(8,128)S(1)} %get-tuple-element.83.conc_ref.b_ref, bf16[384,512]{1,0:T(8,128)(2,1)S(1)} %collective-permute-done.9.refs_2_.cell_ref, bf16[2048,256]{1,0:T(8,128)(2,1)S(1)} %get-tuple-element.70.order_ref, bf16[256,2048]{1,0:T(8,128)(2,1)S(1)} %get-tuple-element.71.stoich_ref, ...), custom_call_target="tpu_custom_call" | custom-call | flops 1 | bytes 1 | tf_op jit(solution)/shard_map/react/pallas_call | solution.py:283
  57.3 2.4 %finish.2 = (bf16[2,2,64,512]{3,2,1,0:T(8,128)(2,1)S(1)}, bf16[2,2,64,512]{3,2,1,0:T(8,128)(2,1)S(1)}) custom-call(s32[2]{0:T(128)S(1)} %copy-done.3, f32[2,256,512]{2,1,0:T(8,128)S(1)} %get-tuple-element.82.a_ref.conc_ref, f32[2,256,512]{2,1,0:T(8,128)S(1)} %get-tuple-element.83.conc_ref.b_ref, f32[2,256,512]{2,1,0:T(8,128)S(1)} %react.6.d_ref, ...), custom_call_target="tpu_custom_call" | custom-call | flops 1 | bytes 1 | tf_op jit(solution)/shard_map/finish/pallas_call | solution.py:405
  59.7 2.8 %collective-permute-start.20 = (bf16[2,2,64,512]{3,2,1,0:T(8,128)(2,1)S(1)}, bf16[2,2,64,512]{3,2,1,0:T(8,128)(2,1)S(1)}, u32[]{:S(2)}, u32[]{:S(2)}) collective-permute-start(bf16[2,2,64,512]{3,2,1,0:T(8,128)(2,1)S(1)} %get-tuple-element.90), channel_id=1, source_target_pairs={{0,4},{1,5},{2,6},{3,7},{4,0},{5,1},{6,2},{7,3},{8,12},{9,13},{10,... | collective-permute-start | bytes 786440 | tf_op jit(solution)/shard_map/ppermute | solution.py:452
  62.4 2.6 %collective-permute-start.21 = (bf16[2,2,64,512]{3,2,1,0:T(8,128)(2,1)S(1)}, bf16[2,2,64,512]{3,2,1,0:T(8,128)(2,1)S(1)}, u32[]{:S(2)}, u32[]{:S(2)}) collective-permute-start(bf16[2,2,64,512]{3,2,1,0:T(8,128)(2,1)S(1)} %get-tuple-element.91), channel_id=1, source_target_pairs={{0,6},{1,7},{2,4},{3,5},{4,2},{5,3},{6,0},{7,1},{8,14},{9,15},{10,... | collective-permute-start | bytes 786440 | tf_op jit(solution)/shard_map/ppermute | solution.py:452
  65.1 3.7 %react.7.d_ref = f32[2,256,512]{2,1,0:T(8,128)S(1)} custom-call(f32[2,256,512]{2,1,0:T(8,128)S(1)} %get-tuple-element.82.a_ref.conc_ref, bf16[2,2,64,512]{3,2,1,0:T(8,128)(2,1)S(1)} %copy-done.1, bf16[2048,256]{1,0:T(8,128)(2,1)S(1)} %get-tuple-element.70.order_ref, bf16[256,2048]{1,0:T(8,128)(2,1)S(1)} %get-tuple-element.71.stoich_ref, ...), custom_call_target="tpu_custom_call" | custom-call | flops 1 | bytes 1 | tf_op jit(solution)/shard_map/react/pallas_call | solution.py:283
  68.8 2.4 %finish.3 = (bf16[1,2,64,512]{3,2,1,0:T(8,128)(2,1)S(1)}, bf16[1,2,64,512]{3,2,1,0:T(8,128)(2,1)S(1)}, bf16[1,2,64,512]{3,2,1,0:T(8,128)(2,1)S(1)}, bf16[1,2,64,512]{3,2,1,0:T(8,128)(2,1)S(1)}) custom-call(s32[2]{0:T(128)S(1)} %copy-done.3, f32[2,256,512]{2,1,0:T(8,128)S(1)} %get-tuple-element.82.a_ref.conc_ref, ...), custom_call_target="tpu_custom_call" | custom-call | flops 1 | bytes 1 | tf_op jit(solution)/shard_map/finish/pallas_call | solution.py:405
  71.3 1.3 %collective-permute-start.22 = (bf16[1,2,64,512]{3,2,1,0:T(8,128)(2,1)S(1)}, bf16[1,2,64,512]{3,2,1,0:T(8,128)(2,1)S(1)}, u32[]{:S(2)}, u32[]{:S(2)}) collective-permute-start(bf16[1,2,64,512]{3,2,1,0:T(8,128)(2,1)S(1)} %get-tuple-element.94), channel_id=1, source_target_pairs={{0,1},{1,0},{2,3},{3,2},{4,5},{5,4},{6,7},{7,6},{8,9},{9,8},{10,11... | collective-permute-start | bytes 393224 | tf_op jit(solution)/shard_map/ppermute | solution.py:452
  72.5 1.7 %collective-permute-start.24 = (bf16[1,2,64,512]{3,2,1,0:T(8,128)(2,1)S(1)}, bf16[1,2,64,512]{3,2,1,0:T(8,128)(2,1)S(1)}, u32[]{:S(2)}, u32[]{:S(2)}) collective-permute-start(bf16[1,2,64,512]{3,2,1,0:T(8,128)(2,1)S(1)} %get-tuple-element.96), channel_id=1, source_target_pairs={{0,3},{1,2},{2,1},{3,0},{4,7},{5,6},{6,5},{7,4},{8,11},{9,10},{10,... | collective-permute-start | bytes 393224 | tf_op jit(solution)/shard_map/ppermute | solution.py:452
  74.3 3.3 %collective-permute-done.23.refs_2_ = bf16[1,2,64,512]{3,2,1,0:T(8,128)(2,1)S(1)} collective-permute-done((bf16[1,2,64,512]{3,2,1,0:T(8,128)(2,1)S(1)}, bf16[1,2,64,512]{3,2,1,0:T(8,128)(2,1)S(1)}, u32[]{:S(2)}, u32[]{:S(2)}) %collective-permute-start.23) | collective-permute-done | bytes 131104 | tf_op jit(solution)/shard_map/ppermute | solution.py:452
  77.6 3.0 %collective-permute-done.24.refs_3_ = bf16[1,2,64,512]{3,2,1,0:T(8,128)(2,1)S(1)} collective-permute-done((bf16[1,2,64,512]{3,2,1,0:T(8,128)(2,1)S(1)}, bf16[1,2,64,512]{3,2,1,0:T(8,128)(2,1)S(1)}, u32[]{:S(2)}, u32[]{:S(2)}) %collective-permute-start.24) | collective-permute-done | bytes 131104 | tf_op jit(solution)/shard_map/ppermute | solution.py:452
  81.1 1.0 %collective-permute-done.25.refs_5_ = bf16[2,2,64,512]{3,2,1,0:T(8,128)(2,1)S(1)} collective-permute-done((bf16[2,2,64,512]{3,2,1,0:T(8,128)(2,1)S(1)}, bf16[2,2,64,512]{3,2,1,0:T(8,128)(2,1)S(1)}, u32[]{:S(2)}, u32[]{:S(2)}) %collective-permute-start.25) | collective-permute-done | bytes 262176 | tf_op jit(solution)/shard_map/ppermute | solution.py:452
  82.5 2.0 %join_out.1 = f32[64,2,4096]{2,1,0:T(2,128)} custom-call(s32[2]{0:T(128)S(1)} %copy-done.3, bf16[1,2,64,512]{3,2,1,0:T(8,128)(2,1)S(1)} %get-tuple-element.97.refs_0_, bf16[1,2,64,512]{3,2,1,0:T(8,128)(2,1)S(1)} %collective-permute-done.22.refs_1_, bf16[1,2,64,512]{3,2,1,0:T(8,128)(2,1)S(1)} %collective-permute-done.23.refs_2_, ...), custom_call_target="tpu_custom_call" | custom-call | flops 1 | bytes 1 | tf_op jit(solution)/shard_map/join_out/pallas_call | solution.py:439
  (48 shorter events, 7.8 us)
Async XLA Ops:
  2.2 11.0 %collective-permute-start = (bf16[2,656,256]{2,1,0:T(8,128)(2,1)}, bf16[2,656,256]{2,1,0:T(8,128)(2,1)S(1)}, u32[]{:S(2)}, u32[]{:S(2)}) collective-permute-start(bf16[2,656,256]{2,1,0:T(8,128)(2,1)} %pack_weights.1.refs_0_), channel_id=1, source_target_pairs={{0,2},{1,7},{2,0},{3,5},{4,6},{5,3},{6,4},{7,1},{8,10},{9,15},{10,... | collective-permute-start | bytes 2015240 | tf_op jit(solution)/shard_map/ppermute | solution.py:474
  2.4 13.5 %collective-permute-start.3 = (bf16[2,656,256]{2,1,0:T(8,128)(2,1)}, bf16[2,656,256]{2,1,0:T(8,128)(2,1)S(1)}, u32[]{:S(2)}, u32[]{:S(2)}) collective-permute-start(bf16[2,656,256]{2,1,0:T(8,128)(2,1)} %pack_weights.1.refs_0_), channel_id=1, source_target_pairs={{0,1},{1,0},{2,3},{3,2},{4,5},{5,4},{6,7},{7,6},{8,9},{9,8},{10,11... | collective-permute-start | bytes 2015240 | tf_op jit(solution)/shard_map/ppermute | solution.py:452
  4.4 14.5 %copy-start = (bf16[2,656,256]{2,1,0:T(8,128)(2,1)S(1)}, bf16[2,656,256]{2,1,0:T(8,128)(2,1)}, u32[]{:S(2)}) copy-start(bf16[2,656,256]{2,1,0:T(8,128)(2,1)} %pack_weights.1.refs_0_) | copy-start | bytes 2015236
  4.4 14.5 %copy-start.3 = (s32[2]{0:T(128)S(1)}, s32[2]{0:T(128)}, u32[]{:S(2)}) copy-start(s32[2]{0:T(128)} %pad_add_fusion.info_ref) | copy-start | bytes 28
  8.5 12.5 %collective-permute-start.2 = (bf16[256,512]{1,0:T(8,128)(2,1)}, bf16[256,512]{1,0:T(8,128)(2,1)S(1)}, u32[]{:S(2)}, u32[]{:S(2)}) collective-permute-start(bf16[256,512]{1,0:T(8,128)(2,1)} %get-tuple-element.58), channel_id=1, source_target_pairs={{0,2},{1,3},{2,0},{3,1},{4,6},{5,7},{6,4},{7,5},{8,10},{9,11},{10,... | collective-permute-start | bytes 786440 | tf_op jit(solution)/shard_map/ppermute | solution.py:452
  9.5 17.5 %collective-permute-start.9 = (bf16[384,512]{1,0:T(8,128)(2,1)}, bf16[384,512]{1,0:T(8,128)(2,1)S(1)}, u32[]{:S(2)}, u32[]{:S(2)}) collective-permute-start(bf16[384,512]{1,0:T(8,128)(2,1)} %get-tuple-element.68), channel_id=1, source_target_pairs={{0,6},{1,7},{2,4},{3,5},{4,2},{5,3},{6,0},{7,1},{8,14},{9,15},{10,... | collective-permute-start | bytes 1179656 | tf_op jit(solution)/shard_map/ppermute | solution.py:452
  13.2 9.3 %copy-start.2 = (bf16[128,512]{1,0:T(8,128)(2,1)S(1)}, bf16[128,512]{1,0:T(8,128)(2,1)}, u32[]{:S(2)}) copy-start(bf16[128,512]{1,0:T(8,128)(2,1)} %get-tuple-element.56.refs_0_) | copy-start | bytes 393220
  13.2 3.6 %collective-permute-start.6 = (bf16[2,208,256]{2,1,0:T(8,128)(2,1)S(1)}, bf16[2,208,256]{2,1,0:T(8,128)(2,1)S(1)}, u32[]{:S(2)}, u32[]{:S(2)}) collective-permute-start(bf16[2,208,256]{2,1,0:T(8,128)(2,1)S(1)} %slice.14), channel_id=1, source_target_pairs={{0,1},{1,0},{2,3},{3,2},{4,5},{5,4},{6,7},{7,6},{8,9},{9,8},{10,11... | collective-permute-start | bytes 638984 | tf_op jit(solution)/shard_map/ppermute | solution.py:452
  15.8 7.3 %copy-start.1 = (bf16[2,2,64,512]{3,2,1,0:T(8,128)(2,1)S(1)}, bf16[2,2,64,512]{3,2,1,0:T(8,128)(2,1)}, u32[]{:S(2)}) copy-start(bf16[2,2,64,512]{3,2,1,0:T(8,128)(2,1)} %get-tuple-element.92.cell_ref) | copy-start | bytes 786436
  15.8 2.4 %collective-permute-start.5 = (bf16[2,224,256]{2,1,0:T(8,128)(2,1)S(1)}, bf16[2,224,256]{2,1,0:T(8,128)(2,1)S(1)}, u32[]{:S(2)}, u32[]{:S(2)}) collective-permute-start(bf16[2,224,256]{2,1,0:T(8,128)(2,1)S(1)} %get-tuple-element.103), channel_id=1, source_target_pairs={{0,1},{1,0},{2,3},{3,2},{4,5},{5,4},{6,7},{7,6},{8,9},{9,8},{10,11... | collective-permute-start | bytes 688136 | tf_op jit(solution)/shard_map/ppermute | solution.py:452
  15.9 3.0 %collective-permute-start.4 = (bf16[2,224,256]{2,1,0:T(8,128)(2,1)S(1)}, bf16[2,224,256]{2,1,0:T(8,128)(2,1)S(1)}, u32[]{:S(2)}, u32[]{:S(2)}) collective-permute-start(bf16[2,224,256]{2,1,0:T(8,128)(2,1)S(1)} %get-tuple-element.104), channel_id=1, source_target_pairs={{0,1},{1,0},{2,3},{3,2},{4,5},{5,4},{6,7},{7,6},{8,9},{9,8},{10,11... | collective-permute-start | bytes 688136 | tf_op jit(solution)/shard_map/ppermute | solution.py:452
  16.9 10.0 %collective-permute-start.8 = (bf16[256,512]{1,0:T(8,128)(2,1)}, bf16[256,512]{1,0:T(8,128)(2,1)S(1)}, u32[]{:S(2)}, u32[]{:S(2)}) collective-permute-start(bf16[256,512]{1,0:T(8,128)(2,1)} %get-tuple-element.67), channel_id=1, source_target_pairs={{0,4},{1,5},{2,6},{3,7},{4,0},{5,1},{6,2},{7,3},{8,12},{9,13},{10,... | collective-permute-start | bytes 786440 | tf_op jit(solution)/shard_map/ppermute | solution.py:452
  18.2 3.0 %collective-permute-start.1 = (bf16[128,512]{1,0:T(8,128)(2,1)}, bf16[128,512]{1,0:T(8,128)(2,1)S(1)}, u32[]{:S(2)}, u32[]{:S(2)}) collective-permute-start(bf16[128,512]{1,0:T(8,128)(2,1)} %get-tuple-element.57), channel_id=1, source_target_pairs={{0,1},{1,0},{2,3},{3,2},{4,5},{5,4},{6,7},{7,6},{8,9},{9,8},{10,11... | collective-permute-start | bytes 393224 | tf_op jit(solution)/shard_map/ppermute | solution.py:452
  21.1 1.4 %collective-permute-start.7 = (bf16[128,512]{1,0:T(8,128)(2,1)S(1)}, bf16[128,512]{1,0:T(8,128)(2,1)S(1)}, u32[]{:S(2)}, u32[]{:S(2)}) collective-permute-start(bf16[128,512]{1,0:T(8,128)(2,1)S(1)} %slice.15), channel_id=1, source_target_pairs={{0,1},{1,0},{2,3},{3,2},{4,5},{5,4},{6,7},{7,6},{8,9},{9,8},{10,11... | collective-permute-start | bytes 393224 | tf_op jit(solution)/shard_map/ppermute | solution.py:452
  27.0 2.8 %collective-permute-start.11 = (bf16[384,512]{1,0:T(8,128)(2,1)S(1)}, bf16[384,512]{1,0:T(8,128)(2,1)S(1)}, u32[]{:S(2)}, u32[]{:S(2)}) collective-permute-start(bf16[384,512]{1,0:T(8,128)(2,1)S(1)} %collective-permute-done.9.refs_2_.cell_ref), channel_id=1, source_target_pairs={{0,1},{1,0},{2,3},{3,2},{4,5},{5,4},{6,7},{7,6},{8,9},{9,8},{10,11... | collective-permute-start | bytes 1179656 | tf_op jit(solution)/shard_map/ppermute | solution.py:452
  28.1 1.7 %collective-permute-start.10 = (bf16[256,512]{1,0:T(8,128)(2,1)S(1)}, bf16[256,512]{1,0:T(8,128)(2,1)S(1)}, u32[]{:S(2)}, u32[]{:S(2)}) collective-permute-start(bf16[256,512]{1,0:T(8,128)(2,1)S(1)} %collective-permute-done.8.refs_0_), channel_id=1, source_target_pairs={{0,1},{1,0},{2,3},{3,2},{4,5},{5,4},{6,7},{7,6},{8,9},{9,8},{10,11... | collective-permute-start | bytes 786440 | tf_op jit(solution)/shard_map/ppermute | solution.py:452
  31.3 10.5 %collective-permute-start.12 = (bf16[256,512]{1,0:T(8,128)(2,1)S(1)}, bf16[256,512]{1,0:T(8,128)(2,1)S(1)}, u32[]{:S(2)}, u32[]{:S(2)}) collective-permute-start(bf16[256,512]{1,0:T(8,128)(2,1)S(1)} %get-tuple-element.77), channel_id=1, source_target_pairs={{0,8},{16,24},{32,40},{48,56},{64,72},{80,88},{96,104},{112,120},{... | collective-permute-start | bytes 786440 | tf_op jit(solution)/shard_map/ppermute | solution.py:456
  32.6 11.2 %collective-permute-start.13 = (bf16[256,512]{1,0:T(8,128)(2,1)S(1)}, bf16[256,512]{1,0:T(8,128)(2,1)S(1)}, u32[]{:S(2)}, u32[]{:S(2)}) collective-permute-start(bf16[256,512]{1,0:T(8,128)(2,1)S(1)} %get-tuple-element.78), channel_id=1, source_target_pairs={{8,16},{24,32},{40,48},{56,64},{72,80},{88,96},{104,112},{16,8},{3... | collective-permute-start | bytes 786440 | tf_op jit(solution)/shard_map/ppermute | solution.py:456
  36.3 5.5 %collective-permute-start.14 = (bf16[2,256,128]{2,1,0:T(8,128)(2,1)S(1)}, bf16[2,256,128]{2,1,0:T(8,128)(2,1)S(1)}, u32[]{:S(2)}, u32[]{:S(2)}) collective-permute-start(bf16[2,256,128]{2,1,0:T(8,128)(2,1)S(1)} %get-tuple-element.79), channel_id=1, source_target_pairs={{0,1},{1,0},{2,3},{3,2},{4,5},{5,4},{6,7},{7,6},{8,9},{9,8},{10,11... | collective-permute-start | bytes 393224 | tf_op jit(solution)/shard_map/ppermute | solution.py:452
  37.3 4.5 %collective-permute-start.15 = (bf16[2,256,128]{2,1,0:T(8,128)(2,1)S(1)}, bf16[2,256,128]{2,1,0:T(8,128)(2,1)S(1)}, u32[]{:S(2)}, u32[]{:S(2)}) collective-permute-start(bf16[2,256,128]{2,1,0:T(8,128)(2,1)S(1)} %get-tuple-element.80), channel_id=1, source_target_pairs={{1,2},{3,4},{5,6},{2,1},{4,3},{6,5},{9,10},{11,12},{13,14},{10,9},... | collective-permute-start | bytes 393224 | tf_op jit(solution)/shard_map/ppermute | solution.py:456
  46.9 10.3 %collective-permute-start.16 = (bf16[256,512]{1,0:T(8,128)(2,1)S(1)}, bf16[256,512]{1,0:T(8,128)(2,1)S(1)}, u32[]{:S(2)}, u32[]{:S(2)}) collective-permute-start(bf16[256,512]{1,0:T(8,128)(2,1)S(1)} %get-tuple-element.84), channel_id=1, source_target_pairs={{0,8},{16,24},{32,40},{48,56},{64,72},{80,88},{96,104},{112,120},{... | collective-permute-start | bytes 786440 | tf_op jit(solution)/shard_map/ppermute | solution.py:456
  47.0 10.3 %collective-permute-start.17 = (bf16[256,512]{1,0:T(8,128)(2,1)S(1)}, bf16[256,512]{1,0:T(8,128)(2,1)S(1)}, u32[]{:S(2)}, u32[]{:S(2)}) collective-permute-start(bf16[256,512]{1,0:T(8,128)(2,1)S(1)} %get-tuple-element.85), channel_id=1, source_target_pairs={{8,16},{24,32},{40,48},{56,64},{72,80},{88,96},{104,112},{16,8},{3... | collective-permute-start | bytes 786440 | tf_op jit(solution)/shard_map/ppermute | solution.py:456
  50.7 6.5 %collective-permute-start.18 = (bf16[2,256,128]{2,1,0:T(8,128)(2,1)S(1)}, bf16[2,256,128]{2,1,0:T(8,128)(2,1)S(1)}, u32[]{:S(2)}, u32[]{:S(2)}) collective-permute-start(bf16[2,256,128]{2,1,0:T(8,128)(2,1)S(1)} %get-tuple-element.86), channel_id=1, source_target_pairs={{0,1},{1,0},{2,3},{3,2},{4,5},{5,4},{6,7},{7,6},{8,9},{9,8},{10,11... | collective-permute-start | bytes 393224 | tf_op jit(solution)/shard_map/ppermute | solution.py:452
  52.6 4.6 %collective-permute-start.19 = (bf16[2,256,128]{2,1,0:T(8,128)(2,1)S(1)}, bf16[2,256,128]{2,1,0:T(8,128)(2,1)S(1)}, u32[]{:S(2)}, u32[]{:S(2)}) collective-permute-start(bf16[2,256,128]{2,1,0:T(8,128)(2,1)S(1)} %get-tuple-element.87), channel_id=1, source_target_pairs={{1,2},{3,4},{5,6},{2,1},{4,3},{6,5},{9,10},{11,12},{13,14},{10,9},... | collective-permute-start | bytes 393224 | tf_op jit(solution)/shard_map/ppermute | solution.py:456
  59.7 20.9 %collective-permute-start.20 = (bf16[2,2,64,512]{3,2,1,0:T(8,128)(2,1)S(1)}, bf16[2,2,64,512]{3,2,1,0:T(8,128)(2,1)S(1)}, u32[]{:S(2)}, u32[]{:S(2)}) collective-permute-start(bf16[2,2,64,512]{3,2,1,0:T(8,128)(2,1)S(1)} %get-tuple-element.90), channel_id=1, source_target_pairs={{0,4},{1,5},{2,6},{3,7},{4,0},{5,1},{6,2},{7,3},{8,12},{9,13},{10,... | collective-permute-start | bytes 786440 | tf_op jit(solution)/shard_map/ppermute | solution.py:452
  62.4 18.1 %collective-permute-start.21 = (bf16[2,2,64,512]{3,2,1,0:T(8,128)(2,1)S(1)}, bf16[2,2,64,512]{3,2,1,0:T(8,128)(2,1)S(1)}, u32[]{:S(2)}, u32[]{:S(2)}) collective-permute-start(bf16[2,2,64,512]{3,2,1,0:T(8,128)(2,1)S(1)} %get-tuple-element.91), channel_id=1, source_target_pairs={{0,6},{1,7},{2,4},{3,5},{4,2},{5,3},{6,0},{7,1},{8,14},{9,15},{10,... | collective-permute-start | bytes 786440 | tf_op jit(solution)/shard_map/ppermute | solution.py:452
  71.3 3.0 %collective-permute-start.22 = (bf16[1,2,64,512]{3,2,1,0:T(8,128)(2,1)S(1)}, bf16[1,2,64,512]{3,2,1,0:T(8,128)(2,1)S(1)}, u32[]{:S(2)}, u32[]{:S(2)}) collective-permute-start(bf16[1,2,64,512]{3,2,1,0:T(8,128)(2,1)S(1)} %get-tuple-element.94), channel_id=1, source_target_pairs={{0,1},{1,0},{2,3},{3,2},{4,5},{5,4},{6,7},{7,6},{8,9},{9,8},{10,11... | collective-permute-start | bytes 393224 | tf_op jit(solution)/shard_map/ppermute | solution.py:452
  72.5 5.1 %collective-permute-start.23 = (bf16[1,2,64,512]{3,2,1,0:T(8,128)(2,1)S(1)}, bf16[1,2,64,512]{3,2,1,0:T(8,128)(2,1)S(1)}, u32[]{:S(2)}, u32[]{:S(2)}) collective-permute-start(bf16[1,2,64,512]{3,2,1,0:T(8,128)(2,1)S(1)} %get-tuple-element.95), channel_id=1, source_target_pairs={{0,2},{1,3},{2,0},{3,1},{4,6},{5,7},{6,4},{7,5},{8,10},{9,11},{10,... | collective-permute-start | bytes 393224 | tf_op jit(solution)/shard_map/ppermute | solution.py:452
  72.5 8.0 %collective-permute-start.24 = (bf16[1,2,64,512]{3,2,1,0:T(8,128)(2,1)S(1)}, bf16[1,2,64,512]{3,2,1,0:T(8,128)(2,1)S(1)}, u32[]{:S(2)}, u32[]{:S(2)}) collective-permute-start(bf16[1,2,64,512]{3,2,1,0:T(8,128)(2,1)S(1)} %get-tuple-element.96), channel_id=1, source_target_pairs={{0,3},{1,2},{2,1},{3,0},{4,7},{5,6},{6,5},{7,4},{8,11},{9,10},{10,... | collective-permute-start | bytes 393224 | tf_op jit(solution)/shard_map/ppermute | solution.py:452
  80.6 1.5 %collective-permute-start.25 = (bf16[2,2,64,512]{3,2,1,0:T(8,128)(2,1)S(1)}, bf16[2,2,64,512]{3,2,1,0:T(8,128)(2,1)S(1)}, u32[]{:S(2)}, u32[]{:S(2)}) collective-permute-start(bf16[2,2,64,512]{3,2,1,0:T(8,128)(2,1)S(1)} %collective-permute-done.20.refs_4_), channel_id=1, source_target_pairs={{0,1},{1,0},{2,3},{3,2},{4,5},{5,4},{6,7},{7,6},{8,9},{9,8},{10,11... | collective-permute-start | bytes 786440 | tf_op jit(solution)/shard_map/ppermute | solution.py:452
  80.8 1.7 %collective-permute-start.26 = (bf16[2,2,64,512]{3,2,1,0:T(8,128)(2,1)S(1)}, bf16[2,2,64,512]{3,2,1,0:T(8,128)(2,1)S(1)}, u32[]{:S(2)}, u32[]{:S(2)}) collective-permute-start(bf16[2,2,64,512]{3,2,1,0:T(8,128)(2,1)S(1)} %collective-permute-done.21.refs_6_), channel_id=1, source_target_pairs={{0,1},{1,0},{2,3},{3,2},{4,5},{5,4},{6,7},{7,6},{8,9},{9,8},{10,11... | collective-permute-start | bytes 786440 | tf_op jit(solution)/shard_map/ppermute | solution.py:452
where the time goes:
time: 85 us; the launch traced here: 84.6 us
  Pallas kernels  35.5 us (42%)
  starting transfers between devices  31.2 us (37%)
  waiting for transfers between devices  16.8 us (20%)
    ppermute x20, starting transfers between devices, send(): return lax.ppermute(v, RING, [(i, i ^ k) for i in range(N)])  20.8 us
    pallas_call x4, Pallas kernels, react_call(): pl.pallas_call(functools.partial(react, far), grid=(2,), out_shape=jax.Sh...  15.1 us
    ppermute x20, waiting for transfers between devices, send(): return lax.ppermute(v, RING, [(i, i ^ k) for i in range(N)])  11.4 us
    ppermute x6, starting transfers between devices, swap(): lax.ppermute(v, axis, [(i, i + 1) for i in firsts] + [(i + 1, i) for i in...  10.2 us
    pallas_call x2, Pallas kernels, finish_call(): pl.pallas_call(functools.partial(finish, which), grid_spec=pltpu.Prefetch...  4.79 us
    pallas_call x1, Pallas kernels, state_call(): pl.pallas_call(pack_state, out_shape=(m(128), m(128), m(256), m(256), m(F...  4.18 us
    ppermute x1, waiting for transfers between devices, on_device(): lax.ppermute(w, RING, [(i, i ^ (6 if i % 2 else 2)) for i in range(N)])  3.32 us
    pallas_call x1, Pallas kernels, advance_call(): pl.pallas_call(advance, grid_spec=pltpu.PrefetchScalarGridSpec(num_scalar...  3.09 us
  transfers between devices with their start and end apart: 27, of which 11 were waited for; matrix products, arithmetic and copies ran while one was open for 1% of the time, Pallas kernels for 29%

commit v1 on v0

--- a/solution.py
+++ b/solution.py
@@ -210,15 +210,15 @@
     )(info, *pieces)
 
 
-def put_edges(info_ref, a, b, ev_ref, od_ref, peer_ref, chip_ref):
+def put_edges(info_ref, a, b, ev_ref, od_ref, peer_ref, chip_ref, rows):
     me = info_ref[0]
     first = (me >> 2) == 0
     core = me & 1
     even = (info_ref[1] & 1) == 0
     lo = jnp.where(first, a[0].astype(F32), b[0].astype(F32))
     hi = jnp.where(first, b[1].astype(F32), a[1].astype(F32))
-    ev_ref[...] = jnp.where(even, hi, lo).astype(BF16)
-    od_ref[...] = jnp.where(even, lo, hi).astype(BF16)
+    ev_ref[rows, :] = jnp.where(even, hi, lo).astype(BF16)
+    od_ref[rows, :] = jnp.where(even, lo, hi).astype(BF16)
     for q in range(2):
         sides = []
         for cut in (slice(0, 128), slice(LN - 128, LN)):
@@ -227,8 +227,8 @@
         low = lax.broadcasted_iota(jnp.int32, sides[0][0].shape, 1) < GY
         left = jnp.where(low, sides[0][0], pltpu.roll(sides[0][1], GY, 1))
         right = jnp.where(low, pltpu.roll(sides[1][0], GY, 1), sides[1][1])
-        peer_ref[q] = jnp.where(core == 0, right, left).astype(BF16)
-        chip_ref[q] = jnp.where(core == 0, left, right).astype(BF16)
+        peer_ref[q, rows, :] = jnp.where(core == 0, right, left).astype(BF16)
+        chip_ref[q, rows, :] = jnp.where(core == 0, left, right).astype(BF16)
 
 
 EDGES = (
@@ -239,20 +239,28 @@
 )
 
 
-def edge_kernel(info_ref, a_ref, b_ref, *edges):
-    put_edges(info_ref, [a_ref[0], a_ref[1]], [b_ref[0], b_ref[1]], *edges)
-
-
-def edges_call(info, a, b):
-    return pl.pallas_call(
-        edge_kernel,
-        out_shape=EDGES,
-        in_specs=[SMEM, VMEM, VMEM],
-        out_specs=(VMEM,) * 4,
+def gather_far(at, info_ref, a_ref, *refs):
+    pieces, out_ref, edges = refs[:4], refs[4], refs[5:]
+    gather_planes(at, info_ref, *pieces, out_ref)
+
+    def block(s, _):
+        rows = pl.ds(pl.multiple_of(s * SB, SB), SB)
+        put_edges(info_ref, [a_ref[0, rows, :], a_ref[1, rows, :]], [out_ref[0, rows, :], out_ref[1, rows, :]], *edges, rows)
+        return 0
+
+    lax.fori_loop(0, S // SB, block, 0)
+
+
+def gather_far_call(info, a, pieces, at):
+    return pl.pallas_call(
+        functools.partial(gather_far, at),
+        out_shape=(jax.ShapeDtypeStruct((2, S, LN), BF16),) + EDGES,
+        in_specs=[SMEM] + [VMEM] * 5,
+        out_specs=(VMEM,) * 5,
         compiler_params=params(6),
-        name="edges",
-        cost_estimate=COST,
-    )(info, a, b)
+        name="gather_far",
+        cost_estimate=COST,
+    )(info, a, *pieces)
 
 
 def react(far, conc_ref, cell_ref, order_ref, stoich_ref, load_ref, lr_ref, change_ref, flux_s):
@@ -348,72 +356,65 @@
     return [ref[0], ref[1]]
 
 
+ROWS = 32
+
+
+def near_rows(rows, a_ref, b_ref, ev_ref, od_ref, peer_ref, chip_ref):
+    def pair(ref):
+        return [ref[0, rows, :], ref[1, rows, :]]
+
+    return pair(a_ref), pair(b_ref), ev_ref[rows, :], od_ref[rows, :], pair(peer_ref), pair(chip_ref)
+
+
 def advance(info_ref, a_ref, b_ref, da_ref, db_ref, ev_ref, od_ref, peer_ref, chip_ref, coef_ref, na_ref, nb_ref, *edges):
-    a, b = two(a_ref), two(b_ref)
-    args = (ev_ref[...], od_ref[...], two(peer_ref), two(chip_ref))
-    new = [diffuse(info_ref, w, a, b, *args, two(d), coef_ref[...]) for w, d in ((0, da_ref), (1, db_ref))]
-    for v, ref in zip(new, (na_ref, nb_ref)):
-        ref[0], ref[1] = v
-    put_edges(info_ref, *new, *edges)
-
-
-ROWS = 64
-
-
-def specs_of(at):
-    return dict(
-        two=pl.BlockSpec((2, ROWS, LN), lambda s, i: (0, at(s, i), 0)),
-        one=pl.BlockSpec((ROWS, LN), lambda s, i: (at(s, i), 0)),
-        side=pl.BlockSpec((2, ROWS, 128), lambda s, i: (0, at(s, i), 0)),
-        col=pl.BlockSpec((ROWS, 128), lambda s, i: (at(s, i), 0)),
-    )
+    def block(s, _):
+        rows = pl.ds(pl.multiple_of(s * ROWS, ROWS), ROWS)
+        args = near_rows(rows, a_ref, b_ref, ev_ref, od_ref, peer_ref, chip_ref)
+        new = []
+        for which, d_ref, out_ref in ((0, da_ref, na_ref), (1, db_ref, nb_ref)):
+            new.append(diffuse(info_ref, which, *args, [d_ref[0, rows, :], d_ref[1, rows, :]], coef_ref[rows, :]))
+            out_ref[0, rows, :], out_ref[1, rows, :] = new[-1]
+        put_edges(info_ref, *new, *edges, rows)
+        return 0
+
+    lax.fori_loop(0, S // ROWS, block, 0, unroll=4)
 
 
 def advance_call(info, a, b, da, db, halos, coef):
-    n = specs_of(lambda s, i: s)
     pair = jax.ShapeDtypeStruct((2, S, LN), F32)
     return pl.pallas_call(
         advance,
-        grid_spec=pltpu.PrefetchScalarGridSpec(
-            num_scalar_prefetch=1,
-            grid=(S // ROWS,),
-            in_specs=[n["two"]] * 4 + [n["one"]] * 2 + [n["side"]] * 2 + [n["col"]],
-            out_specs=[n["two"]] * 2 + [n["one"]] * 2 + [n["side"]] * 2,
-        ),
+        in_specs=[SMEM] + [VMEM] * 9,
+        out_specs=(VMEM,) * 6,
         out_shape=(pair, pair) + EDGES,
-        compiler_params=params(12),
+        compiler_params=params(16),
         name="advance",
         cost_estimate=COST,
     )(info, a, b, da, db, *halos, coef)
 
 
 def finish(which, info_ref, a_ref, b_ref, d_ref, ev_ref, od_ref, peer_ref, chip_ref, coef_ref, *outs):
-    new = diffuse(info_ref, which, two(a_ref), two(b_ref), ev_ref[...], od_ref[...], two(peer_ref), two(chip_ref),
-                  two(d_ref), coef_ref[...])
-    j = pl.program_id(0)
-    each = 4 // len(outs)
-    for n, ref in enumerate(outs):
-        @pl.when(j // each == n)
-        def _(ref=ref):
-            ref[0, 0], ref[0, 1] = [v.astype(BF16) for v in new]
-
-
-def finish_call(which, info, a, b, d, halos, coef, count):
-    n = specs_of(lambda s, i: (i[0] & 3) ^ s)
-    each = 4 // count
-    m = jax.ShapeDtypeStruct((each, 2, SB, LN), BF16)
+    me = info_ref[0]
+    places = [(ref, i) for ref in outs for i in range(ref.shape[0])]
+    for j, (out, at) in enumerate(places):
+        def block(s, _, j=j, out=out, at=at):
+            rows = pl.ds(pl.multiple_of(((me & 3) ^ j) * SB + s * ROWS, ROWS), ROWS)
+            to = pl.ds(pl.multiple_of(s * ROWS, ROWS), ROWS)
+            args = near_rows(rows, a_ref, b_ref, ev_ref, od_ref, peer_ref, chip_ref)
+            new = diffuse(info_ref, which, *args, [d_ref[0, rows, :], d_ref[1, rows, :]], coef_ref[rows, :])
+            for p in range(2):
+                out[at, p, to, :] = new[p].astype(BF16)
+            return 0
+
+        lax.fori_loop(0, SB // ROWS, block, 0, unroll=True)
+
+
+def finish_call(which, info, a, b, d, halos, coef, counts):
     return pl.pallas_call(
         functools.partial(finish, which),
-        grid_spec=pltpu.PrefetchScalarGridSpec(
-            num_scalar_prefetch=1,
-            grid=(4,),
-            in_specs=[n["two"]] * 3 + [n["one"]] * 2 + [n["side"]] * 2 + [n["col"]],
-            out_specs=[
-                pl.BlockSpec((1, 2, SB, LN), lambda s, i, n=n: (jnp.clip(s - each * n, 0, each - 1), 0, 0, 0))
-                for n in range(count)
-            ],
-        ),
-        out_shape=(m,) * count,
+        in_specs=[SMEM] + [VMEM] * 8,
+        out_specs=(VMEM,) * len(counts),
+        out_shape=[jax.ShapeDtypeStruct((n, 2, SB, LN), BF16) for n in counts],
         compiler_params=params(12),
         name="finish",
         cost_estimate=COST,
@@ -458,12 +459,9 @@
 
 def exchange(edges):
     ev, od, peer, chip = edges
-    return (
-        swap(ev, "zy", range(0, 15, 2)),
-        swap(od, "zy", range(1, 15, 2)),
-        send(peer, 1),
-        swap(chip, RING, (1, 3, 5)),
-    )
+    od = swap(od, "zy", range(1, 15, 2))
+    ev = swap(ev, "zy", range(0, 15, 2))
+    return ev, od, send(peer, 1), swap(chip, RING, (1, 3, 5))
 
 
 def on_device(conc, order, stoich, species_class, diff_coef, rate, noise_load, cell_noise):
@@ -484,20 +482,20 @@
     da = react_call(0, a, near, ws)
     opp, outer, da = lax.optimization_barrier((opp, outer, da))
     cells = outer
-    b = gather_call(info, [opp, send(opp, 1), outer, send(outer, 1)], (0, 2, 0, 2))
-    around = exchange(edges_call(info, a, b))
+    b, *edges = gather_far_call(info, a, [opp, send(opp, 1), outer, send(outer, 1)], (0, 2, 0, 2))
+    around = exchange(edges)
     db = react_call(0, b, cells, ws, far=True)
     a, b, *edges = advance_call(info, a, b, da, db, around, coef)
     around = exchange(edges)
     db = react_call(1, b, cells, ws, far=True)
-    opp, outer = finish_call(1, info, a, b, db, around, coef, 2)
+    opp, outer = finish_call(1, info, a, b, db, around, coef, (2, 2))
     opp, outer, near = lax.optimization_barrier((opp, outer, near))
     opp, outer = send(opp, 4), send(outer, 6)
     da = react_call(1, a, near, ws)
-    near_out = finish_call(0, info, a, b, da, around, coef, 4)
-    back = [near_out[0]] + [send(near_out[k], k) for k in range(1, 4)]
-    opp, outer, *back = lax.optimization_barrier((opp, outer, *back))
-    back += [opp, send(opp, 1), outer, send(outer, 1)]
+    mine, peer, inner = finish_call(0, info, a, b, da, around, coef, (1, 1, 2))
+    opp, outer, mine = lax.optimization_barrier((opp, outer, mine))
+    inner = send(inner, 2)
+    back = [mine, send(peer, 1), inner, send(inner[1:], 1), opp, send(opp, 1), outer, send(outer, 1)]
     return join_call(info, back, (0, 0, 0, 0, 0, 1, 0, 1))
 
 

time: 85 us -> 81.1 us (0.954)
  Pallas kernels: 35.5 us -> 33 us
  waiting for transfers between devices: 16.8 us -> 15.6 us
    pallas_call x4, Pallas kernels: 8.72 us -> 6.86 us  [the longest x2 3.1 us: finish_call(): pl.pallas_call(functools.partial(finish, which), in_specs=[SMEM] + [VMEM]...]
    ppermute x20, waiting for transfers between devices: 11.4 us -> 10.2 us  [send(): return lax.ppermute(v, RING, [(i, i ^ k) for i in range(N)])]
  transfers between devices with their start and end apart: 27 -> 27, of which waited for: 11 -> 10; matrix products, arithmetic and copies ran while one was open for 1% -> 1% of each run, Pallas kernels for 29% -> 29%
where the time goes in v1:
time: 81.1 us; the launch traced here: 80.9 us
  Pallas kernels  33 us (41%)
  starting transfers between devices  31 us (38%)
  waiting for transfers between devices  15.6 us (19%)
    ppermute x20, starting transfers between devices, send(): return lax.ppermute(v, RING, [(i, i ^ k) for i in range(N)])  20.6 us
    pallas_call x4, Pallas kernels, react_call(): pl.pallas_call(functools.partial(react, far), grid=(2,), out_shape=jax.Sh...  15.1 us
    ppermute x6, starting transfers between devices, swap(): lax.ppermute(v, axis, [(i, i + 1) for i in firsts] + [(i + 1, i) for i in...  10.2 us
    ppermute x20, waiting for transfers between devices, send(): return lax.ppermute(v, RING, [(i, i ^ k) for i in range(N)])  10.2 us
    pallas_call x1, Pallas kernels, state_call(): pl.pallas_call(pack_state, out_shape=(m(128), m(128), m(256), m(256), m(F...  4.18 us
    ppermute x1, waiting for transfers between devices, on_device(): lax.ppermute(w, RING, [(i, i ^ (6 if i % 2 else 2)) for i in range(N)])  3.32 us
    pallas_call x2, Pallas kernels, finish_call(): pl.pallas_call(functools.partial(finish, which), in_specs=[SMEM] + [VMEM]...  3.1 us
    pallas_call x1, Pallas kernels, advance_call(): pl.pallas_call(advance, in_specs=[SMEM] + [VMEM] * 9, out_specs=(VMEM,) *...  2.72 us
  transfers between devices with their start and end apart: 27, of which 10 were waited for; matrix products, arithmetic and copies ran while one was open for 1% of the time, Pallas kernels for 29%

profile of v1, /device:TPU:103, one launch (start us, length us, event | category | flops | bytes accessed | tf_op | source)
XLA Modules:
  0.0 80.9 jit_solution(1283802397479778332)
XLA Ops:
  0.0 2.2 %pack_weights.1.refs_0_ = bf16[2,656,256]{2,1,0:T(8,128)(2,1)} custom-call(s32[512,256]{1,0:T(8,128)} %order_ref.1, s32[256,512]{1,0:T(8,128)} %stoich_ref.1, f32[2,32,512]{2,1,0:T(8,128)} %bitcast.5, f32[1,512]{1,0:T(1,128)} %bitcast.6, s32[1,64]{1,0:T(1,128)} %bitcast.7, f32[4]{0:T(128)} %coef_ref.1), custom_call_target="tpu_custom_call" | custom-call | flops 1 | bytes 1 | tf_op jit(solution)/shard_map/pack_weights/pallas_call | solution.py:70
  2.4 1.3 %collective-permute-start.3 = (bf16[2,656,256]{2,1,0:T(8,128)(2,1)}, bf16[2,656,256]{2,1,0:T(8,128)(2,1)S(1)}, u32[]{:S(2)}, u32[]{:S(2)}) collective-permute-start(bf16[2,656,256]{2,1,0:T(8,128)(2,1)} %pack_weights.1.refs_0_), channel_id=1, source_target_pairs={{0,1},{1,0},{2,3},{3,2},{4,5},{5,4},{6,7},{7,6},{8,9},{9,8},{10,11... | collective-permute-start | bytes 2015240 | tf_op jit(solution)/shard_map/ppermute | solution.py:453
  4.4 4.2 %pack_state.1 = (bf16[128,512]{1,0:T(8,128)(2,1)}, bf16[128,512]{1,0:T(8,128)(2,1)}, bf16[256,512]{1,0:T(8,128)(2,1)}, bf16[256,512]{1,0:T(8,128)(2,1)}, bf16[38...) custom-call(s32[2]{0:T(128)} %pad_add_fusion.info_ref, f32[64,2,4096]{2,1,0:T(2,128)} %conc_ref.1, ...), custom_call_target="tpu_custom_call" | custom-call | flops 1 | bytes 1 | tf_op jit(solution)/shard_map/pack_state/pallas_call | solution.py:124
  8.5 1.0 %collective-permute-start.2 = (bf16[256,512]{1,0:T(8,128)(2,1)}, bf16[256,512]{1,0:T(8,128)(2,1)S(1)}, u32[]{:S(2)}, u32[]{:S(2)}) collective-permute-start(bf16[256,512]{1,0:T(8,128)(2,1)} %get-tuple-element.55), channel_id=1, source_target_pairs={{0,2},{1,3},{2,0},{3,1},{4,6},{5,7},{6,4},{7,5},{8,10},{9,11},{10,... | collective-permute-start | bytes 786440 | tf_op jit(solution)/shard_map/ppermute | solution.py:453
  9.9 3.3 %collective-permute-done.refs_2_ = bf16[2,656,256]{2,1,0:T(8,128)(2,1)S(1)} collective-permute-done((bf16[2,656,256]{2,1,0:T(8,128)(2,1)}, bf16[2,656,256]{2,1,0:T(8,128)(2,1)S(1)}, u32[]{:S(2)}, u32[]{:S(2)}) %collective-permute-start) | collective-permute-done | bytes 671776 | tf_op jit(solution)/shard_map/ppermute | solution.py:472
  13.2 2.5 %collective-permute-start.6 = (bf16[2,208,256]{2,1,0:T(8,128)(2,1)S(1)}, bf16[2,208,256]{2,1,0:T(8,128)(2,1)S(1)}, u32[]{:S(2)}, u32[]{:S(2)}) collective-permute-start(bf16[2,208,256]{2,1,0:T(8,128)(2,1)S(1)} %slice.17), channel_id=1, source_target_pairs={{0,1},{1,0},{2,3},{3,2},{4,5},{5,4},{6,7},{7,6},{8,9},{9,8},{10,11... | collective-permute-start | bytes 638984 | tf_op jit(solution)/shard_map/ppermute | solution.py:453
  16.9 1.4 %collective-permute-start.8 = (bf16[256,512]{1,0:T(8,128)(2,1)}, bf16[256,512]{1,0:T(8,128)(2,1)S(1)}, u32[]{:S(2)}, u32[]{:S(2)}) collective-permute-start(bf16[256,512]{1,0:T(8,128)(2,1)} %get-tuple-element.64), channel_id=1, source_target_pairs={{0,4},{1,5},{2,6},{3,7},{4,0},{5,1},{6,2},{7,3},{8,12},{9,13},{10,... | collective-permute-start | bytes 786440 | tf_op jit(solution)/shard_map/ppermute | solution.py:453
  18.9 2.2 %sort_weights.1 = (bf16[2048,256]{1,0:T(8,128)(2,1)S(1)}, bf16[256,2048]{1,0:T(8,128)(2,1)S(1)}, bf16[2,2048,128]{2,1,0:T(8,128)(2,1)S(1)}, f32[2048,128]{1,0:T(8,128)S(1)}, f32[256,128]{1,0:T(8,128)S(1)}) custom-call(s32[2]{0:T(128)S(1)} %copy-done.3, bf16[2,656,256]{2,1,0:T(8,128)(2,1)S(1)} %copy-done, ...), custom_call_target="tpu_custom_call" | custom-call | flops 1 | bytes 1 | tf_op jit(solution)/shard_map/sort_weights/pallas_call | solution.py:175
  21.2 1.3 %collective-permute-done.7.refs_3_ = bf16[128,512]{1,0:T(8,128)(2,1)S(1)} collective-permute-done((bf16[128,512]{1,0:T(8,128)(2,1)S(1)}, bf16[128,512]{1,0:T(8,128)(2,1)S(1)}, u32[]{:S(2)}, u32[]{:S(2)}) %collective-permute-start.7) | collective-permute-done | bytes 131104 | tf_op jit(solution)/shard_map/ppermute | solution.py:453
  23.1 3.8 %react.4.da_ref = f32[2,256,512]{2,1,0:T(8,128)S(1)} custom-call(bf16[2,256,512]{2,1,0:T(8,128)(2,1)S(1)} %gather_planes.1.conc_ref.a_ref, bf16[2,2,64,512]{3,2,1,0:T(8,128)(2,1)S(1)} %copy-done.1, bf16[2048,256]{1,0:T(8,128)(2,1)S(1)} %get-tuple-element.67.order_ref, bf16[256,2048]{1,0:T(8,128)(2,1)S(1)} %get-tuple-element.68.stoich_ref, ...), custom_call_target="tpu_custom_call" | custom-call | flops 1 | bytes 1 | tf_op jit(solution)/shard_map/react/pallas_call | solution.py:291
  27.0 1.1 %collective-permute-start.11 = (bf16[384,512]{1,0:T(8,128)(2,1)S(1)}, bf16[384,512]{1,0:T(8,128)(2,1)S(1)}, u32[]{:S(2)}, u32[]{:S(2)}) collective-permute-start(bf16[384,512]{1,0:T(8,128)(2,1)S(1)} %collective-permute-done.9.refs_2_.cell_ref), channel_id=1, source_target_pairs={{0,1},{1,0},{2,3},{3,2},{4,5},{5,4},{6,7},{7,6},{8,9},{9,8},{10,11... | collective-permute-start | bytes 1179656 | tf_op jit(solution)/shard_map/ppermute | solution.py:453
  28.1 1.7 %collective-permute-done.10.refs_1_ = bf16[256,512]{1,0:T(8,128)(2,1)S(1)} collective-permute-done((bf16[256,512]{1,0:T(8,128)(2,1)S(1)}, bf16[256,512]{1,0:T(8,128)(2,1)S(1)}, u32[]{:S(2)}, u32[]{:S(2)}) %collective-permute-start.10) | collective-permute-done | bytes 262176 | tf_op jit(solution)/shard_map/ppermute | solution.py:453
  29.8 1.0 %gather_far.1 = (bf16[2,256,512]{2,1,0:T(8,128)(2,1)S(1)}, bf16[256,512]{1,0:T(8,128)(2,1)S(1)}, bf16[256,512]{1,0:T(8,128)(2,1)S(1)}, bf16[2,256,128]{2,1,0:T(8,128)(2,1)S(1)}, bf16[2,256,128]{2,1,0:T(8,128)(2,1)S(1)}) custom-call(s32[2]{0:T(128)S(1)} %copy-done.3, bf16[2,256,512]{2,1,0:T(8,128)(2,1)S(1)} %gather_planes.1.conc_ref.a_ref, ...), custom_call_target="tpu_custom_call" | custom-call | flops 1 | bytes 1 | tf_op jit(solution)/shard_map/gather_far/pallas_call | solution.py:255
  30.9 1.4 %collective-permute-start.12 = (bf16[256,512]{1,0:T(8,128)(2,1)S(1)}, bf16[256,512]{1,0:T(8,128)(2,1)S(1)}, u32[]{:S(2)}, u32[]{:S(2)}) collective-permute-start(bf16[256,512]{1,0:T(8,128)(2,1)S(1)} %get-tuple-element.75), channel_id=1, source_target_pairs={{0,8},{16,24},{32,40},{48,56},{64,72},{80,88},{96,104},{112,120},{... | collective-permute-start | bytes 786440 | tf_op jit(solution)/shard_map/ppermute | solution.py:457
  32.3 3.6 %collective-permute-start.13 = (bf16[256,512]{1,0:T(8,128)(2,1)S(1)}, bf16[256,512]{1,0:T(8,128)(2,1)S(1)}, u32[]{:S(2)}, u32[]{:S(2)}) collective-permute-start(bf16[256,512]{1,0:T(8,128)(2,1)S(1)} %get-tuple-element.76), channel_id=1, source_target_pairs={{8,16},{24,32},{40,48},{56,64},{72,80},{88,96},{104,112},{16,8},{3... | collective-permute-start | bytes 786440 | tf_op jit(solution)/shard_map/ppermute | solution.py:457
  35.9 1.0 %collective-permute-start.14 = (bf16[2,256,128]{2,1,0:T(8,128)(2,1)S(1)}, bf16[2,256,128]{2,1,0:T(8,128)(2,1)S(1)}, u32[]{:S(2)}, u32[]{:S(2)}) collective-permute-start(bf16[2,256,128]{2,1,0:T(8,128)(2,1)S(1)} %get-tuple-element.77), channel_id=1, source_target_pairs={{0,1},{1,0},{2,3},{3,2},{4,5},{5,4},{6,7},{7,6},{8,9},{9,8},{10,11... | collective-permute-start | bytes 393224 | tf_op jit(solution)/shard_map/ppermute | solution.py:453
  37.6 3.8 %react.5.db_ref = f32[2,256,512]{2,1,0:T(8,128)S(1)} custom-call(bf16[2,256,512]{2,1,0:T(8,128)(2,1)S(1)} %get-tuple-element.73.conc_ref.b_ref, bf16[384,512]{1,0:T(8,128)(2,1)S(1)} %collective-permute-done.9.refs_2_.cell_ref, bf16[2048,256]{1,0:T(8,128)(2,1)S(1)} %get-tuple-element.67.order_ref, bf16[256,2048]{1,0:T(8,128)(2,1)S(1)} %get-tuple-element.68.stoich_ref, ...), custom_call_target="tpu_custom_call" | custom-call | flops 1 | bytes 1 | tf_op jit(solution)/shard_map/react/pallas_call | solution.py:291
  41.4 2.1 %collective-permute-done.13.od_ref = bf16[256,512]{1,0:T(8,128)(2,1)S(1)} collective-permute-done((bf16[256,512]{1,0:T(8,128)(2,1)S(1)}, bf16[256,512]{1,0:T(8,128)(2,1)S(1)}, u32[]{:S(2)}, u32[]{:S(2)}) %collective-permute-start.13) | collective-permute-done | bytes 262176 | tf_op jit(solution)/shard_map/ppermute | solution.py:457
  43.5 2.7 %advance.1 = (f32[2,256,512]{2,1,0:T(8,128)S(1)}, f32[2,256,512]{2,1,0:T(8,128)S(1)}, bf16[256,512]{1,0:T(8,128)(2,1)S(1)}, bf16[256,512]{1,0:T(8,128)(2,1)S(1)}...) custom-call(s32[2]{0:T(128)S(1)} %copy-done.3, ...), custom_call_target="tpu_custom_call" | custom-call | flops 1 | bytes 1 | tf_op jit(solution)/shard_map/advance/pallas_call | solution.py:385
  46.3 3.6 %collective-permute-start.17 = (bf16[256,512]{1,0:T(8,128)(2,1)S(1)}, bf16[256,512]{1,0:T(8,128)(2,1)S(1)}, u32[]{:S(2)}, u32[]{:S(2)}) collective-permute-start(bf16[256,512]{1,0:T(8,128)(2,1)S(1)} %get-tuple-element.83), channel_id=1, source_target_pairs={{8,16},{24,32},{40,48},{56,64},{72,80},{88,96},{104,112},{16,8},{3... | collective-permute-start | bytes 786440 | tf_op jit(solution)/shard_map/ppermute | solution.py:457
  49.9 1.9 %collective-permute-start.18 = (bf16[2,256,128]{2,1,0:T(8,128)(2,1)S(1)}, bf16[2,256,128]{2,1,0:T(8,128)(2,1)S(1)}, u32[]{:S(2)}, u32[]{:S(2)}) collective-permute-start(bf16[2,256,128]{2,1,0:T(8,128)(2,1)S(1)} %get-tuple-element.84), channel_id=1, source_target_pairs={{0,1},{1,0},{2,3},{3,2},{4,5},{5,4},{6,7},{7,6},{8,9},{9,8},{10,11... | collective-permute-start | bytes 393224 | tf_op jit(solution)/shard_map/ppermute | solution.py:453
  52.6 3.8 %react.6.d_ref = f32[2,256,512]{2,1,0:T(8,128)S(1)} custom-call(f32[2,256,512]{2,1,0:T(8,128)S(1)} %get-tuple-element.81.conc_ref.b_ref, bf16[384,512]{1,0:T(8,128)(2,1)S(1)} %collective-permute-done.9.refs_2_.cell_ref, bf16[2048,256]{1,0:T(8,128)(2,1)S(1)} %get-tuple-element.67.order_ref, bf16[256,2048]{1,0:T(8,128)(2,1)S(1)} %get-tuple-element.68.stoich_ref, ...), custom_call_target="tpu_custom_call" | custom-call | flops 1 | bytes 1 | tf_op jit(solution)/shard_map/react/pallas_call | solution.py:291
  56.5 1.5 %finish.2 = (bf16[2,2,64,512]{3,2,1,0:T(8,128)(2,1)S(1)}, bf16[2,2,64,512]{3,2,1,0:T(8,128)(2,1)S(1)}) custom-call(s32[2]{0:T(128)S(1)} %copy-done.3, f32[2,256,512]{2,1,0:T(8,128)S(1)} %get-tuple-element.80.a_ref.conc_ref, f32[2,256,512]{2,1,0:T(8,128)S(1)} %get-tuple-element.81.conc_ref.b_ref, f32[2,256,512]{2,1,0:T(8,128)S(1)} %react.6.d_ref, ...), custom_call_target="tpu_custom_call" | custom-call | flops 1 | bytes 1 | tf_op jit(solution)/shard_map/finish/pallas_call | solution.py:413
  58.1 2.8 %collective-permute-start.20 = (bf16[2,2,64,512]{3,2,1,0:T(8,128)(2,1)S(1)}, bf16[2,2,64,512]{3,2,1,0:T(8,128)(2,1)S(1)}, u32[]{:S(2)}, u32[]{:S(2)}) collective-permute-start(bf16[2,2,64,512]{3,2,1,0:T(8,128)(2,1)S(1)} %get-tuple-element.88), channel_id=1, source_target_pairs={{0,4},{1,5},{2,6},{3,7},{4,0},{5,1},{6,2},{7,3},{8,12},{9,13},{10,... | collective-permute-start | bytes 786440 | tf_op jit(solution)/shard_map/ppermute | solution.py:453
  60.9 2.6 %collective-permute-start.21 = (bf16[2,2,64,512]{3,2,1,0:T(8,128)(2,1)S(1)}, bf16[2,2,64,512]{3,2,1,0:T(8,128)(2,1)S(1)}, u32[]{:S(2)}, u32[]{:S(2)}) collective-permute-start(bf16[2,2,64,512]{3,2,1,0:T(8,128)(2,1)S(1)} %get-tuple-element.89), channel_id=1, source_target_pairs={{0,6},{1,7},{2,4},{3,5},{4,2},{5,3},{6,0},{7,1},{8,14},{9,15},{10,... | collective-permute-start | bytes 786440 | tf_op jit(solution)/shard_map/ppermute | solution.py:453
  63.5 3.7 %react.7.d_ref = f32[2,256,512]{2,1,0:T(8,128)S(1)} custom-call(f32[2,256,512]{2,1,0:T(8,128)S(1)} %get-tuple-element.80.a_ref.conc_ref, bf16[2,2,64,512]{3,2,1,0:T(8,128)(2,1)S(1)} %copy-done.1, bf16[2048,256]{1,0:T(8,128)(2,1)S(1)} %get-tuple-element.67.order_ref, bf16[256,2048]{1,0:T(8,128)(2,1)S(1)} %get-tuple-element.68.stoich_ref, ...), custom_call_target="tpu_custom_call" | custom-call | flops 1 | bytes 1 | tf_op jit(solution)/shard_map/react/pallas_call | solution.py:291
  67.3 1.6 %finish.3 = (bf16[1,2,64,512]{3,2,1,0:T(8,128)(2,1)S(1)}, bf16[1,2,64,512]{3,2,1,0:T(8,128)(2,1)S(1)}, bf16[2,2,64,512]{3,2,1,0:T(8,128)(2,1)S(1)}) custom-call(s32[2]{0:T(128)S(1)} %copy-done.3, f32[2,256,512]{2,1,0:T(8,128)S(1)} %get-tuple-element.80.a_ref.conc_ref, f32[2,256,512]{2,1,0:T(8,128)S(1)} %get-tuple-element.81.conc_ref.b_ref, ...), custom_call_target="tpu_custom_call" | custom-call | flops 1 | bytes 1 | tf_op jit(solution)/shard_map/finish/pallas_call | solution.py:413
  68.9 4.6 %collective-permute-done.21.refs_6_ = bf16[2,2,64,512]{3,2,1,0:T(8,128)(2,1)S(1)} collective-permute-done((bf16[2,2,64,512]{3,2,1,0:T(8,128)(2,1)S(1)}, bf16[2,2,64,512]{3,2,1,0:T(8,128)(2,1)S(1)}, u32[]{:S(2)}, u32[]{:S(2)}) %collective-permute-start.21) | collective-permute-done | bytes 262176 | tf_op jit(solution)/shard_map/ppermute | solution.py:453
  74.5 1.0 %collective-permute-done.23.refs_2_ = bf16[2,2,64,512]{3,2,1,0:T(8,128)(2,1)S(1)} collective-permute-done((bf16[2,2,64,512]{3,2,1,0:T(8,128)(2,1)S(1)}, bf16[2,2,64,512]{3,2,1,0:T(8,128)(2,1)S(1)}, u32[]{:S(2)}, u32[]{:S(2)}) %collective-permute-start.23) | collective-permute-done | bytes 262176 | tf_op jit(solution)/shard_map/ppermute | solution.py:453
  75.5 2.2 %collective-permute-start.24 = (bf16[1,2,64,512]{3,2,1,0:T(8,128)(2,1)S(1)}, bf16[1,2,64,512]{3,2,1,0:T(8,128)(2,1)S(1)}, u32[]{:S(2)}, u32[]{:S(2)}) collective-permute-start(bf16[1,2,64,512]{3,2,1,0:T(8,128)(2,1)S(1)} %slice.20), channel_id=1, source_target_pairs={{0,1},{1,0},{2,3},{3,2},{4,5},{5,4},{6,7},{7,6},{8,9},{9,8},{10,11... | collective-permute-start | bytes 393224 | tf_op jit(solution)/shard_map/ppermute | solution.py:453
  77.7 1.0 %collective-permute-done.24.refs_3_ = bf16[1,2,64,512]{3,2,1,0:T(8,128)(2,1)S(1)} collective-permute-done((bf16[1,2,64,512]{3,2,1,0:T(8,128)(2,1)S(1)}, bf16[1,2,64,512]{3,2,1,0:T(8,128)(2,1)S(1)}, u32[]{:S(2)}, u32[]{:S(2)}) %collective-permute-start.24) | collective-permute-done | bytes 131104 | tf_op jit(solution)/shard_map/ppermute | solution.py:453
  78.7 2.0 %join_out.1 = f32[64,2,4096]{2,1,0:T(2,128)} custom-call(s32[2]{0:T(128)S(1)} %copy-done.3, bf16[1,2,64,512]{3,2,1,0:T(8,128)(2,1)S(1)} %get-tuple-element.92.refs_0_, bf16[1,2,64,512]{3,2,1,0:T(8,128)(2,1)S(1)} %collective-permute-done.22.refs_1_, bf16[2,2,64,512]{3,2,1,0:T(8,128)(2,1)S(1)} %collective-permute-done.23.refs_2_, ...), custom_call_target="tpu_custom_call" | custom-call | flops 1 | bytes 1 | tf_op jit(solution)/shard_map/join_out/pallas_call | solution.py:440
  (48 shorter events, 6.6 us)
Async XLA Ops:
  2.2 11.0 %collective-permute-start = (bf16[2,656,256]{2,1,0:T(8,128)(2,1)}, bf16[2,656,256]{2,1,0:T(8,128)(2,1)S(1)}, u32[]{:S(2)}, u32[]{:S(2)}) collective-permute-start(bf16[2,656,256]{2,1,0:T(8,128)(2,1)} %pack_weights.1.refs_0_), channel_id=1, source_target_pairs={{0,2},{1,7},{2,0},{3,5},{4,6},{5,3},{6,4},{7,1},{8,10},{9,15},{10,... | collective-permute-start | bytes 2015240 | tf_op jit(solution)/shard_map/ppermute | solution.py:472
  2.4 13.5 %collective-permute-start.3 = (bf16[2,656,256]{2,1,0:T(8,128)(2,1)}, bf16[2,656,256]{2,1,0:T(8,128)(2,1)S(1)}, u32[]{:S(2)}, u32[]{:S(2)}) collective-permute-start(bf16[2,656,256]{2,1,0:T(8,128)(2,1)} %pack_weights.1.refs_0_), channel_id=1, source_target_pairs={{0,1},{1,0},{2,3},{3,2},{4,5},{5,4},{6,7},{7,6},{8,9},{9,8},{10,11... | collective-permute-start | bytes 2015240 | tf_op jit(solution)/shard_map/ppermute | solution.py:453
  4.4 14.5 %copy-start = (bf16[2,656,256]{2,1,0:T(8,128)(2,1)S(1)}, bf16[2,656,256]{2,1,0:T(8,128)(2,1)}, u32[]{:S(2)}) copy-start(bf16[2,656,256]{2,1,0:T(8,128)(2,1)} %pack_weights.1.refs_0_) | copy-start | bytes 2015236
  4.4 14.5 %copy-start.3 = (s32[2]{0:T(128)S(1)}, s32[2]{0:T(128)}, u32[]{:S(2)}) copy-start(s32[2]{0:T(128)} %pad_add_fusion.info_ref) | copy-start | bytes 28
  8.5 12.5 %collective-permute-start.2 = (bf16[256,512]{1,0:T(8,128)(2,1)}, bf16[256,512]{1,0:T(8,128)(2,1)S(1)}, u32[]{:S(2)}, u32[]{:S(2)}) collective-permute-start(bf16[256,512]{1,0:T(8,128)(2,1)} %get-tuple-element.55), channel_id=1, source_target_pairs={{0,2},{1,3},{2,0},{3,1},{4,6},{5,7},{6,4},{7,5},{8,10},{9,11},{10,... | collective-permute-start | bytes 786440 | tf_op jit(solution)/shard_map/ppermute | solution.py:453
  9.5 17.5 %collective-permute-start.9 = (bf16[384,512]{1,0:T(8,128)(2,1)}, bf16[384,512]{1,0:T(8,128)(2,1)S(1)}, u32[]{:S(2)}, u32[]{:S(2)}) collective-permute-start(bf16[384,512]{1,0:T(8,128)(2,1)} %get-tuple-element.65), channel_id=1, source_target_pairs={{0,6},{1,7},{2,4},{3,5},{4,2},{5,3},{6,0},{7,1},{8,14},{9,15},{10,... | collective-permute-start | bytes 1179656 | tf_op jit(solution)/shard_map/ppermute | solution.py:453
  13.2 9.3 %copy-start.2 = (bf16[128,512]{1,0:T(8,128)(2,1)S(1)}, bf16[128,512]{1,0:T(8,128)(2,1)}, u32[]{:S(2)}) copy-start(bf16[128,512]{1,0:T(8,128)(2,1)} %get-tuple-element.53.refs_0_) | copy-start | bytes 393220
  13.2 3.6 %collective-permute-start.6 = (bf16[2,208,256]{2,1,0:T(8,128)(2,1)S(1)}, bf16[2,208,256]{2,1,0:T(8,128)(2,1)S(1)}, u32[]{:S(2)}, u32[]{:S(2)}) collective-permute-start(bf16[2,208,256]{2,1,0:T(8,128)(2,1)S(1)} %slice.17), channel_id=1, source_target_pairs={{0,1},{1,0},{2,3},{3,2},{4,5},{5,4},{6,7},{7,6},{8,9},{9,8},{10,11... | collective-permute-start | bytes 638984 | tf_op jit(solution)/shard_map/ppermute | solution.py:453
  15.8 7.3 %copy-start.1 = (bf16[2,2,64,512]{3,2,1,0:T(8,128)(2,1)S(1)}, bf16[2,2,64,512]{3,2,1,0:T(8,128)(2,1)}, u32[]{:S(2)}) copy-start(bf16[2,2,64,512]{3,2,1,0:T(8,128)(2,1)} %get-tuple-element.90.cell_ref) | copy-start | bytes 786436
  15.8 2.4 %collective-permute-start.5 = (bf16[2,224,256]{2,1,0:T(8,128)(2,1)S(1)}, bf16[2,224,256]{2,1,0:T(8,128)(2,1)S(1)}, u32[]{:S(2)}, u32[]{:S(2)}) collective-permute-start(bf16[2,224,256]{2,1,0:T(8,128)(2,1)S(1)} %get-tuple-element.97), channel_id=1, source_target_pairs={{0,1},{1,0},{2,3},{3,2},{4,5},{5,4},{6,7},{7,6},{8,9},{9,8},{10,11... | collective-permute-start | bytes 688136 | tf_op jit(solution)/shard_map/ppermute | solution.py:453
  15.9 3.0 %collective-permute-start.4 = (bf16[2,224,256]{2,1,0:T(8,128)(2,1)S(1)}, bf16[2,224,256]{2,1,0:T(8,128)(2,1)S(1)}, u32[]{:S(2)}, u32[]{:S(2)}) collective-permute-start(bf16[2,224,256]{2,1,0:T(8,128)(2,1)S(1)} %get-tuple-element.98), channel_id=1, source_target_pairs={{0,1},{1,0},{2,3},{3,2},{4,5},{5,4},{6,7},{7,6},{8,9},{9,8},{10,11... | collective-permute-start | bytes 688136 | tf_op jit(solution)/shard_map/ppermute | solution.py:453
  16.9 10.0 %collective-permute-start.8 = (bf16[256,512]{1,0:T(8,128)(2,1)}, bf16[256,512]{1,0:T(8,128)(2,1)S(1)}, u32[]{:S(2)}, u32[]{:S(2)}) collective-permute-start(bf16[256,512]{1,0:T(8,128)(2,1)} %get-tuple-element.64), channel_id=1, source_target_pairs={{0,4},{1,5},{2,6},{3,7},{4,0},{5,1},{6,2},{7,3},{8,12},{9,13},{10,... | collective-permute-start | bytes 786440 | tf_op jit(solution)/shard_map/ppermute | solution.py:453
  18.2 3.0 %collective-permute-start.1 = (bf16[128,512]{1,0:T(8,128)(2,1)}, bf16[128,512]{1,0:T(8,128)(2,1)S(1)}, u32[]{:S(2)}, u32[]{:S(2)}) collective-permute-start(bf16[128,512]{1,0:T(8,128)(2,1)} %get-tuple-element.54), channel_id=1, source_target_pairs={{0,1},{1,0},{2,3},{3,2},{4,5},{5,4},{6,7},{7,6},{8,9},{9,8},{10,11... | collective-permute-start | bytes 393224 | tf_op jit(solution)/shard_map/ppermute | solution.py:453
  21.1 1.4 %collective-permute-start.7 = (bf16[128,512]{1,0:T(8,128)(2,1)S(1)}, bf16[128,512]{1,0:T(8,128)(2,1)S(1)}, u32[]{:S(2)}, u32[]{:S(2)}) collective-permute-start(bf16[128,512]{1,0:T(8,128)(2,1)S(1)} %slice.18), channel_id=1, source_target_pairs={{0,1},{1,0},{2,3},{3,2},{4,5},{5,4},{6,7},{7,6},{8,9},{9,8},{10,11... | collective-permute-start | bytes 393224 | tf_op jit(solution)/shard_map/ppermute | solution.py:453
  27.0 2.8 %collective-permute-start.11 = (bf16[384,512]{1,0:T(8,128)(2,1)S(1)}, bf16[384,512]{1,0:T(8,128)(2,1)S(1)}, u32[]{:S(2)}, u32[]{:S(2)}) collective-permute-start(bf16[384,512]{1,0:T(8,128)(2,1)S(1)} %collective-permute-done.9.refs_2_.cell_ref), channel_id=1, source_target_pairs={{0,1},{1,0},{2,3},{3,2},{4,5},{5,4},{6,7},{7,6},{8,9},{9,8},{10,11... | collective-permute-start | bytes 1179656 | tf_op jit(solution)/shard_map/ppermute | solution.py:453
  28.1 1.7 %collective-permute-start.10 = (bf16[256,512]{1,0:T(8,128)(2,1)S(1)}, bf16[256,512]{1,0:T(8,128)(2,1)S(1)}, u32[]{:S(2)}, u32[]{:S(2)}) collective-permute-start(bf16[256,512]{1,0:T(8,128)(2,1)S(1)} %collective-permute-done.8.refs_0_), channel_id=1, source_target_pairs={{0,1},{1,0},{2,3},{3,2},{4,5},{5,4},{6,7},{7,6},{8,9},{9,8},{10,11... | collective-permute-start | bytes 786440 | tf_op jit(solution)/shard_map/ppermute | solution.py:453
  30.9 10.5 %collective-permute-start.12 = (bf16[256,512]{1,0:T(8,128)(2,1)S(1)}, bf16[256,512]{1,0:T(8,128)(2,1)S(1)}, u32[]{:S(2)}, u32[]{:S(2)}) collective-permute-start(bf16[256,512]{1,0:T(8,128)(2,1)S(1)} %get-tuple-element.75), channel_id=1, source_target_pairs={{0,8},{16,24},{32,40},{48,56},{64,72},{80,88},{96,104},{112,120},{... | collective-permute-start | bytes 786440 | tf_op jit(solution)/shard_map/ppermute | solution.py:457
  32.3 11.2 %collective-permute-start.13 = (bf16[256,512]{1,0:T(8,128)(2,1)S(1)}, bf16[256,512]{1,0:T(8,128)(2,1)S(1)}, u32[]{:S(2)}, u32[]{:S(2)}) collective-permute-start(bf16[256,512]{1,0:T(8,128)(2,1)S(1)} %get-tuple-element.76), channel_id=1, source_target_pairs={{8,16},{24,32},{40,48},{56,64},{72,80},{88,96},{104,112},{16,8},{3... | collective-permute-start | bytes 786440 | tf_op jit(solution)/shard_map/ppermute | solution.py:457
  35.9 5.5 %collective-permute-start.14 = (bf16[2,256,128]{2,1,0:T(8,128)(2,1)S(1)}, bf16[2,256,128]{2,1,0:T(8,128)(2,1)S(1)}, u32[]{:S(2)}, u32[]{:S(2)}) collective-permute-start(bf16[2,256,128]{2,1,0:T(8,128)(2,1)S(1)} %get-tuple-element.77), channel_id=1, source_target_pairs={{0,1},{1,0},{2,3},{3,2},{4,5},{5,4},{6,7},{7,6},{8,9},{9,8},{10,11... | collective-permute-start | bytes 393224 | tf_op jit(solution)/shard_map/ppermute | solution.py:453
  36.9 4.5 %collective-permute-start.15 = (bf16[2,256,128]{2,1,0:T(8,128)(2,1)S(1)}, bf16[2,256,128]{2,1,0:T(8,128)(2,1)S(1)}, u32[]{:S(2)}, u32[]{:S(2)}) collective-permute-start(bf16[2,256,128]{2,1,0:T(8,128)(2,1)S(1)} %get-tuple-element.78), channel_id=1, source_target_pairs={{1,2},{3,4},{5,6},{2,1},{4,3},{6,5},{9,10},{11,12},{13,14},{10,9},... | collective-permute-start | bytes 393224 | tf_op jit(solution)/shard_map/ppermute | solution.py:457
  46.2 10.3 %collective-permute-start.16 = (bf16[256,512]{1,0:T(8,128)(2,1)S(1)}, bf16[256,512]{1,0:T(8,128)(2,1)S(1)}, u32[]{:S(2)}, u32[]{:S(2)}) collective-permute-start(bf16[256,512]{1,0:T(8,128)(2,1)S(1)} %get-tuple-element.82), channel_id=1, source_target_pairs={{0,8},{16,24},{32,40},{48,56},{64,72},{80,88},{96,104},{112,120},{... | collective-permute-start | bytes 786440 | tf_op jit(solution)/shard_map/ppermute | solution.py:457
  46.3 10.3 %collective-permute-start.17 = (bf16[256,512]{1,0:T(8,128)(2,1)S(1)}, bf16[256,512]{1,0:T(8,128)(2,1)S(1)}, u32[]{:S(2)}, u32[]{:S(2)}) collective-permute-start(bf16[256,512]{1,0:T(8,128)(2,1)S(1)} %get-tuple-element.83), channel_id=1, source_target_pairs={{8,16},{24,32},{40,48},{56,64},{72,80},{88,96},{104,112},{16,8},{3... | collective-permute-start | bytes 786440 | tf_op jit(solution)/shard_map/ppermute | solution.py:457
  49.9 6.5 %collective-permute-start.18 = (bf16[2,256,128]{2,1,0:T(8,128)(2,1)S(1)}, bf16[2,256,128]{2,1,0:T(8,128)(2,1)S(1)}, u32[]{:S(2)}, u32[]{:S(2)}) collective-permute-start(bf16[2,256,128]{2,1,0:T(8,128)(2,1)S(1)} %get-tuple-element.84), channel_id=1, source_target_pairs={{0,1},{1,0},{2,3},{3,2},{4,5},{5,4},{6,7},{7,6},{8,9},{9,8},{10,11... | collective-permute-start | bytes 393224 | tf_op jit(solution)/shard_map/ppermute | solution.py:453
  51.8 4.6 %collective-permute-start.19 = (bf16[2,256,128]{2,1,0:T(8,128)(2,1)S(1)}, bf16[2,256,128]{2,1,0:T(8,128)(2,1)S(1)}, u32[]{:S(2)}, u32[]{:S(2)}) collective-permute-start(bf16[2,256,128]{2,1,0:T(8,128)(2,1)S(1)} %get-tuple-element.85), channel_id=1, source_target_pairs={{1,2},{3,4},{5,6},{2,1},{4,3},{6,5},{9,10},{11,12},{13,14},{10,9},... | collective-permute-start | bytes 393224 | tf_op jit(solution)/shard_map/ppermute | solution.py:457
  58.1 10.8 %collective-permute-start.20 = (bf16[2,2,64,512]{3,2,1,0:T(8,128)(2,1)S(1)}, bf16[2,2,64,512]{3,2,1,0:T(8,128)(2,1)S(1)}, u32[]{:S(2)}, u32[]{:S(2)}) collective-permute-start(bf16[2,2,64,512]{3,2,1,0:T(8,128)(2,1)S(1)} %get-tuple-element.88), channel_id=1, source_target_pairs={{0,4},{1,5},{2,6},{3,7},{4,0},{5,1},{6,2},{7,3},{8,12},{9,13},{10,... | collective-permute-start | bytes 786440 | tf_op jit(solution)/shard_map/ppermute | solution.py:453
  60.9 12.6 %collective-permute-start.21 = (bf16[2,2,64,512]{3,2,1,0:T(8,128)(2,1)S(1)}, bf16[2,2,64,512]{3,2,1,0:T(8,128)(2,1)S(1)}, u32[]{:S(2)}, u32[]{:S(2)}) collective-permute-start(bf16[2,2,64,512]{3,2,1,0:T(8,128)(2,1)S(1)} %get-tuple-element.89), channel_id=1, source_target_pairs={{0,6},{1,7},{2,4},{3,5},{4,2},{5,3},{6,0},{7,1},{8,14},{9,15},{10,... | collective-permute-start | bytes 786440 | tf_op jit(solution)/shard_map/ppermute | solution.py:453
  68.8 6.7 %collective-permute-start.23 = (bf16[2,2,64,512]{3,2,1,0:T(8,128)(2,1)S(1)}, bf16[2,2,64,512]{3,2,1,0:T(8,128)(2,1)S(1)}, u32[]{:S(2)}, u32[]{:S(2)}) collective-permute-start(bf16[2,2,64,512]{3,2,1,0:T(8,128)(2,1)S(1)} %get-tuple-element.94), channel_id=1, source_target_pairs={{0,2},{1,3},{2,0},{3,1},{4,6},{5,7},{6,4},{7,5},{8,10},{9,11},{10,... | collective-permute-start | bytes 786440 | tf_op jit(solution)/shard_map/ppermute | solution.py:453
  73.5 5.2 %collective-permute-start.25 = (bf16[2,2,64,512]{3,2,1,0:T(8,128)(2,1)S(1)}, bf16[2,2,64,512]{3,2,1,0:T(8,128)(2,1)S(1)}, u32[]{:S(2)}, u32[]{:S(2)}) collective-permute-start(bf16[2,2,64,512]{3,2,1,0:T(8,128)(2,1)S(1)} %collective-permute-done.20.refs_4_), channel_id=1, source_target_pairs={{0,1},{1,0},{2,3},{3,2},{4,5},{5,4},{6,7},{7,6},{8,9},{9,8},{10,11... | collective-permute-start | bytes 786440 | tf_op jit(solution)/shard_map/ppermute | solution.py:453
  74.0 4.7 %collective-permute-start.26 = (bf16[2,2,64,512]{3,2,1,0:T(8,128)(2,1)S(1)}, bf16[2,2,64,512]{3,2,1,0:T(8,128)(2,1)S(1)}, u32[]{:S(2)}, u32[]{:S(2)}) collective-permute-start(bf16[2,2,64,512]{3,2,1,0:T(8,128)(2,1)S(1)} %collective-permute-done.21.refs_6_), channel_id=1, source_target_pairs={{0,1},{1,0},{2,3},{3,2},{4,5},{5,4},{6,7},{7,6},{8,9},{9,8},{10,11... | collective-permute-start | bytes 786440 | tf_op jit(solution)/shard_map/ppermute | solution.py:453
  74.0 3.7 %collective-permute-start.22 = (bf16[1,2,64,512]{3,2,1,0:T(8,128)(2,1)S(1)}, bf16[1,2,64,512]{3,2,1,0:T(8,128)(2,1)S(1)}, u32[]{:S(2)}, u32[]{:S(2)}) collective-permute-start(bf16[1,2,64,512]{3,2,1,0:T(8,128)(2,1)S(1)} %get-tuple-element.93), channel_id=1, source_target_pairs={{0,1},{1,0},{2,3},{3,2},{4,5},{5,4},{6,7},{7,6},{8,9},{9,8},{10,11... | collective-permute-start | bytes 393224 | tf_op jit(solution)/shard_map/ppermute | solution.py:453
  75.5 3.2 %collective-permute-start.24 = (bf16[1,2,64,512]{3,2,1,0:T(8,128)(2,1)S(1)}, bf16[1,2,64,512]{3,2,1,0:T(8,128)(2,1)S(1)}, u32[]{:S(2)}, u32[]{:S(2)}) collective-permute-start(bf16[1,2,64,512]{3,2,1,0:T(8,128)(2,1)S(1)} %slice.20), channel_id=1, source_target_pairs={{0,1},{1,0},{2,3},{3,2},{4,5},{5,4},{6,7},{7,6},{8,9},{9,8},{10,11... | collective-permute-start | bytes 393224 | tf_op jit(solution)/shard_map/ppermute | solution.py:453

commit v2 on v1

--- a/solution.py
+++ b/solution.py
@@ -210,20 +210,25 @@
     )(info, *pieces)
 
 
-def put_edges(info_ref, a, b, ev_ref, od_ref, peer_ref, chip_ref, rows):
-    me = info_ref[0]
-    first = (me >> 2) == 0
-    core = me & 1
-    even = (info_ref[1] & 1) == 0
-    lo = jnp.where(first, a[0].astype(F32), b[0].astype(F32))
-    hi = jnp.where(first, b[1].astype(F32), a[1].astype(F32))
-    ev_ref[rows, :] = jnp.where(even, hi, lo).astype(BF16)
-    od_ref[rows, :] = jnp.where(even, lo, hi).astype(BF16)
+def by_place(info_ref, body):
+    for even in (True, False):
+        for first in (True, False):
+            here = ((info_ref[1] & 1) == (0 if even else 1)) & ((info_ref[0] >> 2) == (0 if first else 1))
+
+            @pl.when(here)
+            def _(even=even, first=first):
+                body(even, first)
+
+
+def put_edges(info_ref, place, a, b, ev_ref, od_ref, peer_ref, chip_ref, rows):
+    even, first = place
+    core = info_ref[0] & 1
+    one, two = (a, b) if first else (b, a)
+    ev, od = (two[1], one[0]) if even else (one[0], two[1])
+    ev_ref[rows, :] = ev.astype(BF16)
+    od_ref[rows, :] = od.astype(BF16)
     for q in range(2):
-        sides = []
-        for cut in (slice(0, 128), slice(LN - 128, LN)):
-            va, vb = a[q][:, cut].astype(F32), b[q][:, cut].astype(F32)
-            sides.append((jnp.where(first, va, vb), jnp.where(first, vb, va)))
+        sides = [(one[q][:, cut].astype(F32), two[q][:, cut].astype(F32)) for cut in (slice(0, 128), slice(LN - 128, LN))]
         low = lax.broadcasted_iota(jnp.int32, sides[0][0].shape, 1) < GY
         left = jnp.where(low, sides[0][0], pltpu.roll(sides[0][1], GY, 1))
         right = jnp.where(low, pltpu.roll(sides[1][0], GY, 1), sides[1][1])
@@ -243,12 +248,16 @@
     pieces, out_ref, edges = refs[:4], refs[4], refs[5:]
     gather_planes(at, info_ref, *pieces, out_ref)
 
-    def block(s, _):
-        rows = pl.ds(pl.multiple_of(s * SB, SB), SB)
-        put_edges(info_ref, [a_ref[0, rows, :], a_ref[1, rows, :]], [out_ref[0, rows, :], out_ref[1, rows, :]], *edges, rows)
-        return 0
-
-    lax.fori_loop(0, S // SB, block, 0)
+    def body(*place):
+        def block(s, _):
+            rows = pl.ds(pl.multiple_of(s * SB, SB), SB)
+            a, b = [[ref[0, rows, :], ref[1, rows, :]] for ref in (a_ref, out_ref)]
+            put_edges(info_ref, place, a, b, *edges, rows)
+            return 0
+
+        lax.fori_loop(0, S // SB, block, 0, unroll=2)
+
+    by_place(info_ref, body)
 
 
 def gather_far_call(info, a, pieces, at):
@@ -308,19 +317,18 @@
     )(conc, cells, order, stoich, load, lr)
 
 
-def diffuse(info_ref, which, a, b, ev, od, from_peer, from_chip, change, coef):
+def diffuse(info_ref, place, which, a, b, ev, od, from_peer, from_chip, change, coef):
     me = info_ref[0]
     ring = info_ref[1]
-    x_hi = (me >> 2) ^ which
-    first = x_hi == 0
+    even, first = place[0], place[1] == (which == 0)
     own, other = (a, b) if which == 0 else (b, a)
     own, other = [v.astype(F32) for v in own], [v.astype(F32) for v in other]
-    even = (ring & 1) == 0
-    ev, od = ev.astype(F32), od.astype(F32)
-    lo = jnp.where(ring == 0, own[0], jnp.where(even, od, ev))
-    hi = jnp.where(ring == 15, own[1], jnp.where(even, ev, od))
-    below = [jnp.where(first, lo, other[1]), own[0]]
-    above = [own[1], jnp.where(first, other[0], hi)]
+    if first:
+        lo = jnp.where(ring == 0, own[0], (od if even else ev).astype(F32))
+        below, above = [lo, own[0]], [own[1], other[0]]
+    else:
+        hi = jnp.where(ring == 15, own[1], (ev if even else od).astype(F32))
+        below, above = [other[1], own[0]], [own[1], hi]
     rows = own[0].shape[0]
     lane = lax.broadcasted_iota(jnp.int32, (rows, 128), 1)
     low = lane < GY
@@ -331,10 +339,13 @@
         c = own[p]
         peer, chip = from_peer[p].astype(F32), from_chip[p].astype(F32)
         left, right = jnp.where(core == 0, chip, peer), jnp.where(core == 0, peer, chip)
-        left = jnp.where(first, left, pltpu.roll(left, GY, 1))
-        right = jnp.where(first, pltpu.roll(right, GY, 1), right)
+        if first:
+            right = pltpu.roll(right, GY, 1)
+        else:
+            left = pltpu.roll(left, GY, 1)
         vs = [c[:, 128 * j:128 * j + 128] for j in range(LN // 128)]
-        sw = [pltpu.roll(v, GY, 1) for v in vs]
+        vb = [v.astype(BF16) for v in vs]
+        sw = [pltpu.roll(v, GY, 1).astype(F32) for v in vb]
         left = jnp.where(me == 0, vs[0], left)
         right = jnp.where(me == N - 1, vs[-1], right)
         lat = []
@@ -343,8 +354,8 @@
             nxt = right if j == len(vs) - 1 else sw[j + 1]
             x_dn = jnp.where(low, prev, sw[j])
             x_up = jnp.where(low, sw[j], nxt)
-            y_up = jnp.where(column == GY - 1, v, pltpu.roll(v, 127, 1))
-            y_dn = jnp.where(column == 0, v, pltpu.roll(v, 1, 1))
+            y_up = jnp.where(column == GY - 1, v, pltpu.roll(vb[j], 127, 1).astype(F32))
+            y_dn = jnp.where(column == 0, v, pltpu.roll(vb[j], 1, 1).astype(F32))
             lat.append(x_up + x_dn + y_up + y_dn)
         lap = above[p] + below[p] + jnp.concatenate(lat, axis=1) - 6.0 * c
         co = jnp.concatenate([coef] * (LN // 128), axis=1)
@@ -367,17 +378,21 @@
 
 
 def advance(info_ref, a_ref, b_ref, da_ref, db_ref, ev_ref, od_ref, peer_ref, chip_ref, coef_ref, na_ref, nb_ref, *edges):
-    def block(s, _):
-        rows = pl.ds(pl.multiple_of(s * ROWS, ROWS), ROWS)
-        args = near_rows(rows, a_ref, b_ref, ev_ref, od_ref, peer_ref, chip_ref)
-        new = []
-        for which, d_ref, out_ref in ((0, da_ref, na_ref), (1, db_ref, nb_ref)):
-            new.append(diffuse(info_ref, which, *args, [d_ref[0, rows, :], d_ref[1, rows, :]], coef_ref[rows, :]))
-            out_ref[0, rows, :], out_ref[1, rows, :] = new[-1]
-        put_edges(info_ref, *new, *edges, rows)
-        return 0
-
-    lax.fori_loop(0, S // ROWS, block, 0, unroll=4)
+    def body(*place):
+        def block(s, _):
+            rows = pl.ds(pl.multiple_of(s * ROWS, ROWS), ROWS)
+            args = near_rows(rows, a_ref, b_ref, ev_ref, od_ref, peer_ref, chip_ref)
+            new = []
+            for which, d_ref, out_ref in ((0, da_ref, na_ref), (1, db_ref, nb_ref)):
+                change = [d_ref[0, rows, :], d_ref[1, rows, :]]
+                new.append(diffuse(info_ref, place, which, *args, change, coef_ref[rows, :]))
+                out_ref[0, rows, :], out_ref[1, rows, :] = new[-1]
+            put_edges(info_ref, place, *new, *edges, rows)
+            return 0
+
+        lax.fori_loop(0, S // ROWS, block, 0, unroll=4)
+
+    by_place(info_ref, body)
 
 
 def advance_call(info, a, b, da, db, halos, coef):
@@ -396,17 +411,17 @@
 def finish(which, info_ref, a_ref, b_ref, d_ref, ev_ref, od_ref, peer_ref, chip_ref, coef_ref, *outs):
     me = info_ref[0]
     places = [(ref, i) for ref in outs for i in range(ref.shape[0])]
-    for j, (out, at) in enumerate(places):
-        def block(s, _, j=j, out=out, at=at):
-            rows = pl.ds(pl.multiple_of(((me & 3) ^ j) * SB + s * ROWS, ROWS), ROWS)
-            to = pl.ds(pl.multiple_of(s * ROWS, ROWS), ROWS)
-            args = near_rows(rows, a_ref, b_ref, ev_ref, od_ref, peer_ref, chip_ref)
-            new = diffuse(info_ref, which, *args, [d_ref[0, rows, :], d_ref[1, rows, :]], coef_ref[rows, :])
-            for p in range(2):
-                out[at, p, to, :] = new[p].astype(BF16)
-            return 0
-
-        lax.fori_loop(0, SB // ROWS, block, 0, unroll=True)
+
+    def body(*place):
+        for j, (out, at) in enumerate(places):
+            for s in range(SB // ROWS):
+                rows = pl.ds(pl.multiple_of(((me & 3) ^ j) * SB + s * ROWS, ROWS), ROWS)
+                args = near_rows(rows, a_ref, b_ref, ev_ref, od_ref, peer_ref, chip_ref)
+                new = diffuse(info_ref, place, which, *args, [d_ref[0, rows, :], d_ref[1, rows, :]], coef_ref[rows, :])
+                for p in range(2):
+                    out[at, p, s * ROWS:(s + 1) * ROWS, :] = new[p].astype(BF16)
+
+    by_place(info_ref, body)
 
 
 def finish_call(which, info, a, b, d, halos, coef, counts):

time: 81.1 us -> 80.7 us (level)
  no operation moved by 1% of the time
where the time goes in v2:
time: 80.7 us; the launch traced here: 80.4 us
  Pallas kernels  32.6 us (40%)
  starting transfers between devices  30.8 us (38%)
  waiting for transfers between devices  15.8 us (20%)
    ppermute x20, starting transfers between devices, send(): return lax.ppermute(v, RING, [(i, i ^ k) for i in range(N)])  20.6 us
    pallas_call x4, Pallas kernels, react_call(): pl.pallas_call(functools.partial(react, far), grid=(2,), out_shape=jax.Sh...  15 us
    ppermute x20, waiting for transfers between devices, send(): return lax.ppermute(v, RING, [(i, i ^ k) for i in range(N)])  10.2 us
    ppermute x6, starting transfers between devices, swap(): lax.ppermute(v, axis, [(i, i + 1) for i in firsts] + [(i + 1, i) for i in...  10.1 us
    pallas_call x1, Pallas kernels, state_call(): pl.pallas_call(pack_state, out_shape=(m(128), m(128), m(256), m(256), m(F...  4.18 us
    ppermute x1, waiting for transfers between devices, on_device(): lax.ppermute(w, RING, [(i, i ^ (6 if i % 2 else 2)) for i in range(N)])  3.32 us
    pallas_call x2, Pallas kernels, finish_call(): pl.pallas_call(functools.partial(finish, which), in_specs=[SMEM] + [VMEM]...  2.96 us
    pallas_call x1, Pallas kernels, advance_call(): pl.pallas_call(advance, in_specs=[SMEM] + [VMEM] * 9, out_specs=(VMEM,) *...  2.63 us
  transfers between devices with their start and end apart: 27, of which 10 were waited for; matrix products, arithmetic and copies ran while one was open for 1% of the time, Pallas kernels for 29%

profile of v2, /device:TPU:103, one launch (start us, length us, event | category | flops | bytes accessed | tf_op | source)
XLA Modules:
  0.0 80.4 jit_solution(4061712900763021880)
XLA Ops:
  0.0 2.2 %pack_weights.1.refs_0_ = bf16[2,656,256]{2,1,0:T(8,128)(2,1)} custom-call(s32[512,256]{1,0:T(8,128)} %order_ref.1, s32[256,512]{1,0:T(8,128)} %stoich_ref.1, f32[2,32,512]{2,1,0:T(8,128)} %bitcast.5, f32[1,512]{1,0:T(1,128)} %bitcast.6, s32[1,64]{1,0:T(1,128)} %bitcast.7, f32[4]{0:T(128)} %coef_ref.1), custom_call_target="tpu_custom_call" | custom-call | flops 1 | bytes 1 | tf_op jit(solution)/shard_map/pack_weights/pallas_call | solution.py:70
  2.4 1.3 %collective-permute-start.3 = (bf16[2,656,256]{2,1,0:T(8,128)(2,1)}, bf16[2,656,256]{2,1,0:T(8,128)(2,1)S(1)}, u32[]{:S(2)}, u32[]{:S(2)}) collective-permute-start(bf16[2,656,256]{2,1,0:T(8,128)(2,1)} %pack_weights.1.refs_0_), channel_id=1, source_target_pairs={{0,1},{1,0},{2,3},{3,2},{4,5},{5,4},{6,7},{7,6},{8,9},{9,8},{10,11... | collective-permute-start | bytes 2015240 | tf_op jit(solution)/shard_map/ppermute | solution.py:468
  4.4 4.2 %pack_state.1 = (bf16[128,512]{1,0:T(8,128)(2,1)}, bf16[128,512]{1,0:T(8,128)(2,1)}, bf16[256,512]{1,0:T(8,128)(2,1)}, bf16[256,512]{1,0:T(8,128)(2,1)}, bf16[38...) custom-call(s32[2]{0:T(128)} %pad_add_fusion.info_ref, f32[64,2,4096]{2,1,0:T(2,128)} %conc_ref.1, ...), custom_call_target="tpu_custom_call" | custom-call | flops 1 | bytes 1 | tf_op jit(solution)/shard_map/pack_state/pallas_call | solution.py:124
  8.5 1.0 %collective-permute-start.2 = (bf16[256,512]{1,0:T(8,128)(2,1)}, bf16[256,512]{1,0:T(8,128)(2,1)S(1)}, u32[]{:S(2)}, u32[]{:S(2)}) collective-permute-start(bf16[256,512]{1,0:T(8,128)(2,1)} %get-tuple-element.55), channel_id=1, source_target_pairs={{0,2},{1,3},{2,0},{3,1},{4,6},{5,7},{6,4},{7,5},{8,10},{9,11},{10,... | collective-permute-start | bytes 786440 | tf_op jit(solution)/shard_map/ppermute | solution.py:468
  9.9 3.3 %collective-permute-done.refs_2_ = bf16[2,656,256]{2,1,0:T(8,128)(2,1)S(1)} collective-permute-done((bf16[2,656,256]{2,1,0:T(8,128)(2,1)}, bf16[2,656,256]{2,1,0:T(8,128)(2,1)S(1)}, u32[]{:S(2)}, u32[]{:S(2)}) %collective-permute-start) | collective-permute-done | bytes 671776 | tf_op jit(solution)/shard_map/ppermute | solution.py:487
  13.2 2.5 %collective-permute-start.6 = (bf16[2,208,256]{2,1,0:T(8,128)(2,1)S(1)}, bf16[2,208,256]{2,1,0:T(8,128)(2,1)S(1)}, u32[]{:S(2)}, u32[]{:S(2)}) collective-permute-start(bf16[2,208,256]{2,1,0:T(8,128)(2,1)S(1)} %slice.17), channel_id=1, source_target_pairs={{0,1},{1,0},{2,3},{3,2},{4,5},{5,4},{6,7},{7,6},{8,9},{9,8},{10,11... | collective-permute-start | bytes 638984 | tf_op jit(solution)/shard_map/ppermute | solution.py:468
  16.9 1.4 %collective-permute-start.8 = (bf16[256,512]{1,0:T(8,128)(2,1)}, bf16[256,512]{1,0:T(8,128)(2,1)S(1)}, u32[]{:S(2)}, u32[]{:S(2)}) collective-permute-start(bf16[256,512]{1,0:T(8,128)(2,1)} %get-tuple-element.64), channel_id=1, source_target_pairs={{0,4},{1,5},{2,6},{3,7},{4,0},{5,1},{6,2},{7,3},{8,12},{9,13},{10,... | collective-permute-start | bytes 786440 | tf_op jit(solution)/shard_map/ppermute | solution.py:468
  18.9 2.2 %sort_weights.1 = (bf16[2048,256]{1,0:T(8,128)(2,1)S(1)}, bf16[256,2048]{1,0:T(8,128)(2,1)S(1)}, bf16[2,2048,128]{2,1,0:T(8,128)(2,1)S(1)}, f32[2048,128]{1,0:T(8,128)S(1)}, f32[256,128]{1,0:T(8,128)S(1)}) custom-call(s32[2]{0:T(128)S(1)} %copy-done.3, bf16[2,656,256]{2,1,0:T(8,128)(2,1)S(1)} %copy-done, ...), custom_call_target="tpu_custom_call" | custom-call | flops 1 | bytes 1 | tf_op jit(solution)/shard_map/sort_weights/pallas_call | solution.py:175
  21.2 1.3 %collective-permute-done.7.refs_3_ = bf16[128,512]{1,0:T(8,128)(2,1)S(1)} collective-permute-done((bf16[128,512]{1,0:T(8,128)(2,1)S(1)}, bf16[128,512]{1,0:T(8,128)(2,1)S(1)}, u32[]{:S(2)}, u32[]{:S(2)}) %collective-permute-start.7) | collective-permute-done | bytes 131104 | tf_op jit(solution)/shard_map/ppermute | solution.py:468
  23.1 3.8 %react.4.da_ref = f32[2,256,512]{2,1,0:T(8,128)S(1)} custom-call(bf16[2,256,512]{2,1,0:T(8,128)(2,1)S(1)} %gather_planes.1.conc_ref.a_ref, bf16[2,2,64,512]{3,2,1,0:T(8,128)(2,1)S(1)} %copy-done.1, bf16[2048,256]{1,0:T(8,128)(2,1)S(1)} %get-tuple-element.67.order_ref, bf16[256,2048]{1,0:T(8,128)(2,1)S(1)} %get-tuple-element.68.stoich_ref, ...), custom_call_target="tpu_custom_call" | custom-call | flops 1 | bytes 1 | tf_op jit(solution)/shard_map/react/pallas_call | solution.py:300
  27.0 1.1 %collective-permute-start.11 = (bf16[384,512]{1,0:T(8,128)(2,1)S(1)}, bf16[384,512]{1,0:T(8,128)(2,1)S(1)}, u32[]{:S(2)}, u32[]{:S(2)}) collective-permute-start(bf16[384,512]{1,0:T(8,128)(2,1)S(1)} %collective-permute-done.9.refs_2_.cell_ref), channel_id=1, source_target_pairs={{0,1},{1,0},{2,3},{3,2},{4,5},{5,4},{6,7},{7,6},{8,9},{9,8},{10,11... | collective-permute-start | bytes 1179656 | tf_op jit(solution)/shard_map/ppermute | solution.py:468
  28.1 1.7 %collective-permute-done.10.refs_1_ = bf16[256,512]{1,0:T(8,128)(2,1)S(1)} collective-permute-done((bf16[256,512]{1,0:T(8,128)(2,1)S(1)}, bf16[256,512]{1,0:T(8,128)(2,1)S(1)}, u32[]{:S(2)}, u32[]{:S(2)}) %collective-permute-start.10) | collective-permute-done | bytes 262176 | tf_op jit(solution)/shard_map/ppermute | solution.py:468
  29.8 0.8 %gather_far.1 = (bf16[2,256,512]{2,1,0:T(8,128)(2,1)S(1)}, bf16[256,512]{1,0:T(8,128)(2,1)S(1)}, bf16[256,512]{1,0:T(8,128)(2,1)S(1)}, bf16[2,256,128]{2,1,0:T(8,128)(2,1)S(1)}, bf16[2,256,128]{2,1,0:T(8,128)(2,1)S(1)}) custom-call(s32[2]{0:T(128)S(1)} %copy-done.3, bf16[2,256,512]{2,1,0:T(8,128)(2,1)S(1)} %gather_planes.1.conc_ref.a_ref, ...), custom_call_target="tpu_custom_call" | custom-call | flops 1 | bytes 1 | tf_op jit(solution)/shard_map/gather_far/pallas_call | solution.py:264
  30.7 1.4 %collective-permute-start.12 = (bf16[256,512]{1,0:T(8,128)(2,1)S(1)}, bf16[256,512]{1,0:T(8,128)(2,1)S(1)}, u32[]{:S(2)}, u32[]{:S(2)}) collective-permute-start(bf16[256,512]{1,0:T(8,128)(2,1)S(1)} %get-tuple-element.75), channel_id=1, source_target_pairs={{0,8},{16,24},{32,40},{48,56},{64,72},{80,88},{96,104},{112,120},{... | collective-permute-start | bytes 786440 | tf_op jit(solution)/shard_map/ppermute | solution.py:472
  32.1 3.6 %collective-permute-start.13 = (bf16[256,512]{1,0:T(8,128)(2,1)S(1)}, bf16[256,512]{1,0:T(8,128)(2,1)S(1)}, u32[]{:S(2)}, u32[]{:S(2)}) collective-permute-start(bf16[256,512]{1,0:T(8,128)(2,1)S(1)} %get-tuple-element.76), channel_id=1, source_target_pairs={{8,16},{24,32},{40,48},{56,64},{72,80},{88,96},{104,112},{16,8},{3... | collective-permute-start | bytes 786440 | tf_op jit(solution)/shard_map/ppermute | solution.py:472
  35.7 1.0 %collective-permute-start.14 = (bf16[2,256,128]{2,1,0:T(8,128)(2,1)S(1)}, bf16[2,256,128]{2,1,0:T(8,128)(2,1)S(1)}, u32[]{:S(2)}, u32[]{:S(2)}) collective-permute-start(bf16[2,256,128]{2,1,0:T(8,128)(2,1)S(1)} %get-tuple-element.77), channel_id=1, source_target_pairs={{0,1},{1,0},{2,3},{3,2},{4,5},{5,4},{6,7},{7,6},{8,9},{9,8},{10,11... | collective-permute-start | bytes 393224 | tf_op jit(solution)/shard_map/ppermute | solution.py:468
  37.4 3.8 %react.5.db_ref = f32[2,256,512]{2,1,0:T(8,128)S(1)} custom-call(bf16[2,256,512]{2,1,0:T(8,128)(2,1)S(1)} %get-tuple-element.73.conc_ref.b_ref, bf16[384,512]{1,0:T(8,128)(2,1)S(1)} %collective-permute-done.9.refs_2_.cell_ref, bf16[2048,256]{1,0:T(8,128)(2,1)S(1)} %get-tuple-element.67.order_ref, bf16[256,2048]{1,0:T(8,128)(2,1)S(1)} %get-tuple-element.68.stoich_ref, ...), custom_call_target="tpu_custom_call" | custom-call | flops 1 | bytes 1 | tf_op jit(solution)/shard_map/react/pallas_call | solution.py:300
  41.2 2.1 %collective-permute-done.13.od_ref = bf16[256,512]{1,0:T(8,128)(2,1)S(1)} collective-permute-done((bf16[256,512]{1,0:T(8,128)(2,1)S(1)}, bf16[256,512]{1,0:T(8,128)(2,1)S(1)}, u32[]{:S(2)}, u32[]{:S(2)}) %collective-permute-start.13) | collective-permute-done | bytes 262176 | tf_op jit(solution)/shard_map/ppermute | solution.py:472
  43.2 2.6 %advance.1 = (f32[2,256,512]{2,1,0:T(8,128)S(1)}, f32[2,256,512]{2,1,0:T(8,128)S(1)}, bf16[256,512]{1,0:T(8,128)(2,1)S(1)}, bf16[256,512]{1,0:T(8,128)(2,1)S(1)}...) custom-call(s32[2]{0:T(128)S(1)} %copy-done.3, ...), custom_call_target="tpu_custom_call" | custom-call | flops 1 | bytes 1 | tf_op jit(solution)/shard_map/advance/pallas_call | solution.py:400
  46.0 3.6 %collective-permute-start.17 = (bf16[256,512]{1,0:T(8,128)(2,1)S(1)}, bf16[256,512]{1,0:T(8,128)(2,1)S(1)}, u32[]{:S(2)}, u32[]{:S(2)}) collective-permute-start(bf16[256,512]{1,0:T(8,128)(2,1)S(1)} %get-tuple-element.83), channel_id=1, source_target_pairs={{8,16},{24,32},{40,48},{56,64},{72,80},{88,96},{104,112},{16,8},{3... | collective-permute-start | bytes 786440 | tf_op jit(solution)/shard_map/ppermute | solution.py:472
  49.6 1.9 %collective-permute-start.18 = (bf16[2,256,128]{2,1,0:T(8,128)(2,1)S(1)}, bf16[2,256,128]{2,1,0:T(8,128)(2,1)S(1)}, u32[]{:S(2)}, u32[]{:S(2)}) collective-permute-start(bf16[2,256,128]{2,1,0:T(8,128)(2,1)S(1)} %get-tuple-element.84), channel_id=1, source_target_pairs={{0,1},{1,0},{2,3},{3,2},{4,5},{5,4},{6,7},{7,6},{8,9},{9,8},{10,11... | collective-permute-start | bytes 393224 | tf_op jit(solution)/shard_map/ppermute | solution.py:468
  52.2 3.8 %react.6.d_ref = f32[2,256,512]{2,1,0:T(8,128)S(1)} custom-call(f32[2,256,512]{2,1,0:T(8,128)S(1)} %get-tuple-element.81.conc_ref.b_ref, bf16[384,512]{1,0:T(8,128)(2,1)S(1)} %collective-permute-done.9.refs_2_.cell_ref, bf16[2048,256]{1,0:T(8,128)(2,1)S(1)} %get-tuple-element.67.order_ref, bf16[256,2048]{1,0:T(8,128)(2,1)S(1)} %get-tuple-element.68.stoich_ref, ...), custom_call_target="tpu_custom_call" | custom-call | flops 1 | bytes 1 | tf_op jit(solution)/shard_map/react/pallas_call | solution.py:300
  56.2 1.4 %finish.2 = (bf16[2,2,64,512]{3,2,1,0:T(8,128)(2,1)S(1)}, bf16[2,2,64,512]{3,2,1,0:T(8,128)(2,1)S(1)}) custom-call(s32[2]{0:T(128)S(1)} %copy-done.3, f32[2,256,512]{2,1,0:T(8,128)S(1)} %get-tuple-element.80.a_ref.conc_ref, f32[2,256,512]{2,1,0:T(8,128)S(1)} %get-tuple-element.81.conc_ref.b_ref, f32[2,256,512]{2,1,0:T(8,128)S(1)} %react.6.d_ref, ...), custom_call_target="tpu_custom_call" | custom-call | flops 1 | bytes 1 | tf_op jit(solution)/shard_map/finish/pallas_call | solution.py:428
  57.6 2.7 %collective-permute-start.20 = (bf16[2,2,64,512]{3,2,1,0:T(8,128)(2,1)S(1)}, bf16[2,2,64,512]{3,2,1,0:T(8,128)(2,1)S(1)}, u32[]{:S(2)}, u32[]{:S(2)}) collective-permute-start(bf16[2,2,64,512]{3,2,1,0:T(8,128)(2,1)S(1)} %get-tuple-element.88), channel_id=1, source_target_pairs={{0,4},{1,5},{2,6},{3,7},{4,0},{5,1},{6,2},{7,3},{8,12},{9,13},{10,... | collective-permute-start | bytes 786440 | tf_op jit(solution)/shard_map/ppermute | solution.py:468
  60.4 2.7 %collective-permute-start.21 = (bf16[2,2,64,512]{3,2,1,0:T(8,128)(2,1)S(1)}, bf16[2,2,64,512]{3,2,1,0:T(8,128)(2,1)S(1)}, u32[]{:S(2)}, u32[]{:S(2)}) collective-permute-start(bf16[2,2,64,512]{3,2,1,0:T(8,128)(2,1)S(1)} %get-tuple-element.89), channel_id=1, source_target_pairs={{0,6},{1,7},{2,4},{3,5},{4,2},{5,3},{6,0},{7,1},{8,14},{9,15},{10,... | collective-permute-start | bytes 786440 | tf_op jit(solution)/shard_map/ppermute | solution.py:468
  63.0 3.7 %react.7.d_ref = f32[2,256,512]{2,1,0:T(8,128)S(1)} custom-call(f32[2,256,512]{2,1,0:T(8,128)S(1)} %get-tuple-element.80.a_ref.conc_ref, bf16[2,2,64,512]{3,2,1,0:T(8,128)(2,1)S(1)} %copy-done.1, bf16[2048,256]{1,0:T(8,128)(2,1)S(1)} %get-tuple-element.67.order_ref, bf16[256,2048]{1,0:T(8,128)(2,1)S(1)} %get-tuple-element.68.stoich_ref, ...), custom_call_target="tpu_custom_call" | custom-call | flops 1 | bytes 1 | tf_op jit(solution)/shard_map/react/pallas_call | solution.py:300
  66.8 1.6 %finish.3 = (bf16[1,2,64,512]{3,2,1,0:T(8,128)(2,1)S(1)}, bf16[1,2,64,512]{3,2,1,0:T(8,128)(2,1)S(1)}, bf16[2,2,64,512]{3,2,1,0:T(8,128)(2,1)S(1)}) custom-call(s32[2]{0:T(128)S(1)} %copy-done.3, f32[2,256,512]{2,1,0:T(8,128)S(1)} %get-tuple-element.80.a_ref.conc_ref, f32[2,256,512]{2,1,0:T(8,128)S(1)} %get-tuple-element.81.conc_ref.b_ref, ...), custom_call_target="tpu_custom_call" | custom-call | flops 1 | bytes 1 | tf_op jit(solution)/shard_map/finish/pallas_call | solution.py:428
  68.5 4.5 %collective-permute-done.21.refs_6_ = bf16[2,2,64,512]{3,2,1,0:T(8,128)(2,1)S(1)} collective-permute-done((bf16[2,2,64,512]{3,2,1,0:T(8,128)(2,1)S(1)}, bf16[2,2,64,512]{3,2,1,0:T(8,128)(2,1)S(1)}, u32[]{:S(2)}, u32[]{:S(2)}) %collective-permute-start.21) | collective-permute-done | bytes 262176 | tf_op jit(solution)/shard_map/ppermute | solution.py:468
  74.1 1.0 %collective-permute-done.23.refs_2_ = bf16[2,2,64,512]{3,2,1,0:T(8,128)(2,1)S(1)} collective-permute-done((bf16[2,2,64,512]{3,2,1,0:T(8,128)(2,1)S(1)}, bf16[2,2,64,512]{3,2,1,0:T(8,128)(2,1)S(1)}, u32[]{:S(2)}, u32[]{:S(2)}) %collective-permute-start.23) | collective-permute-done | bytes 262176 | tf_op jit(solution)/shard_map/ppermute | solution.py:468
  75.1 2.2 %collective-permute-start.24 = (bf16[1,2,64,512]{3,2,1,0:T(8,128)(2,1)S(1)}, bf16[1,2,64,512]{3,2,1,0:T(8,128)(2,1)S(1)}, u32[]{:S(2)}, u32[]{:S(2)}) collective-permute-start(bf16[1,2,64,512]{3,2,1,0:T(8,128)(2,1)S(1)} %slice.20), channel_id=1, source_target_pairs={{0,1},{1,0},{2,3},{3,2},{4,5},{5,4},{6,7},{7,6},{8,9},{9,8},{10,11... | collective-permute-start | bytes 393224 | tf_op jit(solution)/shard_map/ppermute | solution.py:468
  77.3 1.0 %collective-permute-done.24.refs_3_ = bf16[1,2,64,512]{3,2,1,0:T(8,128)(2,1)S(1)} collective-permute-done((bf16[1,2,64,512]{3,2,1,0:T(8,128)(2,1)S(1)}, bf16[1,2,64,512]{3,2,1,0:T(8,128)(2,1)S(1)}, u32[]{:S(2)}, u32[]{:S(2)}) %collective-permute-start.24) | collective-permute-done | bytes 131104 | tf_op jit(solution)/shard_map/ppermute | solution.py:468
  78.3 2.0 %join_out.1 = f32[64,2,4096]{2,1,0:T(2,128)} custom-call(s32[2]{0:T(128)S(1)} %copy-done.3, bf16[1,2,64,512]{3,2,1,0:T(8,128)(2,1)S(1)} %get-tuple-element.92.refs_0_, bf16[1,2,64,512]{3,2,1,0:T(8,128)(2,1)S(1)} %collective-permute-done.22.refs_1_, bf16[2,2,64,512]{3,2,1,0:T(8,128)(2,1)S(1)} %collective-permute-done.23.refs_2_, ...), custom_call_target="tpu_custom_call" | custom-call | flops 1 | bytes 1 | tf_op jit(solution)/shard_map/join_out/pallas_call | solution.py:455
  (48 shorter events, 6.6 us)
Async XLA Ops:
  2.2 11.0 %collective-permute-start = (bf16[2,656,256]{2,1,0:T(8,128)(2,1)}, bf16[2,656,256]{2,1,0:T(8,128)(2,1)S(1)}, u32[]{:S(2)}, u32[]{:S(2)}) collective-permute-start(bf16[2,656,256]{2,1,0:T(8,128)(2,1)} %pack_weights.1.refs_0_), channel_id=1, source_target_pairs={{0,2},{1,7},{2,0},{3,5},{4,6},{5,3},{6,4},{7,1},{8,10},{9,15},{10,... | collective-permute-start | bytes 2015240 | tf_op jit(solution)/shard_map/ppermute | solution.py:487
  2.4 13.5 %collective-permute-start.3 = (bf16[2,656,256]{2,1,0:T(8,128)(2,1)}, bf16[2,656,256]{2,1,0:T(8,128)(2,1)S(1)}, u32[]{:S(2)}, u32[]{:S(2)}) collective-permute-start(bf16[2,656,256]{2,1,0:T(8,128)(2,1)} %pack_weights.1.refs_0_), channel_id=1, source_target_pairs={{0,1},{1,0},{2,3},{3,2},{4,5},{5,4},{6,7},{7,6},{8,9},{9,8},{10,11... | collective-permute-start | bytes 2015240 | tf_op jit(solution)/shard_map/ppermute | solution.py:468
  4.4 14.5 %copy-start = (bf16[2,656,256]{2,1,0:T(8,128)(2,1)S(1)}, bf16[2,656,256]{2,1,0:T(8,128)(2,1)}, u32[]{:S(2)}) copy-start(bf16[2,656,256]{2,1,0:T(8,128)(2,1)} %pack_weights.1.refs_0_) | copy-start | bytes 2015236
  4.4 14.5 %copy-start.3 = (s32[2]{0:T(128)S(1)}, s32[2]{0:T(128)}, u32[]{:S(2)}) copy-start(s32[2]{0:T(128)} %pad_add_fusion.info_ref) | copy-start | bytes 28
  8.5 12.5 %collective-permute-start.2 = (bf16[256,512]{1,0:T(8,128)(2,1)}, bf16[256,512]{1,0:T(8,128)(2,1)S(1)}, u32[]{:S(2)}, u32[]{:S(2)}) collective-permute-start(bf16[256,512]{1,0:T(8,128)(2,1)} %get-tuple-element.55), channel_id=1, source_target_pairs={{0,2},{1,3},{2,0},{3,1},{4,6},{5,7},{6,4},{7,5},{8,10},{9,11},{10,... | collective-permute-start | bytes 786440 | tf_op jit(solution)/shard_map/ppermute | solution.py:468
  9.5 17.5 %collective-permute-start.9 = (bf16[384,512]{1,0:T(8,128)(2,1)}, bf16[384,512]{1,0:T(8,128)(2,1)S(1)}, u32[]{:S(2)}, u32[]{:S(2)}) collective-permute-start(bf16[384,512]{1,0:T(8,128)(2,1)} %get-tuple-element.65), channel_id=1, source_target_pairs={{0,6},{1,7},{2,4},{3,5},{4,2},{5,3},{6,0},{7,1},{8,14},{9,15},{10,... | collective-permute-start | bytes 1179656 | tf_op jit(solution)/shard_map/ppermute | solution.py:468
  13.2 9.3 %copy-start.2 = (bf16[128,512]{1,0:T(8,128)(2,1)S(1)}, bf16[128,512]{1,0:T(8,128)(2,1)}, u32[]{:S(2)}) copy-start(bf16[128,512]{1,0:T(8,128)(2,1)} %get-tuple-element.53.refs_0_) | copy-start | bytes 393220
  13.2 3.6 %collective-permute-start.6 = (bf16[2,208,256]{2,1,0:T(8,128)(2,1)S(1)}, bf16[2,208,256]{2,1,0:T(8,128)(2,1)S(1)}, u32[]{:S(2)}, u32[]{:S(2)}) collective-permute-start(bf16[2,208,256]{2,1,0:T(8,128)(2,1)S(1)} %slice.17), channel_id=1, source_target_pairs={{0,1},{1,0},{2,3},{3,2},{4,5},{5,4},{6,7},{7,6},{8,9},{9,8},{10,11... | collective-permute-start | bytes 638984 | tf_op jit(solution)/shard_map/ppermute | solution.py:468
  15.8 7.3 %copy-start.1 = (bf16[2,2,64,512]{3,2,1,0:T(8,128)(2,1)S(1)}, bf16[2,2,64,512]{3,2,1,0:T(8,128)(2,1)}, u32[]{:S(2)}) copy-start(bf16[2,2,64,512]{3,2,1,0:T(8,128)(2,1)} %get-tuple-element.90.cell_ref) | copy-start | bytes 786436
  15.8 2.4 %collective-permute-start.5 = (bf16[2,224,256]{2,1,0:T(8,128)(2,1)S(1)}, bf16[2,224,256]{2,1,0:T(8,128)(2,1)S(1)}, u32[]{:S(2)}, u32[]{:S(2)}) collective-permute-start(bf16[2,224,256]{2,1,0:T(8,128)(2,1)S(1)} %get-tuple-element.97), channel_id=1, source_target_pairs={{0,1},{1,0},{2,3},{3,2},{4,5},{5,4},{6,7},{7,6},{8,9},{9,8},{10,11... | collective-permute-start | bytes 688136 | tf_op jit(solution)/shard_map/ppermute | solution.py:468
  15.9 3.0 %collective-permute-start.4 = (bf16[2,224,256]{2,1,0:T(8,128)(2,1)S(1)}, bf16[2,224,256]{2,1,0:T(8,128)(2,1)S(1)}, u32[]{:S(2)}, u32[]{:S(2)}) collective-permute-start(bf16[2,224,256]{2,1,0:T(8,128)(2,1)S(1)} %get-tuple-element.98), channel_id=1, source_target_pairs={{0,1},{1,0},{2,3},{3,2},{4,5},{5,4},{6,7},{7,6},{8,9},{9,8},{10,11... | collective-permute-start | bytes 688136 | tf_op jit(solution)/shard_map/ppermute | solution.py:468
  16.9 10.0 %collective-permute-start.8 = (bf16[256,512]{1,0:T(8,128)(2,1)}, bf16[256,512]{1,0:T(8,128)(2,1)S(1)}, u32[]{:S(2)}, u32[]{:S(2)}) collective-permute-start(bf16[256,512]{1,0:T(8,128)(2,1)} %get-tuple-element.64), channel_id=1, source_target_pairs={{0,4},{1,5},{2,6},{3,7},{4,0},{5,1},{6,2},{7,3},{8,12},{9,13},{10,... | collective-permute-start | bytes 786440 | tf_op jit(solution)/shard_map/ppermute | solution.py:468
  18.2 3.0 %collective-permute-start.1 = (bf16[128,512]{1,0:T(8,128)(2,1)}, bf16[128,512]{1,0:T(8,128)(2,1)S(1)}, u32[]{:S(2)}, u32[]{:S(2)}) collective-permute-start(bf16[128,512]{1,0:T(8,128)(2,1)} %get-tuple-element.54), channel_id=1, source_target_pairs={{0,1},{1,0},{2,3},{3,2},{4,5},{5,4},{6,7},{7,6},{8,9},{9,8},{10,11... | collective-permute-start | bytes 393224 | tf_op jit(solution)/shard_map/ppermute | solution.py:468
  21.1 1.4 %collective-permute-start.7 = (bf16[128,512]{1,0:T(8,128)(2,1)S(1)}, bf16[128,512]{1,0:T(8,128)(2,1)S(1)}, u32[]{:S(2)}, u32[]{:S(2)}) collective-permute-start(bf16[128,512]{1,0:T(8,128)(2,1)S(1)} %slice.18), channel_id=1, source_target_pairs={{0,1},{1,0},{2,3},{3,2},{4,5},{5,4},{6,7},{7,6},{8,9},{9,8},{10,11... | collective-permute-start | bytes 393224 | tf_op jit(solution)/shard_map/ppermute | solution.py:468
  27.0 2.8 %collective-permute-start.11 = (bf16[384,512]{1,0:T(8,128)(2,1)S(1)}, bf16[384,512]{1,0:T(8,128)(2,1)S(1)}, u32[]{:S(2)}, u32[]{:S(2)}) collective-permute-start(bf16[384,512]{1,0:T(8,128)(2,1)S(1)} %collective-permute-done.9.refs_2_.cell_ref), channel_id=1, source_target_pairs={{0,1},{1,0},{2,3},{3,2},{4,5},{5,4},{6,7},{7,6},{8,9},{9,8},{10,11... | collective-permute-start | bytes 1179656 | tf_op jit(solution)/shard_map/ppermute | solution.py:468
  28.1 1.7 %collective-permute-start.10 = (bf16[256,512]{1,0:T(8,128)(2,1)S(1)}, bf16[256,512]{1,0:T(8,128)(2,1)S(1)}, u32[]{:S(2)}, u32[]{:S(2)}) collective-permute-start(bf16[256,512]{1,0:T(8,128)(2,1)S(1)} %collective-permute-done.8.refs_0_), channel_id=1, source_target_pairs={{0,1},{1,0},{2,3},{3,2},{4,5},{5,4},{6,7},{7,6},{8,9},{9,8},{10,11... | collective-permute-start | bytes 786440 | tf_op jit(solution)/shard_map/ppermute | solution.py:468
  30.7 10.5 %collective-permute-start.12 = (bf16[256,512]{1,0:T(8,128)(2,1)S(1)}, bf16[256,512]{1,0:T(8,128)(2,1)S(1)}, u32[]{:S(2)}, u32[]{:S(2)}) collective-permute-start(bf16[256,512]{1,0:T(8,128)(2,1)S(1)} %get-tuple-element.75), channel_id=1, source_target_pairs={{0,8},{16,24},{32,40},{48,56},{64,72},{80,88},{96,104},{112,120},{... | collective-permute-start | bytes 786440 | tf_op jit(solution)/shard_map/ppermute | solution.py:472
  32.1 11.2 %collective-permute-start.13 = (bf16[256,512]{1,0:T(8,128)(2,1)S(1)}, bf16[256,512]{1,0:T(8,128)(2,1)S(1)}, u32[]{:S(2)}, u32[]{:S(2)}) collective-permute-start(bf16[256,512]{1,0:T(8,128)(2,1)S(1)} %get-tuple-element.76), channel_id=1, source_target_pairs={{8,16},{24,32},{40,48},{56,64},{72,80},{88,96},{104,112},{16,8},{3... | collective-permute-start | bytes 786440 | tf_op jit(solution)/shard_map/ppermute | solution.py:472
  35.7 5.5 %collective-permute-start.14 = (bf16[2,256,128]{2,1,0:T(8,128)(2,1)S(1)}, bf16[2,256,128]{2,1,0:T(8,128)(2,1)S(1)}, u32[]{:S(2)}, u32[]{:S(2)}) collective-permute-start(bf16[2,256,128]{2,1,0:T(8,128)(2,1)S(1)} %get-tuple-element.77), channel_id=1, source_target_pairs={{0,1},{1,0},{2,3},{3,2},{4,5},{5,4},{6,7},{7,6},{8,9},{9,8},{10,11... | collective-permute-start | bytes 393224 | tf_op jit(solution)/shard_map/ppermute | solution.py:468
  36.7 4.5 %collective-permute-start.15 = (bf16[2,256,128]{2,1,0:T(8,128)(2,1)S(1)}, bf16[2,256,128]{2,1,0:T(8,128)(2,1)S(1)}, u32[]{:S(2)}, u32[]{:S(2)}) collective-permute-start(bf16[2,256,128]{2,1,0:T(8,128)(2,1)S(1)} %get-tuple-element.78), channel_id=1, source_target_pairs={{1,2},{3,4},{5,6},{2,1},{4,3},{6,5},{9,10},{11,12},{13,14},{10,9},... | collective-permute-start | bytes 393224 | tf_op jit(solution)/shard_map/ppermute | solution.py:472
  45.9 10.1 %collective-permute-start.16 = (bf16[256,512]{1,0:T(8,128)(2,1)S(1)}, bf16[256,512]{1,0:T(8,128)(2,1)S(1)}, u32[]{:S(2)}, u32[]{:S(2)}) collective-permute-start(bf16[256,512]{1,0:T(8,128)(2,1)S(1)} %get-tuple-element.82), channel_id=1, source_target_pairs={{0,8},{16,24},{32,40},{48,56},{64,72},{80,88},{96,104},{112,120},{... | collective-permute-start | bytes 786440 | tf_op jit(solution)/shard_map/ppermute | solution.py:472
  46.0 10.3 %collective-permute-start.17 = (bf16[256,512]{1,0:T(8,128)(2,1)S(1)}, bf16[256,512]{1,0:T(8,128)(2,1)S(1)}, u32[]{:S(2)}, u32[]{:S(2)}) collective-permute-start(bf16[256,512]{1,0:T(8,128)(2,1)S(1)} %get-tuple-element.83), channel_id=1, source_target_pairs={{8,16},{24,32},{40,48},{56,64},{72,80},{88,96},{104,112},{16,8},{3... | collective-permute-start | bytes 786440 | tf_op jit(solution)/shard_map/ppermute | solution.py:472
  49.6 6.3 %collective-permute-start.18 = (bf16[2,256,128]{2,1,0:T(8,128)(2,1)S(1)}, bf16[2,256,128]{2,1,0:T(8,128)(2,1)S(1)}, u32[]{:S(2)}, u32[]{:S(2)}) collective-permute-start(bf16[2,256,128]{2,1,0:T(8,128)(2,1)S(1)} %get-tuple-element.84), channel_id=1, source_target_pairs={{0,1},{1,0},{2,3},{3,2},{4,5},{5,4},{6,7},{7,6},{8,9},{9,8},{10,11... | collective-permute-start | bytes 393224 | tf_op jit(solution)/shard_map/ppermute | solution.py:468
  51.5 4.5 %collective-permute-start.19 = (bf16[2,256,128]{2,1,0:T(8,128)(2,1)S(1)}, bf16[2,256,128]{2,1,0:T(8,128)(2,1)S(1)}, u32[]{:S(2)}, u32[]{:S(2)}) collective-permute-start(bf16[2,256,128]{2,1,0:T(8,128)(2,1)S(1)} %get-tuple-element.85), channel_id=1, source_target_pairs={{1,2},{3,4},{5,6},{2,1},{4,3},{6,5},{9,10},{11,12},{13,14},{10,9},... | collective-permute-start | bytes 393224 | tf_op jit(solution)/shard_map/ppermute | solution.py:472
  57.6 10.9 %collective-permute-start.20 = (bf16[2,2,64,512]{3,2,1,0:T(8,128)(2,1)S(1)}, bf16[2,2,64,512]{3,2,1,0:T(8,128)(2,1)S(1)}, u32[]{:S(2)}, u32[]{:S(2)}) collective-permute-start(bf16[2,2,64,512]{3,2,1,0:T(8,128)(2,1)S(1)} %get-tuple-element.88), channel_id=1, source_target_pairs={{0,4},{1,5},{2,6},{3,7},{4,0},{5,1},{6,2},{7,3},{8,12},{9,13},{10,... | collective-permute-start | bytes 786440 | tf_op jit(solution)/shard_map/ppermute | solution.py:468
  60.4 12.6 %collective-permute-start.21 = (bf16[2,2,64,512]{3,2,1,0:T(8,128)(2,1)S(1)}, bf16[2,2,64,512]{3,2,1,0:T(8,128)(2,1)S(1)}, u32[]{:S(2)}, u32[]{:S(2)}) collective-permute-start(bf16[2,2,64,512]{3,2,1,0:T(8,128)(2,1)S(1)} %get-tuple-element.89), channel_id=1, source_target_pairs={{0,6},{1,7},{2,4},{3,5},{4,2},{5,3},{6,0},{7,1},{8,14},{9,15},{10,... | collective-permute-start | bytes 786440 | tf_op jit(solution)/shard_map/ppermute | solution.py:468
  68.4 6.7 %collective-permute-start.23 = (bf16[2,2,64,512]{3,2,1,0:T(8,128)(2,1)S(1)}, bf16[2,2,64,512]{3,2,1,0:T(8,128)(2,1)S(1)}, u32[]{:S(2)}, u32[]{:S(2)}) collective-permute-start(bf16[2,2,64,512]{3,2,1,0:T(8,128)(2,1)S(1)} %get-tuple-element.94), channel_id=1, source_target_pairs={{0,2},{1,3},{2,0},{3,1},{4,6},{5,7},{6,4},{7,5},{8,10},{9,11},{10,... | collective-permute-start | bytes 786440 | tf_op jit(solution)/shard_map/ppermute | solution.py:468
  73.0 5.3 %collective-permute-start.25 = (bf16[2,2,64,512]{3,2,1,0:T(8,128)(2,1)S(1)}, bf16[2,2,64,512]{3,2,1,0:T(8,128)(2,1)S(1)}, u32[]{:S(2)}, u32[]{:S(2)}) collective-permute-start(bf16[2,2,64,512]{3,2,1,0:T(8,128)(2,1)S(1)} %collective-permute-done.20.refs_4_), channel_id=1, source_target_pairs={{0,1},{1,0},{2,3},{3,2},{4,5},{5,4},{6,7},{7,6},{8,9},{9,8},{10,11... | collective-permute-start | bytes 786440 | tf_op jit(solution)/shard_map/ppermute | solution.py:468
  73.5 4.7 %collective-permute-start.26 = (bf16[2,2,64,512]{3,2,1,0:T(8,128)(2,1)S(1)}, bf16[2,2,64,512]{3,2,1,0:T(8,128)(2,1)S(1)}, u32[]{:S(2)}, u32[]{:S(2)}) collective-permute-start(bf16[2,2,64,512]{3,2,1,0:T(8,128)(2,1)S(1)} %collective-permute-done.21.refs_6_), channel_id=1, source_target_pairs={{0,1},{1,0},{2,3},{3,2},{4,5},{5,4},{6,7},{7,6},{8,9},{9,8},{10,11... | collective-permute-start | bytes 786440 | tf_op jit(solution)/shard_map/ppermute | solution.py:468
  73.6 3.7 %collective-permute-start.22 = (bf16[1,2,64,512]{3,2,1,0:T(8,128)(2,1)S(1)}, bf16[1,2,64,512]{3,2,1,0:T(8,128)(2,1)S(1)}, u32[]{:S(2)}, u32[]{:S(2)}) collective-permute-start(bf16[1,2,64,512]{3,2,1,0:T(8,128)(2,1)S(1)} %get-tuple-element.93), channel_id=1, source_target_pairs={{0,1},{1,0},{2,3},{3,2},{4,5},{5,4},{6,7},{7,6},{8,9},{9,8},{10,11... | collective-permute-start | bytes 393224 | tf_op jit(solution)/shard_map/ppermute | solution.py:468
  75.1 3.2 %collective-permute-start.24 = (bf16[1,2,64,512]{3,2,1,0:T(8,128)(2,1)S(1)}, bf16[1,2,64,512]{3,2,1,0:T(8,128)(2,1)S(1)}, u32[]{:S(2)}, u32[]{:S(2)}) collective-permute-start(bf16[1,2,64,512]{3,2,1,0:T(8,128)(2,1)S(1)} %slice.20), channel_id=1, source_target_pairs={{0,1},{1,0},{2,3},{3,2},{4,5},{5,4},{6,7},{7,6},{8,9},{9,8},{10,11... | collective-permute-start | bytes 393224 | tf_op jit(solution)/shard_map/ppermute | solution.py:468

commit v3 on v2

--- a/solution.py
+++ b/solution.py
@@ -443,10 +443,10 @@
     for k in range(N):
         lanes = pl.ds(pl.multiple_of((me ^ k) * LN, LN), LN)
         for p in range(2):
-            buf[k, p] = pieces[k][at[k], p].astype(F32)
-            c = pltpu.make_async_copy(buf.at[k, p], out_ref.at[:, p, lanes], sem.at[k, p])
-            c.start()
-            copies.append(c)
+            buf[k, :, p, :] = pieces[k][at[k], p].astype(F32)
+        c = pltpu.make_async_copy(buf.at[k], out_ref.at[:, :, lanes], sem.at[k])
+        c.start()
+        copies.append(c)
     for c in copies:
         c.wait()
 
@@ -457,7 +457,7 @@
         out_shape=jax.ShapeDtypeStruct((SB, 2, N * LN), F32),
         in_specs=[SMEM] + [VMEM] * N,
         out_specs=pl.BlockSpec(memory_space=pl.ANY),
-        scratch_shapes=[pltpu.VMEM((N, 2, SB, LN), F32), pltpu.SemaphoreType.DMA((N, 2))],
+        scratch_shapes=[pltpu.VMEM((N, SB, 2, LN), F32), pltpu.SemaphoreType.DMA((N,))],
         compiler_params=params(12),
         name="join_out",
         cost_estimate=COST,

time: 80.7 us -> 80.7 us (level)
  no operation moved by 1% of the time
where the time goes in v3:
time: 80.7 us; the launch traced here: 80.4 us
  Pallas kernels  32.5 us (40%)
  starting transfers between devices  30.8 us (38%)
  waiting for transfers between devices  15.8 us (20%)
    ppermute x20, starting transfers between devices, send(): return lax.ppermute(v, RING, [(i, i ^ k) for i in range(N)])  20.6 us
    pallas_call x4, Pallas kernels, react_call(): pl.pallas_call(functools.partial(react, far), grid=(2,), out_shape=jax.Sh...  15 us
    ppermute x20, waiting for transfers between devices, send(): return lax.ppermute(v, RING, [(i, i ^ k) for i in range(N)])  10.2 us
    ppermute x6, starting transfers between devices, swap(): lax.ppermute(v, axis, [(i, i + 1) for i in firsts] + [(i + 1, i) for i in...  10.1 us
    pallas_call x1, Pallas kernels, state_call(): pl.pallas_call(pack_state, out_shape=(m(128), m(128), m(256), m(256), m(F...  4.18 us
    ppermute x1, waiting for transfers between devices, on_device(): lax.ppermute(w, RING, [(i, i ^ (6 if i % 2 else 2)) for i in range(N)])  3.32 us
    pallas_call x2, Pallas kernels, finish_call(): pl.pallas_call(functools.partial(finish, which), in_specs=[SMEM] + [VMEM]...  2.96 us
    pallas_call x1, Pallas kernels, advance_call(): pl.pallas_call(advance, in_specs=[SMEM] + [VMEM] * 9, out_specs=(VMEM,) *...  2.63 us
  transfers between devices with their start and end apart: 27, of which 10 were waited for; matrix products, arithmetic and copies ran while one was open for 1% of the time, Pallas kernels for 29%

profile of v3, /device:TPU:103, one launch (start us, length us, event | category | flops | bytes accessed | tf_op | source)
XLA Modules:
  0.0 80.4 jit_solution(9898359756423450070)
XLA Ops:
  0.0 2.2 %pack_weights.1.refs_0_ = bf16[2,656,256]{2,1,0:T(8,128)(2,1)} custom-call(s32[512,256]{1,0:T(8,128)} %order_ref.1, s32[256,512]{1,0:T(8,128)} %stoich_ref.1, f32[2,32,512]{2,1,0:T(8,128)} %bitcast.5, f32[1,512]{1,0:T(1,128)} %bitcast.6, s32[1,64]{1,0:T(1,128)} %bitcast.7, f32[4]{0:T(128)} %coef_ref.1), custom_call_target="tpu_custom_call" | custom-call | flops 1 | bytes 1 | tf_op jit(solution)/shard_map/pack_weights/pallas_call | solution.py:70
  2.4 1.3 %collective-permute-start.3 = (bf16[2,656,256]{2,1,0:T(8,128)(2,1)}, bf16[2,656,256]{2,1,0:T(8,128)(2,1)S(1)}, u32[]{:S(2)}, u32[]{:S(2)}) collective-permute-start(bf16[2,656,256]{2,1,0:T(8,128)(2,1)} %pack_weights.1.refs_0_), channel_id=1, source_target_pairs={{0,1},{1,0},{2,3},{3,2},{4,5},{5,4},{6,7},{7,6},{8,9},{9,8},{10,11... | collective-permute-start | bytes 2015240 | tf_op jit(solution)/shard_map/ppermute | solution.py:468
  4.4 4.2 %pack_state.1 = (bf16[128,512]{1,0:T(8,128)(2,1)}, bf16[128,512]{1,0:T(8,128)(2,1)}, bf16[256,512]{1,0:T(8,128)(2,1)}, bf16[256,512]{1,0:T(8,128)(2,1)}, bf16[38...) custom-call(s32[2]{0:T(128)} %pad_add_fusion.info_ref, f32[64,2,4096]{2,1,0:T(2,128)} %conc_ref.1, ...), custom_call_target="tpu_custom_call" | custom-call | flops 1 | bytes 1 | tf_op jit(solution)/shard_map/pack_state/pallas_call | solution.py:124
  8.5 1.0 %collective-permute-start.2 = (bf16[256,512]{1,0:T(8,128)(2,1)}, bf16[256,512]{1,0:T(8,128)(2,1)S(1)}, u32[]{:S(2)}, u32[]{:S(2)}) collective-permute-start(bf16[256,512]{1,0:T(8,128)(2,1)} %get-tuple-element.55), channel_id=1, source_target_pairs={{0,2},{1,3},{2,0},{3,1},{4,6},{5,7},{6,4},{7,5},{8,10},{9,11},{10,... | collective-permute-start | bytes 786440 | tf_op jit(solution)/shard_map/ppermute | solution.py:468
  9.9 3.3 %collective-permute-done.refs_2_ = bf16[2,656,256]{2,1,0:T(8,128)(2,1)S(1)} collective-permute-done((bf16[2,656,256]{2,1,0:T(8,128)(2,1)}, bf16[2,656,256]{2,1,0:T(8,128)(2,1)S(1)}, u32[]{:S(2)}, u32[]{:S(2)}) %collective-permute-start) | collective-permute-done | bytes 671776 | tf_op jit(solution)/shard_map/ppermute | solution.py:487
  13.2 2.5 %collective-permute-start.6 = (bf16[2,208,256]{2,1,0:T(8,128)(2,1)S(1)}, bf16[2,208,256]{2,1,0:T(8,128)(2,1)S(1)}, u32[]{:S(2)}, u32[]{:S(2)}) collective-permute-start(bf16[2,208,256]{2,1,0:T(8,128)(2,1)S(1)} %slice.17), channel_id=1, source_target_pairs={{0,1},{1,0},{2,3},{3,2},{4,5},{5,4},{6,7},{7,6},{8,9},{9,8},{10,11... | collective-permute-start | bytes 638984 | tf_op jit(solution)/shard_map/ppermute | solution.py:468
  16.9 1.4 %collective-permute-start.8 = (bf16[256,512]{1,0:T(8,128)(2,1)}, bf16[256,512]{1,0:T(8,128)(2,1)S(1)}, u32[]{:S(2)}, u32[]{:S(2)}) collective-permute-start(bf16[256,512]{1,0:T(8,128)(2,1)} %get-tuple-element.64), channel_id=1, source_target_pairs={{0,4},{1,5},{2,6},{3,7},{4,0},{5,1},{6,2},{7,3},{8,12},{9,13},{10,... | collective-permute-start | bytes 786440 | tf_op jit(solution)/shard_map/ppermute | solution.py:468
  18.9 2.2 %sort_weights.1 = (bf16[2048,256]{1,0:T(8,128)(2,1)S(1)}, bf16[256,2048]{1,0:T(8,128)(2,1)S(1)}, bf16[2,2048,128]{2,1,0:T(8,128)(2,1)S(1)}, f32[2048,128]{1,0:T(8,128)S(1)}, f32[256,128]{1,0:T(8,128)S(1)}) custom-call(s32[2]{0:T(128)S(1)} %copy-done.3, bf16[2,656,256]{2,1,0:T(8,128)(2,1)S(1)} %copy-done, ...), custom_call_target="tpu_custom_call" | custom-call | flops 1 | bytes 1 | tf_op jit(solution)/shard_map/sort_weights/pallas_call | solution.py:175
  21.2 1.3 %collective-permute-done.7.refs_3_ = bf16[128,512]{1,0:T(8,128)(2,1)S(1)} collective-permute-done((bf16[128,512]{1,0:T(8,128)(2,1)S(1)}, bf16[128,512]{1,0:T(8,128)(2,1)S(1)}, u32[]{:S(2)}, u32[]{:S(2)}) %collective-permute-start.7) | collective-permute-done | bytes 131104 | tf_op jit(solution)/shard_map/ppermute | solution.py:468
  23.1 3.8 %react.4.da_ref = f32[2,256,512]{2,1,0:T(8,128)S(1)} custom-call(bf16[2,256,512]{2,1,0:T(8,128)(2,1)S(1)} %gather_planes.1.conc_ref.a_ref, bf16[2,2,64,512]{3,2,1,0:T(8,128)(2,1)S(1)} %copy-done.1, bf16[2048,256]{1,0:T(8,128)(2,1)S(1)} %get-tuple-element.67.order_ref, bf16[256,2048]{1,0:T(8,128)(2,1)S(1)} %get-tuple-element.68.stoich_ref, ...), custom_call_target="tpu_custom_call" | custom-call | flops 1 | bytes 1 | tf_op jit(solution)/shard_map/react/pallas_call | solution.py:300
  27.0 1.1 %collective-permute-start.11 = (bf16[384,512]{1,0:T(8,128)(2,1)S(1)}, bf16[384,512]{1,0:T(8,128)(2,1)S(1)}, u32[]{:S(2)}, u32[]{:S(2)}) collective-permute-start(bf16[384,512]{1,0:T(8,128)(2,1)S(1)} %collective-permute-done.9.refs_2_.cell_ref), channel_id=1, source_target_pairs={{0,1},{1,0},{2,3},{3,2},{4,5},{5,4},{6,7},{7,6},{8,9},{9,8},{10,11... | collective-permute-start | bytes 1179656 | tf_op jit(solution)/shard_map/ppermute | solution.py:468
  28.1 1.7 %collective-permute-done.10.refs_1_ = bf16[256,512]{1,0:T(8,128)(2,1)S(1)} collective-permute-done((bf16[256,512]{1,0:T(8,128)(2,1)S(1)}, bf16[256,512]{1,0:T(8,128)(2,1)S(1)}, u32[]{:S(2)}, u32[]{:S(2)}) %collective-permute-start.10) | collective-permute-done | bytes 262176 | tf_op jit(solution)/shard_map/ppermute | solution.py:468
  29.8 0.8 %gather_far.1 = (bf16[2,256,512]{2,1,0:T(8,128)(2,1)S(1)}, bf16[256,512]{1,0:T(8,128)(2,1)S(1)}, bf16[256,512]{1,0:T(8,128)(2,1)S(1)}, bf16[2,256,128]{2,1,0:T(8,128)(2,1)S(1)}, bf16[2,256,128]{2,1,0:T(8,128)(2,1)S(1)}) custom-call(s32[2]{0:T(128)S(1)} %copy-done.3, bf16[2,256,512]{2,1,0:T(8,128)(2,1)S(1)} %gather_planes.1.conc_ref.a_ref, ...), custom_call_target="tpu_custom_call" | custom-call | flops 1 | bytes 1 | tf_op jit(solution)/shard_map/gather_far/pallas_call | solution.py:264
  30.7 1.4 %collective-permute-start.12 = (bf16[256,512]{1,0:T(8,128)(2,1)S(1)}, bf16[256,512]{1,0:T(8,128)(2,1)S(1)}, u32[]{:S(2)}, u32[]{:S(2)}) collective-permute-start(bf16[256,512]{1,0:T(8,128)(2,1)S(1)} %get-tuple-element.75), channel_id=1, source_target_pairs={{0,8},{16,24},{32,40},{48,56},{64,72},{80,88},{96,104},{112,120},{... | collective-permute-start | bytes 786440 | tf_op jit(solution)/shard_map/ppermute | solution.py:472
  32.1 3.6 %collective-permute-start.13 = (bf16[256,512]{1,0:T(8,128)(2,1)S(1)}, bf16[256,512]{1,0:T(8,128)(2,1)S(1)}, u32[]{:S(2)}, u32[]{:S(2)}) collective-permute-start(bf16[256,512]{1,0:T(8,128)(2,1)S(1)} %get-tuple-element.76), channel_id=1, source_target_pairs={{8,16},{24,32},{40,48},{56,64},{72,80},{88,96},{104,112},{16,8},{3... | collective-permute-start | bytes 786440 | tf_op jit(solution)/shard_map/ppermute | solution.py:472
  35.7 1.0 %collective-permute-start.14 = (bf16[2,256,128]{2,1,0:T(8,128)(2,1)S(1)}, bf16[2,256,128]{2,1,0:T(8,128)(2,1)S(1)}, u32[]{:S(2)}, u32[]{:S(2)}) collective-permute-start(bf16[2,256,128]{2,1,0:T(8,128)(2,1)S(1)} %get-tuple-element.77), channel_id=1, source_target_pairs={{0,1},{1,0},{2,3},{3,2},{4,5},{5,4},{6,7},{7,6},{8,9},{9,8},{10,11... | collective-permute-start | bytes 393224 | tf_op jit(solution)/shard_map/ppermute | solution.py:468
  37.4 3.8 %react.5.db_ref = f32[2,256,512]{2,1,0:T(8,128)S(1)} custom-call(bf16[2,256,512]{2,1,0:T(8,128)(2,1)S(1)} %get-tuple-element.73.conc_ref.b_ref, bf16[384,512]{1,0:T(8,128)(2,1)S(1)} %collective-permute-done.9.refs_2_.cell_ref, bf16[2048,256]{1,0:T(8,128)(2,1)S(1)} %get-tuple-element.67.order_ref, bf16[256,2048]{1,0:T(8,128)(2,1)S(1)} %get-tuple-element.68.stoich_ref, ...), custom_call_target="tpu_custom_call" | custom-call | flops 1 | bytes 1 | tf_op jit(solution)/shard_map/react/pallas_call | solution.py:300
  41.2 2.1 %collective-permute-done.13.od_ref = bf16[256,512]{1,0:T(8,128)(2,1)S(1)} collective-permute-done((bf16[256,512]{1,0:T(8,128)(2,1)S(1)}, bf16[256,512]{1,0:T(8,128)(2,1)S(1)}, u32[]{:S(2)}, u32[]{:S(2)}) %collective-permute-start.13) | collective-permute-done | bytes 262176 | tf_op jit(solution)/shard_map/ppermute | solution.py:472
  43.2 2.6 %advance.1 = (f32[2,256,512]{2,1,0:T(8,128)S(1)}, f32[2,256,512]{2,1,0:T(8,128)S(1)}, bf16[256,512]{1,0:T(8,128)(2,1)S(1)}, bf16[256,512]{1,0:T(8,128)(2,1)S(1)}...) custom-call(s32[2]{0:T(128)S(1)} %copy-done.3, ...), custom_call_target="tpu_custom_call" | custom-call | flops 1 | bytes 1 | tf_op jit(solution)/shard_map/advance/pallas_call | solution.py:400
  46.0 3.6 %collective-permute-start.17 = (bf16[256,512]{1,0:T(8,128)(2,1)S(1)}, bf16[256,512]{1,0:T(8,128)(2,1)S(1)}, u32[]{:S(2)}, u32[]{:S(2)}) collective-permute-start(bf16[256,512]{1,0:T(8,128)(2,1)S(1)} %get-tuple-element.83), channel_id=1, source_target_pairs={{8,16},{24,32},{40,48},{56,64},{72,80},{88,96},{104,112},{16,8},{3... | collective-permute-start | bytes 786440 | tf_op jit(solution)/shard_map/ppermute | solution.py:472
  49.6 1.9 %collective-permute-start.18 = (bf16[2,256,128]{2,1,0:T(8,128)(2,1)S(1)}, bf16[2,256,128]{2,1,0:T(8,128)(2,1)S(1)}, u32[]{:S(2)}, u32[]{:S(2)}) collective-permute-start(bf16[2,256,128]{2,1,0:T(8,128)(2,1)S(1)} %get-tuple-element.84), channel_id=1, source_target_pairs={{0,1},{1,0},{2,3},{3,2},{4,5},{5,4},{6,7},{7,6},{8,9},{9,8},{10,11... | collective-permute-start | bytes 393224 | tf_op jit(solution)/shard_map/ppermute | solution.py:468
  52.2 3.8 %react.6.d_ref = f32[2,256,512]{2,1,0:T(8,128)S(1)} custom-call(f32[2,256,512]{2,1,0:T(8,128)S(1)} %get-tuple-element.81.conc_ref.b_ref, bf16[384,512]{1,0:T(8,128)(2,1)S(1)} %collective-permute-done.9.refs_2_.cell_ref, bf16[2048,256]{1,0:T(8,128)(2,1)S(1)} %get-tuple-element.67.order_ref, bf16[256,2048]{1,0:T(8,128)(2,1)S(1)} %get-tuple-element.68.stoich_ref, ...), custom_call_target="tpu_custom_call" | custom-call | flops 1 | bytes 1 | tf_op jit(solution)/shard_map/react/pallas_call | solution.py:300
  56.2 1.4 %finish.2 = (bf16[2,2,64,512]{3,2,1,0:T(8,128)(2,1)S(1)}, bf16[2,2,64,512]{3,2,1,0:T(8,128)(2,1)S(1)}) custom-call(s32[2]{0:T(128)S(1)} %copy-done.3, f32[2,256,512]{2,1,0:T(8,128)S(1)} %get-tuple-element.80.a_ref.conc_ref, f32[2,256,512]{2,1,0:T(8,128)S(1)} %get-tuple-element.81.conc_ref.b_ref, f32[2,256,512]{2,1,0:T(8,128)S(1)} %react.6.d_ref, ...), custom_call_target="tpu_custom_call" | custom-call | flops 1 | bytes 1 | tf_op jit(solution)/shard_map/finish/pallas_call | solution.py:428
  57.6 2.7 %collective-permute-start.20 = (bf16[2,2,64,512]{3,2,1,0:T(8,128)(2,1)S(1)}, bf16[2,2,64,512]{3,2,1,0:T(8,128)(2,1)S(1)}, u32[]{:S(2)}, u32[]{:S(2)}) collective-permute-start(bf16[2,2,64,512]{3,2,1,0:T(8,128)(2,1)S(1)} %get-tuple-element.88), channel_id=1, source_target_pairs={{0,4},{1,5},{2,6},{3,7},{4,0},{5,1},{6,2},{7,3},{8,12},{9,13},{10,... | collective-permute-start | bytes 786440 | tf_op jit(solution)/shard_map/ppermute | solution.py:468
  60.4 2.7 %collective-permute-start.21 = (bf16[2,2,64,512]{3,2,1,0:T(8,128)(2,1)S(1)}, bf16[2,2,64,512]{3,2,1,0:T(8,128)(2,1)S(1)}, u32[]{:S(2)}, u32[]{:S(2)}) collective-permute-start(bf16[2,2,64,512]{3,2,1,0:T(8,128)(2,1)S(1)} %get-tuple-element.89), channel_id=1, source_target_pairs={{0,6},{1,7},{2,4},{3,5},{4,2},{5,3},{6,0},{7,1},{8,14},{9,15},{10,... | collective-permute-start | bytes 786440 | tf_op jit(solution)/shard_map/ppermute | solution.py:468
  63.0 3.7 %react.7.d_ref = f32[2,256,512]{2,1,0:T(8,128)S(1)} custom-call(f32[2,256,512]{2,1,0:T(8,128)S(1)} %get-tuple-element.80.a_ref.conc_ref, bf16[2,2,64,512]{3,2,1,0:T(8,128)(2,1)S(1)} %copy-done.1, bf16[2048,256]{1,0:T(8,128)(2,1)S(1)} %get-tuple-element.67.order_ref, bf16[256,2048]{1,0:T(8,128)(2,1)S(1)} %get-tuple-element.68.stoich_ref, ...), custom_call_target="tpu_custom_call" | custom-call | flops 1 | bytes 1 | tf_op jit(solution)/shard_map/react/pallas_call | solution.py:300
  66.8 1.6 %finish.3 = (bf16[1,2,64,512]{3,2,1,0:T(8,128)(2,1)S(1)}, bf16[1,2,64,512]{3,2,1,0:T(8,128)(2,1)S(1)}, bf16[2,2,64,512]{3,2,1,0:T(8,128)(2,1)S(1)}) custom-call(s32[2]{0:T(128)S(1)} %copy-done.3, f32[2,256,512]{2,1,0:T(8,128)S(1)} %get-tuple-element.80.a_ref.conc_ref, f32[2,256,512]{2,1,0:T(8,128)S(1)} %get-tuple-element.81.conc_ref.b_ref, ...), custom_call_target="tpu_custom_call" | custom-call | flops 1 | bytes 1 | tf_op jit(solution)/shard_map/finish/pallas_call | solution.py:428
  68.5 4.5 %collective-permute-done.21.refs_6_ = bf16[2,2,64,512]{3,2,1,0:T(8,128)(2,1)S(1)} collective-permute-done((bf16[2,2,64,512]{3,2,1,0:T(8,128)(2,1)S(1)}, bf16[2,2,64,512]{3,2,1,0:T(8,128)(2,1)S(1)}, u32[]{:S(2)}, u32[]{:S(2)}) %collective-permute-start.21) | collective-permute-done | bytes 262176 | tf_op jit(solution)/shard_map/ppermute | solution.py:468
  74.1 1.0 %collective-permute-done.23.refs_2_ = bf16[2,2,64,512]{3,2,1,0:T(8,128)(2,1)S(1)} collective-permute-done((bf16[2,2,64,512]{3,2,1,0:T(8,128)(2,1)S(1)}, bf16[2,2,64,512]{3,2,1,0:T(8,128)(2,1)S(1)}, u32[]{:S(2)}, u32[]{:S(2)}) %collective-permute-start.23) | collective-permute-done | bytes 262176 | tf_op jit(solution)/shard_map/ppermute | solution.py:468
  75.1 2.2 %collective-permute-start.24 = (bf16[1,2,64,512]{3,2,1,0:T(8,128)(2,1)S(1)}, bf16[1,2,64,512]{3,2,1,0:T(8,128)(2,1)S(1)}, u32[]{:S(2)}, u32[]{:S(2)}) collective-permute-start(bf16[1,2,64,512]{3,2,1,0:T(8,128)(2,1)S(1)} %slice.20), channel_id=1, source_target_pairs={{0,1},{1,0},{2,3},{3,2},{4,5},{5,4},{6,7},{7,6},{8,9},{9,8},{10,11... | collective-permute-start | bytes 393224 | tf_op jit(solution)/shard_map/ppermute | solution.py:468
  77.3 1.0 %collective-permute-done.24.refs_3_ = bf16[1,2,64,512]{3,2,1,0:T(8,128)(2,1)S(1)} collective-permute-done((bf16[1,2,64,512]{3,2,1,0:T(8,128)(2,1)S(1)}, bf16[1,2,64,512]{3,2,1,0:T(8,128)(2,1)S(1)}, u32[]{:S(2)}, u32[]{:S(2)}) %collective-permute-start.24) | collective-permute-done | bytes 131104 | tf_op jit(solution)/shard_map/ppermute | solution.py:468
  78.3 2.0 %join_out.1 = f32[64,2,4096]{2,1,0:T(2,128)} custom-call(s32[2]{0:T(128)S(1)} %copy-done.3, bf16[1,2,64,512]{3,2,1,0:T(8,128)(2,1)S(1)} %get-tuple-element.92.refs_0_, bf16[1,2,64,512]{3,2,1,0:T(8,128)(2,1)S(1)} %collective-permute-done.22.refs_1_, bf16[2,2,64,512]{3,2,1,0:T(8,128)(2,1)S(1)} %collective-permute-done.23.refs_2_, ...), custom_call_target="tpu_custom_call" | custom-call | flops 1 | bytes 1 | tf_op jit(solution)/shard_map/join_out/pallas_call | solution.py:455
  (48 shorter events, 6.6 us)
Async XLA Ops:
  2.2 11.0 %collective-permute-start = (bf16[2,656,256]{2,1,0:T(8,128)(2,1)}, bf16[2,656,256]{2,1,0:T(8,128)(2,1)S(1)}, u32[]{:S(2)}, u32[]{:S(2)}) collective-permute-start(bf16[2,656,256]{2,1,0:T(8,128)(2,1)} %pack_weights.1.refs_0_), channel_id=1, source_target_pairs={{0,2},{1,7},{2,0},{3,5},{4,6},{5,3},{6,4},{7,1},{8,10},{9,15},{10,... | collective-permute-start | bytes 2015240 | tf_op jit(solution)/shard_map/ppermute | solution.py:487
  2.4 13.5 %collective-permute-start.3 = (bf16[2,656,256]{2,1,0:T(8,128)(2,1)}, bf16[2,656,256]{2,1,0:T(8,128)(2,1)S(1)}, u32[]{:S(2)}, u32[]{:S(2)}) collective-permute-start(bf16[2,656,256]{2,1,0:T(8,128)(2,1)} %pack_weights.1.refs_0_), channel_id=1, source_target_pairs={{0,1},{1,0},{2,3},{3,2},{4,5},{5,4},{6,7},{7,6},{8,9},{9,8},{10,11... | collective-permute-start | bytes 2015240 | tf_op jit(solution)/shard_map/ppermute | solution.py:468
  4.4 14.5 %copy-start = (bf16[2,656,256]{2,1,0:T(8,128)(2,1)S(1)}, bf16[2,656,256]{2,1,0:T(8,128)(2,1)}, u32[]{:S(2)}) copy-start(bf16[2,656,256]{2,1,0:T(8,128)(2,1)} %pack_weights.1.refs_0_) | copy-start | bytes 2015236
  4.4 14.5 %copy-start.3 = (s32[2]{0:T(128)S(1)}, s32[2]{0:T(128)}, u32[]{:S(2)}) copy-start(s32[2]{0:T(128)} %pad_add_fusion.info_ref) | copy-start | bytes 28
  8.5 12.5 %collective-permute-start.2 = (bf16[256,512]{1,0:T(8,128)(2,1)}, bf16[256,512]{1,0:T(8,128)(2,1)S(1)}, u32[]{:S(2)}, u32[]{:S(2)}) collective-permute-start(bf16[256,512]{1,0:T(8,128)(2,1)} %get-tuple-element.55), channel_id=1, source_target_pairs={{0,2},{1,3},{2,0},{3,1},{4,6},{5,7},{6,4},{7,5},{8,10},{9,11},{10,... | collective-permute-start | bytes 786440 | tf_op jit(solution)/shard_map/ppermute | solution.py:468
  9.5 17.5 %collective-permute-start.9 = (bf16[384,512]{1,0:T(8,128)(2,1)}, bf16[384,512]{1,0:T(8,128)(2,1)S(1)}, u32[]{:S(2)}, u32[]{:S(2)}) collective-permute-start(bf16[384,512]{1,0:T(8,128)(2,1)} %get-tuple-element.65), channel_id=1, source_target_pairs={{0,6},{1,7},{2,4},{3,5},{4,2},{5,3},{6,0},{7,1},{8,14},{9,15},{10,... | collective-permute-start | bytes 1179656 | tf_op jit(solution)/shard_map/ppermute | solution.py:468
  13.2 9.3 %copy-start.2 = (bf16[128,512]{1,0:T(8,128)(2,1)S(1)}, bf16[128,512]{1,0:T(8,128)(2,1)}, u32[]{:S(2)}) copy-start(bf16[128,512]{1,0:T(8,128)(2,1)} %get-tuple-element.53.refs_0_) | copy-start | bytes 393220
  13.2 3.6 %collective-permute-start.6 = (bf16[2,208,256]{2,1,0:T(8,128)(2,1)S(1)}, bf16[2,208,256]{2,1,0:T(8,128)(2,1)S(1)}, u32[]{:S(2)}, u32[]{:S(2)}) collective-permute-start(bf16[2,208,256]{2,1,0:T(8,128)(2,1)S(1)} %slice.17), channel_id=1, source_target_pairs={{0,1},{1,0},{2,3},{3,2},{4,5},{5,4},{6,7},{7,6},{8,9},{9,8},{10,11... | collective-permute-start | bytes 638984 | tf_op jit(solution)/shard_map/ppermute | solution.py:468
  15.8 7.3 %copy-start.1 = (bf16[2,2,64,512]{3,2,1,0:T(8,128)(2,1)S(1)}, bf16[2,2,64,512]{3,2,1,0:T(8,128)(2,1)}, u32[]{:S(2)}) copy-start(bf16[2,2,64,512]{3,2,1,0:T(8,128)(2,1)} %get-tuple-element.90.cell_ref) | copy-start | bytes 786436
  15.8 2.4 %collective-permute-start.5 = (bf16[2,224,256]{2,1,0:T(8,128)(2,1)S(1)}, bf16[2,224,256]{2,1,0:T(8,128)(2,1)S(1)}, u32[]{:S(2)}, u32[]{:S(2)}) collective-permute-start(bf16[2,224,256]{2,1,0:T(8,128)(2,1)S(1)} %get-tuple-element.97), channel_id=1, source_target_pairs={{0,1},{1,0},{2,3},{3,2},{4,5},{5,4},{6,7},{7,6},{8,9},{9,8},{10,11... | collective-permute-start | bytes 688136 | tf_op jit(solution)/shard_map/ppermute | solution.py:468
  15.9 3.0 %collective-permute-start.4 = (bf16[2,224,256]{2,1,0:T(8,128)(2,1)S(1)}, bf16[2,224,256]{2,1,0:T(8,128)(2,1)S(1)}, u32[]{:S(2)}, u32[]{:S(2)}) collective-permute-start(bf16[2,224,256]{2,1,0:T(8,128)(2,1)S(1)} %get-tuple-element.98), channel_id=1, source_target_pairs={{0,1},{1,0},{2,3},{3,2},{4,5},{5,4},{6,7},{7,6},{8,9},{9,8},{10,11... | collective-permute-start | bytes 688136 | tf_op jit(solution)/shard_map/ppermute | solution.py:468
  16.9 10.0 %collective-permute-start.8 = (bf16[256,512]{1,0:T(8,128)(2,1)}, bf16[256,512]{1,0:T(8,128)(2,1)S(1)}, u32[]{:S(2)}, u32[]{:S(2)}) collective-permute-start(bf16[256,512]{1,0:T(8,128)(2,1)} %get-tuple-element.64), channel_id=1, source_target_pairs={{0,4},{1,5},{2,6},{3,7},{4,0},{5,1},{6,2},{7,3},{8,12},{9,13},{10,... | collective-permute-start | bytes 786440 | tf_op jit(solution)/shard_map/ppermute | solution.py:468
  18.2 3.0 %collective-permute-start.1 = (bf16[128,512]{1,0:T(8,128)(2,1)}, bf16[128,512]{1,0:T(8,128)(2,1)S(1)}, u32[]{:S(2)}, u32[]{:S(2)}) collective-permute-start(bf16[128,512]{1,0:T(8,128)(2,1)} %get-tuple-element.54), channel_id=1, source_target_pairs={{0,1},{1,0},{2,3},{3,2},{4,5},{5,4},{6,7},{7,6},{8,9},{9,8},{10,11... | collective-permute-start | bytes 393224 | tf_op jit(solution)/shard_map/ppermute | solution.py:468
  21.1 1.4 %collective-permute-start.7 = (bf16[128,512]{1,0:T(8,128)(2,1)S(1)}, bf16[128,512]{1,0:T(8,128)(2,1)S(1)}, u32[]{:S(2)}, u32[]{:S(2)}) collective-permute-start(bf16[128,512]{1,0:T(8,128)(2,1)S(1)} %slice.18), channel_id=1, source_target_pairs={{0,1},{1,0},{2,3},{3,2},{4,5},{5,4},{6,7},{7,6},{8,9},{9,8},{10,11... | collective-permute-start | bytes 393224 | tf_op jit(solution)/shard_map/ppermute | solution.py:468
  27.0 2.8 %collective-permute-start.11 = (bf16[384,512]{1,0:T(8,128)(2,1)S(1)}, bf16[384,512]{1,0:T(8,128)(2,1)S(1)}, u32[]{:S(2)}, u32[]{:S(2)}) collective-permute-start(bf16[384,512]{1,0:T(8,128)(2,1)S(1)} %collective-permute-done.9.refs_2_.cell_ref), channel_id=1, source_target_pairs={{0,1},{1,0},{2,3},{3,2},{4,5},{5,4},{6,7},{7,6},{8,9},{9,8},{10,11... | collective-permute-start | bytes 1179656 | tf_op jit(solution)/shard_map/ppermute | solution.py:468
  28.1 1.7 %collective-permute-start.10 = (bf16[256,512]{1,0:T(8,128)(2,1)S(1)}, bf16[256,512]{1,0:T(8,128)(2,1)S(1)}, u32[]{:S(2)}, u32[]{:S(2)}) collective-permute-start(bf16[256,512]{1,0:T(8,128)(2,1)S(1)} %collective-permute-done.8.refs_0_), channel_id=1, source_target_pairs={{0,1},{1,0},{2,3},{3,2},{4,5},{5,4},{6,7},{7,6},{8,9},{9,8},{10,11... | collective-permute-start | bytes 786440 | tf_op jit(solution)/shard_map/ppermute | solution.py:468
  30.7 10.5 %collective-permute-start.12 = (bf16[256,512]{1,0:T(8,128)(2,1)S(1)}, bf16[256,512]{1,0:T(8,128)(2,1)S(1)}, u32[]{:S(2)}, u32[]{:S(2)}) collective-permute-start(bf16[256,512]{1,0:T(8,128)(2,1)S(1)} %get-tuple-element.75), channel_id=1, source_target_pairs={{0,8},{16,24},{32,40},{48,56},{64,72},{80,88},{96,104},{112,120},{... | collective-permute-start | bytes 786440 | tf_op jit(solution)/shard_map/ppermute | solution.py:472
  32.1 11.2 %collective-permute-start.13 = (bf16[256,512]{1,0:T(8,128)(2,1)S(1)}, bf16[256,512]{1,0:T(8,128)(2,1)S(1)}, u32[]{:S(2)}, u32[]{:S(2)}) collective-permute-start(bf16[256,512]{1,0:T(8,128)(2,1)S(1)} %get-tuple-element.76), channel_id=1, source_target_pairs={{8,16},{24,32},{40,48},{56,64},{72,80},{88,96},{104,112},{16,8},{3... | collective-permute-start | bytes 786440 | tf_op jit(solution)/shard_map/ppermute | solution.py:472
  35.7 5.5 %collective-permute-start.14 = (bf16[2,256,128]{2,1,0:T(8,128)(2,1)S(1)}, bf16[2,256,128]{2,1,0:T(8,128)(2,1)S(1)}, u32[]{:S(2)}, u32[]{:S(2)}) collective-permute-start(bf16[2,256,128]{2,1,0:T(8,128)(2,1)S(1)} %get-tuple-element.77), channel_id=1, source_target_pairs={{0,1},{1,0},{2,3},{3,2},{4,5},{5,4},{6,7},{7,6},{8,9},{9,8},{10,11... | collective-permute-start | bytes 393224 | tf_op jit(solution)/shard_map/ppermute | solution.py:468
  36.7 4.5 %collective-permute-start.15 = (bf16[2,256,128]{2,1,0:T(8,128)(2,1)S(1)}, bf16[2,256,128]{2,1,0:T(8,128)(2,1)S(1)}, u32[]{:S(2)}, u32[]{:S(2)}) collective-permute-start(bf16[2,256,128]{2,1,0:T(8,128)(2,1)S(1)} %get-tuple-element.78), channel_id=1, source_target_pairs={{1,2},{3,4},{5,6},{2,1},{4,3},{6,5},{9,10},{11,12},{13,14},{10,9},... | collective-permute-start | bytes 393224 | tf_op jit(solution)/shard_map/ppermute | solution.py:472
  45.9 10.1 %collective-permute-start.16 = (bf16[256,512]{1,0:T(8,128)(2,1)S(1)}, bf16[256,512]{1,0:T(8,128)(2,1)S(1)}, u32[]{:S(2)}, u32[]{:S(2)}) collective-permute-start(bf16[256,512]{1,0:T(8,128)(2,1)S(1)} %get-tuple-element.82), channel_id=1, source_target_pairs={{0,8},{16,24},{32,40},{48,56},{64,72},{80,88},{96,104},{112,120},{... | collective-permute-start | bytes 786440 | tf_op jit(solution)/shard_map/ppermute | solution.py:472
  46.0 10.3 %collective-permute-start.17 = (bf16[256,512]{1,0:T(8,128)(2,1)S(1)}, bf16[256,512]{1,0:T(8,128)(2,1)S(1)}, u32[]{:S(2)}, u32[]{:S(2)}) collective-permute-start(bf16[256,512]{1,0:T(8,128)(2,1)S(1)} %get-tuple-element.83), channel_id=1, source_target_pairs={{8,16},{24,32},{40,48},{56,64},{72,80},{88,96},{104,112},{16,8},{3... | collective-permute-start | bytes 786440 | tf_op jit(solution)/shard_map/ppermute | solution.py:472
  49.6 6.3 %collective-permute-start.18 = (bf16[2,256,128]{2,1,0:T(8,128)(2,1)S(1)}, bf16[2,256,128]{2,1,0:T(8,128)(2,1)S(1)}, u32[]{:S(2)}, u32[]{:S(2)}) collective-permute-start(bf16[2,256,128]{2,1,0:T(8,128)(2,1)S(1)} %get-tuple-element.84), channel_id=1, source_target_pairs={{0,1},{1,0},{2,3},{3,2},{4,5},{5,4},{6,7},{7,6},{8,9},{9,8},{10,11... | collective-permute-start | bytes 393224 | tf_op jit(solution)/shard_map/ppermute | solution.py:468
  51.5 4.5 %collective-permute-start.19 = (bf16[2,256,128]{2,1,0:T(8,128)(2,1)S(1)}, bf16[2,256,128]{2,1,0:T(8,128)(2,1)S(1)}, u32[]{:S(2)}, u32[]{:S(2)}) collective-permute-start(bf16[2,256,128]{2,1,0:T(8,128)(2,1)S(1)} %get-tuple-element.85), channel_id=1, source_target_pairs={{1,2},{3,4},{5,6},{2,1},{4,3},{6,5},{9,10},{11,12},{13,14},{10,9},... | collective-permute-start | bytes 393224 | tf_op jit(solution)/shard_map/ppermute | solution.py:472
  57.6 10.9 %collective-permute-start.20 = (bf16[2,2,64,512]{3,2,1,0:T(8,128)(2,1)S(1)}, bf16[2,2,64,512]{3,2,1,0:T(8,128)(2,1)S(1)}, u32[]{:S(2)}, u32[]{:S(2)}) collective-permute-start(bf16[2,2,64,512]{3,2,1,0:T(8,128)(2,1)S(1)} %get-tuple-element.88), channel_id=1, source_target_pairs={{0,4},{1,5},{2,6},{3,7},{4,0},{5,1},{6,2},{7,3},{8,12},{9,13},{10,... | collective-permute-start | bytes 786440 | tf_op jit(solution)/shard_map/ppermute | solution.py:468
  60.4 12.6 %collective-permute-start.21 = (bf16[2,2,64,512]{3,2,1,0:T(8,128)(2,1)S(1)}, bf16[2,2,64,512]{3,2,1,0:T(8,128)(2,1)S(1)}, u32[]{:S(2)}, u32[]{:S(2)}) collective-permute-start(bf16[2,2,64,512]{3,2,1,0:T(8,128)(2,1)S(1)} %get-tuple-element.89), channel_id=1, source_target_pairs={{0,6},{1,7},{2,4},{3,5},{4,2},{5,3},{6,0},{7,1},{8,14},{9,15},{10,... | collective-permute-start | bytes 786440 | tf_op jit(solution)/shard_map/ppermute | solution.py:468
  68.4 6.7 %collective-permute-start.23 = (bf16[2,2,64,512]{3,2,1,0:T(8,128)(2,1)S(1)}, bf16[2,2,64,512]{3,2,1,0:T(8,128)(2,1)S(1)}, u32[]{:S(2)}, u32[]{:S(2)}) collective-permute-start(bf16[2,2,64,512]{3,2,1,0:T(8,128)(2,1)S(1)} %get-tuple-element.94), channel_id=1, source_target_pairs={{0,2},{1,3},{2,0},{3,1},{4,6},{5,7},{6,4},{7,5},{8,10},{9,11},{10,... | collective-permute-start | bytes 786440 | tf_op jit(solution)/shard_map/ppermute | solution.py:468
  73.0 5.3 %collective-permute-start.25 = (bf16[2,2,64,512]{3,2,1,0:T(8,128)(2,1)S(1)}, bf16[2,2,64,512]{3,2,1,0:T(8,128)(2,1)S(1)}, u32[]{:S(2)}, u32[]{:S(2)}) collective-permute-start(bf16[2,2,64,512]{3,2,1,0:T(8,128)(2,1)S(1)} %collective-permute-done.20.refs_4_), channel_id=1, source_target_pairs={{0,1},{1,0},{2,3},{3,2},{4,5},{5,4},{6,7},{7,6},{8,9},{9,8},{10,11... | collective-permute-start | bytes 786440 | tf_op jit(solution)/shard_map/ppermute | solution.py:468
  73.5 4.7 %collective-permute-start.26 = (bf16[2,2,64,512]{3,2,1,0:T(8,128)(2,1)S(1)}, bf16[2,2,64,512]{3,2,1,0:T(8,128)(2,1)S(1)}, u32[]{:S(2)}, u32[]{:S(2)}) collective-permute-start(bf16[2,2,64,512]{3,2,1,0:T(8,128)(2,1)S(1)} %collective-permute-done.21.refs_6_), channel_id=1, source_target_pairs={{0,1},{1,0},{2,3},{3,2},{4,5},{5,4},{6,7},{7,6},{8,9},{9,8},{10,11... | collective-permute-start | bytes 786440 | tf_op jit(solution)/shard_map/ppermute | solution.py:468
  73.6 3.7 %collective-permute-start.22 = (bf16[1,2,64,512]{3,2,1,0:T(8,128)(2,1)S(1)}, bf16[1,2,64,512]{3,2,1,0:T(8,128)(2,1)S(1)}, u32[]{:S(2)}, u32[]{:S(2)}) collective-permute-start(bf16[1,2,64,512]{3,2,1,0:T(8,128)(2,1)S(1)} %get-tuple-element.93), channel_id=1, source_target_pairs={{0,1},{1,0},{2,3},{3,2},{4,5},{5,4},{6,7},{7,6},{8,9},{9,8},{10,11... | collective-permute-start | bytes 393224 | tf_op jit(solution)/shard_map/ppermute | solution.py:468
  75.1 3.2 %collective-permute-start.24 = (bf16[1,2,64,512]{3,2,1,0:T(8,128)(2,1)S(1)}, bf16[1,2,64,512]{3,2,1,0:T(8,128)(2,1)S(1)}, u32[]{:S(2)}, u32[]{:S(2)}) collective-permute-start(bf16[1,2,64,512]{3,2,1,0:T(8,128)(2,1)S(1)} %slice.20), channel_id=1, source_target_pairs={{0,1},{1,0},{2,3},{3,2},{4,5},{5,4},{6,7},{7,6},{8,9},{9,8},{10,11... | collective-permute-start | bytes 393224 | tf_op jit(solution)/shard_map/ppermute | solution.py:468
